TPU v7x, 32 devices: a whole 2x2x4 slice. The times are simulated.
32 devices in a mesh: shot: 4 (over y, core), dom: 8 (over z, x).
Axes of the slice: x: 2, y: 2, z: 4, core: 2. Of those that a mesh axis runs over, the one named last changes fastest.
Arguments:
- wave_before: float32 [4, 128, 64, 256], P('shot', 'dom'), may hold values from -1.5 to 1.5
- wave_current: float32 [4, 128, 64, 256], P('shot', 'dom'), may hold values from -1.5 to 1.5
- adjoint_far: float32 [4, 128, 64, 256], P('shot', 'dom'), may hold values from -1.5 to 1.5
- adjoint_near: float32 [4, 128, 64, 256], P('shot', 'dom'), may hold values from -1.5 to 1.5
- labels: int32 [128, 64, 256], P('dom'), may hold values from 0 to 7
- table: float32 [8], replicated, may hold values from 0.03 to 0.12
- source_index: int32 [4, 3], P('shot'), may hold values from 0 to 255, as said below
- wavelet: float32 [4, 4], P('shot'), may hold values from -6 to 6
- receiver_index: int32 [4, 1024, 3], P('shot'), may hold values from 0 to 255, as said below
- residual: float32 [4, 4, 1024], P('shot'), may hold values from -6 to 6
Outputs:
- final_wave: float32 [4, 128, 64, 256], P('shot', 'dom')
- first_adjoint: float32 [4, 128, 64, 256], P('shot', 'dom')
- gradient: float32 [128, 64, 256], P('dom')
Inputs may be any that keep to these rules, and one draw needn't show every extreme that they name: `source_index`: column 0 is a cell index along x below 128, column 1 along z below 64, column 2 along y below 256. The first shot's source lies at the far corner of the grid and the second shot's source at depth 0. `receiver_index`: last index 0 is a cell index along x below 128, 1 along z below 64, 2 along y below 256; receivers may share a cell. In every shot the first receiver lies at the far corner of the grid and the second at depth 0.
All inputs are finite; a program needn't handle non-finite values.
Results may differ from a plain program's by a relative error of at most 0.00002.
Values sent between devices are 32-bit elements; how exact they have to be, the bound alone decides.
No kernel may reach another device: no remote copies, remote signals or barrier semaphores. Data moves between devices by JAX's collectives and lax.ppermute only.
A program may use at most 128 MiB of HBM per device.

v0:
```python
import jax
import jax.numpy as jnp
from jax import lax
from jax.sharding import PartitionSpec as P

centre_coef = -205.0 / 72.0
side_coefs = (8.0 / 5.0, -1.0 / 5.0, 8.0 / 315.0, -1.0 / 560.0)


def padded(block, sides, width):
    for axis, dim in sides:
        count = lax.axis_size(axis)
        forward = [(i, i + 1) for i in range(count - 1)]
        backward = [(target, source) for source, target in forward]
        low = lax.ppermute(
            lax.slice_in_dim(block, block.shape[dim] - width, None, axis=dim), axis, forward
        )
        high = lax.ppermute(lax.slice_in_dim(block, 0, width, axis=dim), axis, backward)
        block = jnp.concatenate([low, block, high], axis=dim)
    return block


def stencil(extended, centre):
    planes = centre.shape[1]
    depth = centre.shape[2]
    across = centre.shape[3]
    padded_yz = jnp.pad(centre, ((0, 0), (0, 0), (4, 4), (4, 4)))
    result = 3.0 * centre_coef * centre
    for k in range(1, 5):
        coef = side_coefs[k - 1]
        result = result + coef * (
            extended[:, 4 + k : 4 + k + planes]
            + extended[:, 4 - k : 4 - k + planes]
            + padded_yz[:, :, 4 + k : 4 + k + depth, 4 : 4 + across]
            + padded_yz[:, :, 4 - k : 4 - k + depth, 4 : 4 + across]
            + padded_yz[:, :, 4 : 4 + depth, 4 + k : 4 + k + across]
            + padded_yz[:, :, 4 : 4 + depth, 4 - k : 4 - k + across]
        )
    return result


def rates(labels, table):
    result = jnp.zeros(labels.shape, jnp.float32)
    for region in range(table.shape[0]):
        result = result + jnp.where(labels == region, table[region], jnp.zeros((), jnp.float32))
    return result


def inject(field_in, index_x, index_z, index_y, values, first_plane, planes):
    local_x = index_x - first_plane
    valid = (local_x >= 0) & (local_x < planes)
    local_x = jnp.where(valid, local_x, planes)
    return field_in.at[0, local_x, index_z, index_y].add(values, mode="drop")


def per_device(
    wave_before,
    wave_current,
    adjoint_far,
    adjoint_near,
    labels,
    table,
    source_index,
    wavelet,
    receiver_index,
    residual,
):
    planes = wave_current.shape[1]
    first_plane = lax.axis_index("dom") * planes
    steps_count = wavelet.shape[1]
    rate = rates(labels, table)[None]
    source_x = source_index[0, 0]
    source_z = source_index[0, 1]
    source_y = source_index[0, 2]
    receiver_x = receiver_index[0, :, 0]
    receiver_z = receiver_index[0, :, 1]
    receiver_y = receiver_index[0, :, 2]
    gradient = jnp.zeros_like(wave_current)
    stored = []
    previous, current = (wave_before, wave_current)
    for step in range(steps_count):
        extended = padded(current, (("dom", 1),), 4)
        lap_current = stencil(extended, current)
        stored.append(lap_current)
        upcoming = 2.0 * current - previous + rate * lap_current
        upcoming = inject(
            upcoming, source_x, source_z, source_y, wavelet[0, step], first_plane, planes
        )
        previous, current = (current, upcoming)
    later, adjoint = (adjoint_far, adjoint_near)
    for step in reversed(range(steps_count)):
        gradient = gradient + adjoint * stored[step]
        scaled = rate * adjoint
        extended = padded(scaled, (("dom", 1),), 4)
        earlier = 2.0 * adjoint - later + stencil(extended, scaled)
        earlier = inject(
            earlier, receiver_x, receiver_z, receiver_y, residual[0, step], first_plane, planes
        )
        later, adjoint = (adjoint, earlier)
    total = lax.psum(gradient[0], "shot")
    return (current, adjoint, total)


def solution(mesh):
    placed = (
        P("shot", "dom", None, None),
        P("shot", "dom", None, None),
        P("shot", "dom", None, None),
        P("shot", "dom", None, None),
        P("dom", None, None),
        P(),
        P("shot", None),
        P("shot", None),
        P("shot", None, None),
        P("shot", None, None),
    )
    return jax.shard_map(
        per_device,
        mesh=mesh,
        in_specs=placed,
        out_specs=(
            P("shot", "dom", None, None),
            P("shot", "dom", None, None),
            P("dom", None, None),
        ),
        check_vma=False,
    )
```

profile of v0, /device:TPU:0, one launch (start us, length us, event | category | flops | bytes accessed | tf_op | source)
XLA Modules:
  0.0 284.2 jit_solution(527471331362998423)
XLA Ops:
  10.4 6.2 %collective-permute-start.1 = (f32[1,4,64,256]{3,2,1,0:T(8,128)}, f32[1,4,64,256]{3,2,1,0:T(8,128)}, u32[]{:S(2)}, u32[]{:S(2)}) collective-permute-start(f32[1,4,64,256]{3,2,1,0:T(8,128)} %get-tuple-element.70), channel_id=1, source_target_pairs={{0,1},{1,2},{2,3},{3,4},{4,5},{5,6},{6,7},{8,9},{9,10},{10,11},{11... | collective-permute-start | bytes 786440 | tf_op jit(solution)/shard_map/ppermute | solution.py:15
  18.3 7.0 %bitcast_multiply_fusion.3 = f32[1,16,64,256]{3,2,1,0:T(8,128)S(1)} fusion(f32[1,16,64,256]{3,2,1,0:T(8,128)} %param.21, f32[]{:T(128)} %bitcast.7, s32[16,64,256]{2,1,0:T(8,128)S(1)} %copy-done, f32[]{:T(128)} %bitcast.6, f32[]{:T(128)} %bitcast.5, f32[]{:T(128)} %bitcast.4, f32[]{:T(128)} %bitcast.3, f32[]{:T(128)} %bitcast.2, f32[]{:T(128)} %bitcast.1, ...), kind=kLoop, calls=%fused_computation.503 | loop fusion | flops 6291456 | bytes 3145760 | tf_op jit(solution)/shard_map/mul | solution.py:93
  27.4 5.5 %collective-permute-start.9 = (f32[1,4,64,256]{3,2,1,0:T(8,128)}, f32[1,4,64,256]{3,2,1,0:T(8,128)}, u32[]{:S(2)}, u32[]{:S(2)}) collective-permute-start(f32[1,4,64,256]{3,2,1,0:T(8,128)} %get-tuple-element.78), channel_id=1, source_target_pairs={{0,1},{1,2},{2,3},{3,4},{4,5},{5,6},{6,7},{8,9},{9,10},{10,11},{11... | collective-permute-start | bytes 786440 | tf_op jit(solution)/shard_map/ppermute | solution.py:15
  42.1 5.0 %fusion.96 = f32[1,16,64,256]{3,2,1,0:T(8,128)S(1)} fusion(f32[1,16,64,256]{3,2,1,0:T(8,128)S(1)} %bitcast_multiply_fusion.3, f32[1,4,64,256]{3,2,1,0:T(8,128)} %collective-permute-done.9, f32[1,4,64,256]{3,2,1,0:T(8,128)S(1)} %collective-permute-done.8, f32[1,16,64,256]{3,2,1,0:T(8,128)} %param.20, f32[1,16,64,256]{3,2,1,0:T(8,128)S(1)} %copy-done.4), kind=kLoop, calls=%fused_computation.312 | loop fusion | flops 10485760 | bytes 4718592 | tf_op jit(solution)/shard_map/add | solution.py:95
  47.6 6.5 %scatter_fusion = f32[262144]{0:T(1024)S(1)} fusion(f32[262144]{0:T(1024)S(1)} %bitcast.57, s32[1024]{0:T(1024)S(1)} %broadcast_select_fusion, f32[1024]{0:T(1024)S(1)} %bitcast.67), kind=kCustom, calls=%fused_computation | custom fusion | flops 1024 | bytes 16384
  54.4 5.7 %bitcast_multiply_fusion.2 = f32[1,16,64,256]{3,2,1,0:T(8,128)S(1)} fusion(f32[1,16,64,256]{3,2,1,0:T(8,128)S(1)} %reshape.240, f32[]{:T(128)} %bitcast.7, s32[16,64,256]{2,1,0:T(8,128)S(1)} %copy-done, f32[]{:T(128)} %bitcast.6, f32[]{:T(128)} %bitcast.5, f32[]{:T(128)} %bitcast.4, f32[]{:T(128)} %bitcast.3, f32[]{:T(128)} %bitcast.2, f32[]{:T(128)} %bitcast.1, ...), kind=kLoop, calls=%fused_computation.502 | loop fusion | flops 6291456 | bytes 3145760 | tf_op jit(solution)/shard_map/mul | solution.py:93
  62.4 5.7 %collective-permute-start.11 = (f32[1,4,64,256]{3,2,1,0:T(8,128)}, f32[1,4,64,256]{3,2,1,0:T(8,128)}, u32[]{:S(2)}, u32[]{:S(2)}) collective-permute-start(f32[1,4,64,256]{3,2,1,0:T(8,128)} %get-tuple-element.76), channel_id=1, source_target_pairs={{0,1},{1,2},{2,3},{3,4},{4,5},{5,6},{6,7},{8,9},{9,10},{10,11},{11... | collective-permute-start | bytes 786440 | tf_op jit(solution)/shard_map/ppermute | solution.py:15
  70.4 8.7 %fusion.266 = (f32[1,16,64,256]{3,2,1,0:T(8,128)S(1)}, f32[1,16,64,256]{3,2,1,0:T(8,128)}) fusion(f32[1,16,64,256]{3,2,1,0:T(8,128)S(1)} %copy-done.15, f32[1,16,64,256]{3,2,1,0:T(8,128)S(1)} %copy-done.11, f32[]{:T(128)} %bitcast.7, s32[16,64,256]{2,1,0:T(8,128)S(1)} %copy-done, f32[]{:T(128)} %bitcast.6, f32[]{:T(128)} %bitcast.5, f32[]{:T(128)} %bitcast.4, ...), kind=kLoop, calls=%fused_computation.508 | loop fusion | flops 14680064 | bytes 13631520 | tf_op jit(solution)/shard_map/add | solution.py:85
  87.8 5.5 %collective-permute-start.3 = (f32[1,4,64,256]{3,2,1,0:T(8,128)}, f32[1,4,64,256]{3,2,1,0:T(8,128)}, u32[]{:S(2)}, u32[]{:S(2)}) collective-permute-start(f32[1,4,64,256]{3,2,1,0:T(8,128)} %get-tuple-element.68), channel_id=1, source_target_pairs={{0,1},{1,2},{2,3},{3,4},{4,5},{5,6},{6,7},{8,9},{9,10},{10,11},{11... | collective-permute-start | bytes 786440 | tf_op jit(solution)/shard_map/ppermute | solution.py:15
  93.3 15.0 %fusion.67 = f32[1,16,64,256]{3,2,1,0:T(8,128)S(1)} fusion(f32[1,16,64,256]{3,2,1,0:T(8,128)} %copy-done.12, f32[1,4,64,256]{3,2,1,0:T(8,128)} %collective-permute-done.11, f32[1,4,64,256]{3,2,1,0:T(8,128)S(1)} %collective-permute-done.10, f32[1,16,64,256]{3,2,1,0:T(8,128)S(1)} %copy-done.5, f32[1,16,64,256]{3,2,1,0:T(8,128)S(1)} %reshape.240), kind=kLoop, calls=%fused_computation.283 | loop fusion | flops 10485760 | bytes 4718592 | tf_op jit(solution)/shard_map/add | solution.py:95
  108.8 6.5 %scatter_fusion.1 = f32[262144]{0:T(1024)S(1)} fusion(f32[262144]{0:T(1024)S(1)} %bitcast.58, s32[1024]{0:T(1024)S(1)} %broadcast_select_fusion, f32[1024]{0:T(1024)S(1)} %bitcast.66), kind=kCustom, calls=%fused_computation.1 | custom fusion | flops 1024 | bytes 16384
  116.5 21.6 %fusion.267 = (f32[1,16,64,256]{3,2,1,0:T(8,128)S(1)}, f32[1,16,64,256]{3,2,1,0:T(8,128)}) fusion(f32[1,16,64,256]{3,2,1,0:T(8,128)} %param.19, f32[1,16,64,256]{3,2,1,0:T(8,128)} %scatter-add.48, f32[]{:T(128)} %bitcast.7, s32[16,64,256]{2,1,0:T(8,128)S(1)} %copy-done, f32[]{:T(128)} %bitcast.6, f32[]{:T(128)} %bitcast.5, f32[]{:T(128)} %bitcast.4, ...), kind=kLoop, calls=%fused_computation.509 | loop fusion | flops 16777216 | bytes 5767200 | tf_op jit(solution)/shard_map/add | solution.py:85
  146.0 5.0 %collective-permute-start.5 = (f32[1,4,64,256]{3,2,1,0:T(8,128)S(1)}, f32[1,4,64,256]{3,2,1,0:T(8,128)S(1)}, u32[]{:S(2)}, u32[]{:S(2)}) collective-permute-start(f32[1,4,64,256]{3,2,1,0:T(8,128)S(1)} %get-tuple-element.66), channel_id=1, source_target_pairs={{0,1},{1,2},{2,3},{3,4},{4,5},{5,6},{6,7},{8,9},{9,10},{10,11},{11... | collective-permute-start | bytes 786440 | tf_op jit(solution)/shard_map/ppermute | solution.py:15
  151.0 5.8 %bitcast_multiply_fusion.1 = f32[1,16,64,256]{3,2,1,0:T(8,128)S(1)} fusion(f32[1,16,64,256]{3,2,1,0:T(8,128)S(1)} %copy-done.1, f32[]{:T(128)} %bitcast.7, s32[16,64,256]{2,1,0:T(8,128)S(1)} %copy-done, f32[]{:T(128)} %bitcast.6, f32[]{:T(128)} %bitcast.5, f32[]{:T(128)} %bitcast.4, f32[]{:T(128)} %bitcast.3, f32[]{:T(128)} %bitcast.2, f32[]{:T(128)} %bitcast.1, ...), kind=kLoop, calls=%fused_computation.501 | loop fusion | flops 6291456 | bytes 3145760 | tf_op jit(solution)/shard_map/mul | solution.py:93
  159.1 6.2 %collective-permute-start.13 = (f32[1,4,64,256]{3,2,1,0:T(8,128)}, f32[1,4,64,256]{3,2,1,0:T(8,128)}, u32[]{:S(2)}, u32[]{:S(2)}) collective-permute-start(f32[1,4,64,256]{3,2,1,0:T(8,128)} %get-tuple-element.74), channel_id=1, source_target_pairs={{0,1},{1,2},{2,3},{3,4},{4,5},{5,6},{6,7},{8,9},{9,10},{10,11},{11... | collective-permute-start | bytes 786440 | tf_op jit(solution)/shard_map/ppermute | solution.py:15
  165.3 10.3 %fusion.268 = (f32[1,16,64,256]{3,2,1,0:T(8,128)S(1)}, f32[1,16,64,256]{3,2,1,0:T(8,128)}) fusion(f32[1,16,64,256]{3,2,1,0:T(8,128)S(1)} %copy-done.7, f32[1,16,64,256]{3,2,1,0:T(8,128)S(1)} %copy-done.9, f32[]{:T(128)} %bitcast.7, s32[16,64,256]{2,1,0:T(8,128)S(1)} %copy-done, f32[]{:T(128)} %bitcast.6, f32[]{:T(128)} %bitcast.5, f32[]{:T(128)} %bitcast.4, ...), kind=kLoop, calls=%fused_computation.510 | loop fusion | flops 16777216 | bytes 5767200 | tf_op jit(solution)/shard_map/add | solution.py:85
  184.4 5.4 %collective-permute-start.7 = (f32[1,4,64,256]{3,2,1,0:T(8,128)}, f32[1,4,64,256]{3,2,1,0:T(8,128)}, u32[]{:S(2)}, u32[]{:S(2)}) collective-permute-start(f32[1,4,64,256]{3,2,1,0:T(8,128)} %get-tuple-element.64), channel_id=1, source_target_pairs={{0,1},{1,2},{2,3},{3,4},{4,5},{5,6},{6,7},{8,9},{9,10},{10,11},{11... | collective-permute-start | bytes 786440 | tf_op jit(solution)/shard_map/ppermute | solution.py:15
  189.9 4.9 %fusion.38 = f32[1,16,64,256]{3,2,1,0:T(8,128)S(1)} fusion(f32[1,16,64,256]{3,2,1,0:T(8,128)S(1)} %copy-done.14, f32[1,4,64,256]{3,2,1,0:T(8,128)} %collective-permute-done.13, f32[1,4,64,256]{3,2,1,0:T(8,128)S(1)} %collective-permute-done.12, f32[1,16,64,256]{3,2,1,0:T(8,128)S(1)} %reshape.240, f32[1,16,64,256]{3,2,1,0:T(8,128)S(1)} %copy-done.1), kind=kLoop, calls=%fused_computation.254 | loop fusion | flops 10485760 | bytes 4718592 | tf_op jit(solution)/shard_map/add | solution.py:95
  195.3 6.5 %scatter_fusion.2 = f32[262144]{0:T(1024)S(1)} fusion(f32[262144]{0:T(1024)S(1)} %bitcast.59, s32[1024]{0:T(1024)S(1)} %broadcast_select_fusion, f32[1024]{0:T(1024)S(1)} %bitcast.65), kind=kCustom, calls=%fused_computation.2 | custom fusion | flops 1024 | bytes 16384
  203.1 18.2 %add_bitcast_fusion = (f32[16,64,256]{2,1,0:T(8,128)}, f32[1,16,64,256]{3,2,1,0:T(8,128)}) fusion(f32[1,16,64,256]{3,2,1,0:T(8,128)} %reshape.248, f32[1,16,64,256]{3,2,1,0:T(8,128)} %get-tuple-element.58, f32[1,16,64,256]{3,2,1,0:T(8,128)} %reshape.244, f32[1,16,64,256]{3,2,1,0:T(8,128)} %get-tuple-element.56, f32[1,16,64,256]{3,2,1,0:T(8,128)S(1)} %reshape.240, ...), kind=kLoop, calls=%fused_computation.512 | loop fusion | flops 11534336 | bytes 11010048 | tf_op jit(solution)/shard_map/squeeze | solution.py:100
  221.3 8.7 %bitcast_multiply_fusion = (f32[1,16,64,256]{3,2,1,0:T(8,128)S(1)}, f32[1,16,64,256]{3,2,1,0:T(8,128)}) fusion(f32[1,16,64,256]{3,2,1,0:T(8,128)S(1)} %copy-done.3, f32[]{:T(128)} %bitcast.7, s32[16,64,256]{2,1,0:T(8,128)S(1)} %copy-done, f32[]{:T(128)} %bitcast.6, f32[]{:T(128)} %bitcast.5, f32[]{:T(128)} %bitcast.4, f32[]{:T(128)} %bitcast.3, f32[]{:T(128)} %bitcast.2, ...), kind=kLoop, calls=%fused_computation.500 | loop fusion | flops 7340032 | bytes 7340064 | tf_op jit(solution)/shard_map/mul | solution.py:93
  232.1 5.7 %collective-permute-start.15 = (f32[1,4,64,256]{3,2,1,0:T(8,128)}, f32[1,4,64,256]{3,2,1,0:T(8,128)}, u32[]{:S(2)}, u32[]{:S(2)}) collective-permute-start(f32[1,4,64,256]{3,2,1,0:T(8,128)} %get-tuple-element.60), channel_id=1, source_target_pairs={{0,1},{1,2},{2,3},{3,4},{4,5},{5,6},{6,7},{8,9},{9,10},{10,11},{11... | collective-permute-start | bytes 786440 | tf_op jit(solution)/shard_map/ppermute | solution.py:15
  250.3 6.5 %scatter_fusion.3 = f32[262144]{0:T(1024)S(1)} fusion(f32[262144]{0:T(1024)S(1)} %bitcast.56, s32[1024]{0:T(1024)S(1)} %broadcast_select_fusion, f32[1024]{0:T(1024)S(1)} %bitcast.64), kind=kCustom, calls=%fused_computation.3 | custom fusion | flops 1024 | bytes 16384
  258.0 17.0 %all-reduce.10.cloned.1.call-done = f32[16,64,256]{2,1,0:T(8,128)} async-done(((f32[16,64,256]{2,1,0:T(8,128)}), f32[16,64,256]{2,1,0:T(8,128)}) %all-reduce.10.cloned.1.call-update) | async-done | bytes 1048592 | tf_op jit(solution)/shard_map/psum | solution.py:100
  (111 shorter events, 59.0 us)
Async XLA Ops:
  7.2 267.9 %all-reduce.10.cloned.1.call-start = ((), (), s32[]{:S(2)}) async-start(), calls=%async_computation | async-start | bytes 2097152 | tf_op jit(solution)/shard_map/psum | solution.py:100
  9.2 60.2 %collective-permute-start = (f32[1,4,64,256]{3,2,1,0:T(8,128)}, f32[1,4,64,256]{3,2,1,0:T(8,128)}, u32[]{:S(2)}, u32[]{:S(2)}) collective-permute-start(f32[1,4,64,256]{3,2,1,0:T(8,128)} %get-tuple-element.69), channel_id=1, source_target_pairs={{1,0},{2,1},{3,2},{4,3},{5,4},{6,5},{7,6},{9,8},{10,9},{11,10},{12... | collective-permute-start | bytes 786440 | tf_op jit(solution)/shard_map/ppermute | solution.py:18
  10.4 57.7 %collective-permute-start.1 = (f32[1,4,64,256]{3,2,1,0:T(8,128)}, f32[1,4,64,256]{3,2,1,0:T(8,128)}, u32[]{:S(2)}, u32[]{:S(2)}) collective-permute-start(f32[1,4,64,256]{3,2,1,0:T(8,128)} %get-tuple-element.70), channel_id=1, source_target_pairs={{0,1},{1,2},{2,3},{3,4},{4,5},{5,6},{6,7},{8,9},{9,10},{10,11},{11... | collective-permute-start | bytes 786440 | tf_op jit(solution)/shard_map/ppermute | solution.py:15
  18.3 18.3 %copy-start.17 = (s32[1,1024,3]{1,0,2:T(1,128)S(1)}, s32[1,1024,3]{1,0,2:T(1,128)}, u32[]{:S(2)}) copy-start(s32[1,1024,3]{1,0,2:T(1,128)} %param.26) | copy-start | bytes 36868
  18.3 18.4 %copy-start.20 = (s32[4]{0:T(128)S(1)}, s32[4]{0:T(128)}, u32[]{:S(2)}) copy-start(s32[4]{0:T(128)} %constant.158) | copy-start | bytes 52
  18.3 18.5 %copy-start.22 = (s32[4]{0:T(128)S(1)}, s32[4]{0:T(128)}, u32[]{:S(2)}) copy-start(s32[4]{0:T(128)} %constant.155) | copy-start | bytes 52
  18.3 19.8 %copy-start.21 = (s32[4]{0:T(128)S(1)}, s32[4]{0:T(128)}, u32[]{:S(2)}) copy-start(s32[4]{0:T(128)} %constant.129.clone.1) | copy-start | bytes 52
  18.3 20.5 %copy-start.18 = (f32[1,4]{1,0:T(1,128)S(1)}, f32[1,4]{1,0:T(1,128)}, u32[]{:S(2)}) copy-start(f32[1,4]{1,0:T(1,128)} %param.25) | copy-start | bytes 52
  18.3 21.2 %copy-start.16 = (f32[1,4,1024]{2,1,0:T(4,128)S(1)}, f32[1,4,1024]{2,1,0:T(4,128)}, u32[]{:S(2)}) copy-start(f32[1,4,1024]{2,1,0:T(4,128)} %param.27) | copy-start | bytes 49156
  26.2 13.4 %collective-permute-start.8 = (f32[1,4,64,256]{3,2,1,0:T(8,128)}, f32[1,4,64,256]{3,2,1,0:T(8,128)S(1)}, u32[]{:S(2)}, u32[]{:S(2)}) collective-permute-start(f32[1,4,64,256]{3,2,1,0:T(8,128)} %get-tuple-element.77), channel_id=1, source_target_pairs={{1,0},{2,1},{3,2},{4,3},{5,4},{6,5},{7,6},{9,8},{10,9},{11,10},{12... | collective-permute-start | bytes 786440 | tf_op jit(solution)/shard_map/ppermute | solution.py:18
  27.4 14.7 %collective-permute-start.9 = (f32[1,4,64,256]{3,2,1,0:T(8,128)}, f32[1,4,64,256]{3,2,1,0:T(8,128)}, u32[]{:S(2)}, u32[]{:S(2)}) collective-permute-start(f32[1,4,64,256]{3,2,1,0:T(8,128)} %get-tuple-element.78), channel_id=1, source_target_pairs={{0,1},{1,2},{2,3},{3,4},{4,5},{5,6},{6,7},{8,9},{9,10},{10,11},{11... | collective-permute-start | bytes 786440 | tf_op jit(solution)/shard_map/ppermute | solution.py:15
  61.0 32.3 %collective-permute-start.10 = (f32[1,4,64,256]{3,2,1,0:T(8,128)}, f32[1,4,64,256]{3,2,1,0:T(8,128)S(1)}, u32[]{:S(2)}, u32[]{:S(2)}) collective-permute-start(f32[1,4,64,256]{3,2,1,0:T(8,128)} %get-tuple-element.75), channel_id=1, source_target_pairs={{1,0},{2,1},{3,2},{4,3},{5,4},{6,5},{7,6},{9,8},{10,9},{11,10},{12... | collective-permute-start | bytes 786440 | tf_op jit(solution)/shard_map/ppermute | solution.py:18
  62.4 30.9 %collective-permute-start.11 = (f32[1,4,64,256]{3,2,1,0:T(8,128)}, f32[1,4,64,256]{3,2,1,0:T(8,128)}, u32[]{:S(2)}, u32[]{:S(2)}) collective-permute-start(f32[1,4,64,256]{3,2,1,0:T(8,128)} %get-tuple-element.76), channel_id=1, source_target_pairs={{0,1},{1,2},{2,3},{3,4},{4,5},{5,6},{6,7},{8,9},{9,10},{10,11},{11... | collective-permute-start | bytes 786440 | tf_op jit(solution)/shard_map/ppermute | solution.py:15
  86.5 30.0 %collective-permute-start.2 = (f32[1,4,64,256]{3,2,1,0:T(8,128)}, f32[1,4,64,256]{3,2,1,0:T(8,128)}, u32[]{:S(2)}, u32[]{:S(2)}) collective-permute-start(f32[1,4,64,256]{3,2,1,0:T(8,128)} %get-tuple-element.67), channel_id=1, source_target_pairs={{1,0},{2,1},{3,2},{4,3},{5,4},{6,5},{7,6},{9,8},{10,9},{11,10},{12... | collective-permute-start | bytes 786440 | tf_op jit(solution)/shard_map/ppermute | solution.py:18
  87.8 28.7 %collective-permute-start.3 = (f32[1,4,64,256]{3,2,1,0:T(8,128)}, f32[1,4,64,256]{3,2,1,0:T(8,128)}, u32[]{:S(2)}, u32[]{:S(2)}) collective-permute-start(f32[1,4,64,256]{3,2,1,0:T(8,128)} %get-tuple-element.68), channel_id=1, source_target_pairs={{0,1},{1,2},{2,3},{3,4},{4,5},{5,6},{6,7},{8,9},{9,10},{10,11},{11... | collective-permute-start | bytes 786440 | tf_op jit(solution)/shard_map/ppermute | solution.py:15
  144.7 20.5 %collective-permute-start.4 = (f32[1,4,64,256]{3,2,1,0:T(8,128)S(1)}, f32[1,4,64,256]{3,2,1,0:T(8,128)S(1)}, u32[]{:S(2)}, u32[]{:S(2)}) collective-permute-start(f32[1,4,64,256]{3,2,1,0:T(8,128)S(1)} %get-tuple-element.65), channel_id=1, source_target_pairs={{1,0},{2,1},{3,2},{4,3},{5,4},{6,5},{7,6},{9,8},{10,9},{11,10},{12... | collective-permute-start | bytes 786440 | tf_op jit(solution)/shard_map/ppermute | solution.py:18
  146.0 19.2 %collective-permute-start.5 = (f32[1,4,64,256]{3,2,1,0:T(8,128)S(1)}, f32[1,4,64,256]{3,2,1,0:T(8,128)S(1)}, u32[]{:S(2)}, u32[]{:S(2)}) collective-permute-start(f32[1,4,64,256]{3,2,1,0:T(8,128)S(1)} %get-tuple-element.66), channel_id=1, source_target_pairs={{0,1},{1,2},{2,3},{3,4},{4,5},{5,6},{6,7},{8,9},{9,10},{10,11},{11... | collective-permute-start | bytes 786440 | tf_op jit(solution)/shard_map/ppermute | solution.py:15
  157.7 32.2 %collective-permute-start.12 = (f32[1,4,64,256]{3,2,1,0:T(8,128)}, f32[1,4,64,256]{3,2,1,0:T(8,128)S(1)}, u32[]{:S(2)}, u32[]{:S(2)}) collective-permute-start(f32[1,4,64,256]{3,2,1,0:T(8,128)} %get-tuple-element.73), channel_id=1, source_target_pairs={{1,0},{2,1},{3,2},{4,3},{5,4},{6,5},{7,6},{9,8},{10,9},{11,10},{12... | collective-permute-start | bytes 786440 | tf_op jit(solution)/shard_map/ppermute | solution.py:18
  159.1 30.8 %collective-permute-start.13 = (f32[1,4,64,256]{3,2,1,0:T(8,128)}, f32[1,4,64,256]{3,2,1,0:T(8,128)}, u32[]{:S(2)}, u32[]{:S(2)}) collective-permute-start(f32[1,4,64,256]{3,2,1,0:T(8,128)} %get-tuple-element.74), channel_id=1, source_target_pairs={{0,1},{1,2},{2,3},{3,4},{4,5},{5,6},{6,7},{8,9},{9,10},{10,11},{11... | collective-permute-start | bytes 786440 | tf_op jit(solution)/shard_map/ppermute | solution.py:15
  183.2 19.9 %collective-permute-start.6 = (f32[1,4,64,256]{3,2,1,0:T(8,128)}, f32[1,4,64,256]{3,2,1,0:T(8,128)}, u32[]{:S(2)}, u32[]{:S(2)}) collective-permute-start(f32[1,4,64,256]{3,2,1,0:T(8,128)} %get-tuple-element.63), channel_id=1, source_target_pairs={{1,0},{2,1},{3,2},{4,3},{5,4},{6,5},{7,6},{9,8},{10,9},{11,10},{12... | collective-permute-start | bytes 786440 | tf_op jit(solution)/shard_map/ppermute | solution.py:18
  184.4 18.6 %collective-permute-start.7 = (f32[1,4,64,256]{3,2,1,0:T(8,128)}, f32[1,4,64,256]{3,2,1,0:T(8,128)}, u32[]{:S(2)}, u32[]{:S(2)}) collective-permute-start(f32[1,4,64,256]{3,2,1,0:T(8,128)} %get-tuple-element.64), channel_id=1, source_target_pairs={{0,1},{1,2},{2,3},{3,4},{4,5},{5,6},{6,7},{8,9},{9,10},{10,11},{11... | collective-permute-start | bytes 786440 | tf_op jit(solution)/shard_map/ppermute | solution.py:15
  203.1 18.2 %copy-start.3 = (f32[1,16,64,256]{3,2,1,0:T(8,128)S(1)}, f32[1,16,64,256]{3,2,1,0:T(8,128)}, u32[]{:S(2)}) copy-start(f32[1,16,64,256]{3,2,1,0:T(8,128)} %reshape.248) | copy-start | bytes 3145732
  230.8 12.2 %collective-permute-start.14 = (f32[1,4,64,256]{3,2,1,0:T(8,128)}, f32[1,4,64,256]{3,2,1,0:T(8,128)S(1)}, u32[]{:S(2)}, u32[]{:S(2)}) collective-permute-start(f32[1,4,64,256]{3,2,1,0:T(8,128)} %get-tuple-element.59), channel_id=1, source_target_pairs={{1,0},{2,1},{3,2},{4,3},{5,4},{6,5},{7,6},{9,8},{10,9},{11,10},{12... | collective-permute-start | bytes 786440 | tf_op jit(solution)/shard_map/ppermute | solution.py:18
  232.1 12.9 %collective-permute-start.15 = (f32[1,4,64,256]{3,2,1,0:T(8,128)}, f32[1,4,64,256]{3,2,1,0:T(8,128)}, u32[]{:S(2)}, u32[]{:S(2)}) collective-permute-start(f32[1,4,64,256]{3,2,1,0:T(8,128)} %get-tuple-element.60), channel_id=1, source_target_pairs={{0,1},{1,2},{2,3},{3,4},{4,5},{5,6},{6,7},{8,9},{9,10},{10,11},{11... | collective-permute-start | bytes 786440 | tf_op jit(solution)/shard_map/ppermute | solution.py:15
  (16 other events, 146.9 us)
Sparse Core Ops, SparseCore 0:
  237.9 37.0 all-reduce.9
where the time goes:
time: 286 us; the launch traced here: 284 us
  other arithmetic  148 us (52%)
  starting transfers between devices  55.7 us (19%)
  local copies, waits for them, and re-layouts  32.3 us (11%)
  between operations  26.5 us (9%)
  waiting for transfers between devices  21.6 us (8%)
    ppermute x8, starting transfers between devices, padded(): lax.ppermute(lax.slice_in_dim(block, block.shape[dim] - width, None, axis...  45.1 us
    add x3, other arithmetic, per_device(): upcoming = 2.0 * current - previous + rate * lap_current  40.6 us
    add x4, other arithmetic, per_device(): earlier = 2.0 * adjoint - later + stencil(extended, scaled)  29.6 us
    mul x4, other arithmetic, per_device(): scaled = rate * adjoint  27.2 us
    unnamed x7, other arithmetic  26 us
    squeeze x1, other arithmetic, per_device(): total = lax.psum(gradient[0], 'shot')  18.2 us
    psum x1, waiting for transfers between devices, per_device(): total = lax.psum(gradient[0], 'shot')  17 us
    ppermute x8, starting transfers between devices, padded(): lax.ppermute(lax.slice_in_dim(block, 0, width, axis=dim), axis, backward)  10.5 us
  transfers between devices with their start and end apart: 17, of which 3 were waited for; matrix products, arithmetic and copies ran while one was open for 42% of the time, Pallas kernels for 0%

commit v1 on v0

v1 whole, which is shorter than its diff:
```python
import functools

import jax
import jax.numpy as jnp
from jax import lax
from jax.experimental import pallas as pl
from jax.experimental.pallas import tpu as pltpu
from jax.sharding import PartitionSpec as P

centre_coef = -205.0 / 72.0
side_coefs = (8.0 / 5.0, -1.0 / 5.0, 8.0 / 315.0, -1.0 / 560.0)
unit = 5040.0
side_units = (8064.0, -1008.0, 128.0, -9.0)
halo = 4

vmem = pl.BlockSpec(memory_space=pltpu.VMEM)
smem = pl.BlockSpec(memory_space=pltpu.SMEM)


def call(kernel, args, in_specs, out_shapes, scratch=(), flops=0):
    moved = sum(a.size * a.dtype.itemsize for a in args) + sum(4 * s.size for s in out_shapes)
    return pl.pallas_call(
        kernel,
        out_shape=out_shapes,
        in_specs=in_specs,
        out_specs=[vmem] * len(out_shapes),
        scratch_shapes=list(scratch),
        compiler_params=pltpu.CompilerParams(vmem_limit_bytes=24 * 1024 * 1024),
        cost_estimate=pl.CostEstimate(flops=flops, bytes_accessed=moved, transcendentals=0),
    )(*args)


def f32(*shape):
    return jax.ShapeDtypeStruct(shape, jnp.float32)


def band(size, block):
    row = lax.broadcasted_iota(jnp.int32, (size, size), 0)
    col = lax.broadcasted_iota(jnp.int32, (size, size), 1)
    apart = jnp.abs(row - col)
    value = jnp.zeros((size, size), jnp.float32)
    for k in range(1, 5):
        value = jnp.where(apart == k, side_units[k - 1], value)
    if block != size:
        value = jnp.where(lax.div(row, block) == lax.div(col, block), value, 0.0)
    return value.astype(jnp.bfloat16)


def pieces(value):
    high = value.astype(jnp.bfloat16)
    rest = value - high.astype(jnp.float32)
    middle = rest.astype(jnp.bfloat16)
    low = (rest - middle.astype(jnp.float32)).astype(jnp.bfloat16)
    return high, middle, low


def dot(a, b):
    return lax.dot_general(a, b, (((1,), (0,)), ((), ())), preferred_element_type=jnp.float32)


def laplacian(ext, first, group, along_y, along_z):
    _, nz, ny = ext.shape
    centre = ext[pl.ds(first + halo, group)]
    high, middle, low = pieces(centre.reshape(group * nz, ny))
    across = dot(low, along_y) + dot(along_z, low)
    across = across + (dot(middle, along_y) + dot(along_z, middle))
    across = across + (dot(high, along_y) + dot(along_z, high))
    result = 3.0 * centre_coef * centre + across.reshape(group, nz, ny) * (1.0 / unit)
    for k in range(1, 5):
        result = result + side_coefs[k - 1] * (
            ext[pl.ds(first + halo + k, group)] + ext[pl.ds(first + halo - k, group)]
        )
    return result


def group_of(planes, nz):
    group = max(1, min(planes, 256 // nz))
    while planes % group:
        group -= 1
    return group


def place(ext, info, near, far):
    planes = ext.shape[0] - 2 * halo
    odd = info[0]
    spot = jnp.where(odd == 1, 0, planes + halo)
    ext[pl.ds(spot, halo)] = near[...]
    ext[pl.ds(planes + halo - spot, halo)] = far[...]


def edge_spots(info, planes):
    odd = info[0]
    near = jnp.where(odd == 1, 0, planes - halo)
    return near, planes - halo - near


def prepare_kernel(info, table, labels, field, rate, near_edge, far_edge):
    value = jnp.zeros(labels.shape, jnp.float32)
    label = labels[...]
    for region in range(table.shape[0]):
        value = jnp.where(label == region, table[region], value)
    rate[...] = value
    near, far = edge_spots(info, labels.shape[0])
    near_edge[...] = rate[pl.ds(near, halo)] * field[pl.ds(near, halo)]
    far_edge[...] = rate[pl.ds(far, halo)] * field[pl.ds(far, halo)]


def receivers_kernel(info, index, values, injected):
    steps, planes, nz, ny = injected.shape
    count = index.shape[1]
    local = index[0:1, :] - info[1]
    cell = jnp.where((local >= 0) & (local < planes), local * nz + index[1:2, :], -1)
    at_y = lax.broadcasted_iota(jnp.int32, (ny, count), 0) == index[2:3, :]
    parts = []
    for step in range(steps):
        for piece in pieces(values[step : step + 1, :]):
            spread = jnp.where(at_y, piece.astype(jnp.float32), 0.0)
            parts.append(spread.astype(jnp.bfloat16))
    group = group_of(planes, nz)
    rows = group * nz
    for part in range(planes // group):
        at_cell = lax.broadcasted_iota(jnp.int32, (rows, count), 0) + part * rows == cell
        picked = jnp.where(at_cell, 1.0, 0.0).astype(jnp.bfloat16)
        for step in range(steps):
            total = None
            for piece in reversed(parts[3 * step : 3 * step + 3]):
                term = lax.dot_general(
                    picked, piece, (((1,), (1,)), ((), ())), preferred_element_type=jnp.float32
                )
                total = term if total is None else total + term
            injected[step, pl.ds(part * group, group)] = total.reshape(group, nz, ny)


def forward_kernel(step, with_edges, info, source, wavelet, *refs):
    if with_edges:
        current, previous, near, far, rate, upcoming, lap, near_edge, far_edge, ext = refs
    else:
        current, previous, near, far, rate, partial, adjoint, upcoming, keep, send, ext = refs
    planes, nz, ny = current.shape
    place(ext, info, near, far)
    ext[pl.ds(halo, planes)] = current[...]
    group = group_of(planes, nz)
    along_y = band(ny, ny)
    along_z = band(group * nz, nz)
    half = planes // 2
    for part in range(planes // group):
        first = part * group
        here = pl.ds(first, group)
        value = laplacian(ext, first, group, along_y, along_z)
        upcoming[here] = 2.0 * current[here] - previous[here] + rate[here] * value
        if with_edges:
            lap[here] = value
        else:
            ext[here] = partial[here] + adjoint[here] * value
    x = source[0, 0] - info[1]
    z = source[0, 1]
    y = source[0, 2]

    @pl.when((x >= 0) & (x < planes))
    def _():
        base = pl.multiple_of(lax.div(z, 8) * 8, 8)
        rows = lax.broadcasted_iota(jnp.int32, (8, ny), 0)
        cols = lax.broadcasted_iota(jnp.int32, (8, ny), 1)
        hit = (rows == z - base) & (cols == y)
        tile = upcoming[x, pl.ds(base, 8), :]
        upcoming[x, pl.ds(base, 8), :] = tile + jnp.where(hit, wavelet[0, step], 0.0)

    if with_edges:
        near_at, far_at = edge_spots(info, planes)
        near_edge[...] = upcoming[pl.ds(near_at, halo)]
        far_edge[...] = upcoming[pl.ds(far_at, halo)]
    else:
        mine = info[2] * half
        keep[...] = ext[pl.ds(mine, half)]
        send[...] = ext[pl.ds(half - mine, half)]


def adjoint_kernel(step, kind, info, *refs):
    if kind == "first":
        current, later, near, far, rate, injected, earlier, near_edge, far_edge, ext = refs
    elif kind == "third":
        (current, later, near, far, rate, injected, lap1, lap2, lap3,
         earlier, near_edge, far_edge, partial, ext) = refs
    else:
        current, later, near, far, rate, injected, earlier, ext = refs
    planes, nz, ny = current.shape
    place(ext, info, near, far)
    ext[pl.ds(halo, planes)] = rate[...] * current[...]
    group = group_of(planes, nz)
    along_y = band(ny, ny)
    along_z = band(group * nz, nz)
    for part in range(planes // group):
        first = part * group
        here = pl.ds(first, group)
        value = laplacian(ext, first, group, along_y, along_z)
        value = 2.0 * current[here] - later[here] + value + injected[step, here]
        earlier[here] = value
        if kind == "third":
            partial[here] = (
                later[here] * lap3[here] + current[here] * lap2[here] + value * lap1[here]
            )
    if kind != "last":
        near_at, far_at = edge_spots(info, planes)
        near_edge[...] = rate[pl.ds(near_at, halo)] * earlier[pl.ds(near_at, halo)]
        far_edge[...] = rate[pl.ds(far_at, halo)] * earlier[pl.ds(far_at, halo)]


def assemble_kernel(info, kept, got, total):
    half = kept.shape[0]
    mine = info[2] * half
    total[pl.ds(mine, half)] = kept[...]
    total[pl.ds(half - mine, half)] = got[...]


def swap(near_edge, far_edge):
    count = lax.axis_size("dom")
    near_pairs = [(i, i ^ 1) for i in range(count) if i ^ 1 < count]
    far_pairs = [(i, i + 1) for i in range(1, count - 1, 2)]
    far_pairs = far_pairs + [(b, a) for a, b in far_pairs]
    return (
        lax.ppermute(near_edge, "dom", near_pairs),
        lax.ppermute(far_edge, "dom", far_pairs),
    )


def per_device(
    wave_before,
    wave_current,
    adjoint_far,
    adjoint_near,
    labels,
    table,
    source_index,
    wavelet,
    receiver_index,
    residual,
):
    planes, nz, ny = wave_current.shape[1:]
    steps = wavelet.shape[1]
    place_x = lax.axis_index("dom")
    shot = lax.axis_index("shot")
    odd = place_x % 2
    info = jnp.stack([odd, place_x * planes, shot % 2]).astype(jnp.int32)
    u0, u1 = wave_before[0], wave_current[0]
    a6, a5 = adjoint_far[0], adjoint_near[0]
    block = f32(planes, nz, ny)
    edge = f32(halo, nz, ny)
    scratch = [pltpu.VMEM((planes + 2 * halo, nz, ny), jnp.float32)]
    cells = planes * nz * ny

    near_at = jnp.where(odd == 1, 0, planes - halo)
    near_edge = lax.dynamic_slice_in_dim(u1, near_at, halo, axis=0)
    far_edge = lax.dynamic_slice_in_dim(u1, planes - halo - near_at, halo, axis=0)
    u_halo = swap(near_edge, far_edge)

    rate, near_edge, far_edge = call(
        prepare_kernel, (info, table, labels, a5), [smem, smem, vmem, vmem], [block, edge, edge]
    )
    a_halo = swap(near_edge, far_edge)

    (injected,) = call(
        receivers_kernel,
        (info, receiver_index[0].T, residual[0]),
        [smem, vmem, vmem],
        [f32(steps, planes, nz, ny)],
        flops=2 * steps * 3 * cells * residual.shape[2],
    )

    work = 12 * cells * 256
    laps = []
    previous, current = u0, u1
    later, adjoint = a6, a5
    for n in range(steps):
        if n < steps - 1:
            upcoming, lap, near_edge, far_edge = call(
                functools.partial(forward_kernel, n, True),
                (info, source_index, wavelet, current, previous, *u_halo, rate),
                [smem] * 3 + [vmem] * 5,
                [block, block, edge, edge],
                scratch,
                work,
            )
            laps.append(lap)
            u_halo = swap(near_edge, far_edge)
        else:
            half = f32(planes // 2, nz, ny)
            upcoming, keep, send = call(
                functools.partial(forward_kernel, n, False),
                (info, source_index, wavelet, current, previous, *u_halo, rate, partial, a5),
                [smem] * 3 + [vmem] * 7,
                [block, half, half],
                scratch,
                work,
            )
        previous, current = current, upcoming
        step = steps - 1 - n
        if n == steps - 1:
            (earlier,) = call(
                functools.partial(adjoint_kernel, step, "last"),
                (info, adjoint, later, *a_halo, rate, injected),
                [smem] + [vmem] * 6,
                [block],
                scratch,
                work,
            )
        elif n == steps - 2:
            earlier, near_edge, far_edge, partial = call(
                functools.partial(adjoint_kernel, step, "third"),
                (info, adjoint, later, *a_halo, rate, injected, *laps),
                [smem] + [vmem] * 9,
                [block, edge, edge, block],
                scratch,
                work,
            )
            a_halo = swap(near_edge, far_edge)
        else:
            earlier, near_edge, far_edge = call(
                functools.partial(adjoint_kernel, step, "first"),
                (info, adjoint, later, *a_halo, rate, injected),
                [smem] + [vmem] * 6,
                [block, edge, edge],
                scratch,
                work,
            )
            a_halo = swap(near_edge, far_edge)
        later, adjoint = adjoint, earlier

    shots = lax.axis_size("shot")
    pairs = [(i, i ^ 1) for i in range(shots)]
    across = [(i, i ^ 2) for i in range(shots)]
    kept = keep + lax.ppermute(send, "shot", pairs)
    kept = kept + lax.ppermute(kept, "shot", across)
    got = lax.ppermute(kept, "shot", pairs)
    (total,) = call(
        assemble_kernel, (info, kept, got), [smem, vmem, vmem], [block]
    )
    return (current[None], adjoint[None], total)


def solution(mesh):
    placed = (
        P("shot", "dom", None, None),
        P("shot", "dom", None, None),
        P("shot", "dom", None, None),
        P("shot", "dom", None, None),
        P("dom", None, None),
        P(),
        P("shot", None),
        P("shot", None),
        P("shot", None, None),
        P("shot", None, None),
    )
    return jax.shard_map(
        per_device,
        mesh=mesh,
        in_specs=placed,
        out_specs=(
            P("shot", "dom", None, None),
            P("shot", "dom", None, None),
            P("dom", None, None),
        ),
        check_vma=False,
    )
```

time: 286 us -> 132 us (0.46)
  other arithmetic: 148 us -> 0.24 us
  waiting for transfers between devices: 21.6 us -> 57.4 us
  Pallas kernels: 0 us -> 32.1 us
  between operations: 26.5 us -> 0.9 us
  local copies, waits for them, and re-layouts: 32.3 us -> 8.68 us
  starting transfers between devices: 55.7 us -> 32.1 us
    add x11 -> x2, other arithmetic: 76 us -> 0.17 us  [the longest x1 0.1 us: per_device(): kept = keep + lax.ppermute(send, 'shot', pairs)]
    ppermute x16 -> x19, waiting for transfers between devices: 4.54 us -> 57.4 us  [the longest x8 43 us: swap(): lax.ppermute(near_edge, 'dom', near_pairs)]
    pallas_call x0 -> x11, Pallas kernels: none -> 32.1 us  [call(): pl.pallas_call(kernel, out_shape=out_shapes, in_specs=in_specs, out_specs...]
    mul x4 -> x0, other arithmetic: 27.2 us -> none  [per_device(): scaled = rate * adjoint]
    unnamed x7 -> x0, other arithmetic: 26 us -> none
    ppermute x16 -> x19, starting transfers between devices: 55.6 us -> 32.1 us  [the longest x8 24.9 us: swap(): lax.ppermute(near_edge, 'dom', near_pairs)]
    squeeze x1 -> x0, other arithmetic: 18.2 us -> none  [per_device(): total = lax.psum(gradient[0], 'shot')]
    psum x1 -> x0, waiting for transfers between devices: 17 us -> none  [per_device(): total = lax.psum(gradient[0], 'shot')]
  transfers between devices with their start and end apart: 17 -> 19, of which waited for: 3 -> 8; matrix products, arithmetic and copies ran while one was open for 42% -> 1% of each run, Pallas kernels for 0% -> 21%
where the time goes in v1:
time: 132 us; the launch traced here: 131 us
  waiting for transfers between devices  57.4 us (43%)
  starting transfers between devices  32.1 us (24%)
  Pallas kernels  32.1 us (24%)
  local copies, waits for them, and re-layouts  8.68 us (7%)
    ppermute x8, waiting for transfers between devices, swap(): lax.ppermute(near_edge, 'dom', near_pairs)  43 us
    pallas_call x11, Pallas kernels, call(): pl.pallas_call(kernel, out_shape=out_shapes, in_specs=in_specs, out_specs...  32.1 us
    ppermute x8, starting transfers between devices, swap(): lax.ppermute(near_edge, 'dom', near_pairs)  24.9 us
    ppermute x1, waiting for transfers between devices, per_device(): kept = kept + lax.ppermute(kept, 'shot', across)  12.4 us
    unnamed x25, local copies, waits for them, and re-layouts  7.61 us
    ppermute x8, starting transfers between devices, swap(): lax.ppermute(far_edge, 'dom', far_pairs)  5.51 us
  transfers between devices with their start and end apart: 19, of which 8 were waited for; matrix products, arithmetic and copies ran while one was open for 1% of the time, Pallas kernels for 21%

profile of v1, /device:TPU:0, one launch (start us, length us, event | category | flops | bytes accessed | tf_op | source)
XLA Modules:
  0.0 131.3 jit_solution(11063220546680006748)
XLA Ops:
  2.4 5.8 %collective-permute-start = (f32[4,64,256]{2,1,0:T(8,128)S(1)}, f32[4,64,256]{2,1,0:T(8,128)S(1)}, u32[]{:S(2)}, u32[]{:S(2)}) collective-permute-start(f32[4,64,256]{2,1,0:T(8,128)S(1)} %get-tuple-element.60), channel_id=1, source_target_pairs={{0,1},{1,0},{2,3},{3,2},{4,5},{5,4},{6,7},{7,6},{8,9},{9,8},{10,11... | collective-permute-start | bytes 786440 | tf_op jit(solution)/shard_map/ppermute | solution.py:221
  11.4 1.6 %shard_map.121 = (f32[16,64,256]{2,1,0:T(8,128)S(1)}, f32[4,64,256]{2,1,0:T(8,128)S(1)}, f32[4,64,256]{2,1,0:T(8,128)S(1)}) custom-call(s32[3]{0:T(128)S(1)} %pad_add_fusion.info, f32[8]{0:T(128)S(1)} %copy-done.10, s32[16,64,256]{2,1,0:T(8,128)S(1)} %copy-done.6, f32[16,64,256]{2,1,0:T(8,128)S(1)} %bitcast.19), custom_call_target="tpu_custom_call" | custom-call | bytes 3670060 | tf_op jit(solution)/shard_map/pallas_call | solution.py:22
  14.5 9.9 %collective-permute-done.refs_2_ = f32[4,64,256]{2,1,0:T(8,128)S(1)} collective-permute-done((f32[4,64,256]{2,1,0:T(8,128)S(1)}, f32[4,64,256]{2,1,0:T(8,128)S(1)}, u32[]{:S(2)}, u32[]{:S(2)}) %collective-permute-start) | collective-permute-done | bytes 262176 | tf_op jit(solution)/shard_map/ppermute | solution.py:221
  28.1 2.4 %shard_map.122 = (f32[16,64,256]{2,1,0:T(8,128)S(1)}, f32[16,64,256]{2,1,0:T(8,128)S(1)}, f32[4,64,256]{2,1,0:T(8,128)S(1)}, f32[4,64,256]{2,1,0:T(8,128)S(1)}) custom-call(s32[3]{0:T(128)S(1)} %pad_add_fusion.info, s32[1,3]{1,0:T(1,128)S(1)} %copy-done.7, f32[1,4]{1,0:T(1,128)S(1)} %copy-done.8, f32[16,64,256]{2,1,0:T(8,128)S(1)} %bitcast.23, ...), custom_call_target="tpu_custom_call" | custom-call | flops 805306368 | bytes 6291496 | tf_op jit(solution)/shard_map/pallas_call | solution.py:22
  30.5 2.5 %collective-permute-start.2 = (f32[4,64,256]{2,1,0:T(8,128)S(1)}, f32[4,64,256]{2,1,0:T(8,128)S(1)}, u32[]{:S(2)}, u32[]{:S(2)}) collective-permute-start(f32[4,64,256]{2,1,0:T(8,128)S(1)} %get-tuple-element.33), channel_id=1, source_target_pairs={{0,1},{1,0},{2,3},{3,2},{4,5},{5,4},{6,7},{7,6},{8,9},{9,8},{10,11... | collective-permute-start | bytes 786440 | tf_op jit(solution)/shard_map/ppermute | solution.py:221
  33.7 7.2 %shard_map.125.refs_5_ = f32[4,16,64,256]{3,2,1,0:T(8,128)S(1)} custom-call(s32[3]{0:T(128)S(1)} %pad_add_fusion.info, s32[3,1024]{1,0:T(4,128)S(1)} %bitcast.27, f32[4,1024]{1,0:T(4,128)S(1)} %bitcast.28), custom_call_target="tpu_custom_call" | custom-call | flops 6442450944 | bytes 4222988 | tf_op jit(solution)/shard_map/pallas_call | solution.py:22
  41.0 2.4 %shard_map.126 = (f32[16,64,256]{2,1,0:T(8,128)S(1)}, f32[4,64,256]{2,1,0:T(8,128)S(1)}, f32[4,64,256]{2,1,0:T(8,128)S(1)}) custom-call(s32[3]{0:T(128)S(1)} %pad_add_fusion.info, f32[16,64,256]{2,1,0:T(8,128)S(1)} %bitcast.20, f32[16,64,256]{2,1,0:T(8,128)S(1)} %bitcast.26, f32[4,64,256]{2,1,0:T(8,128)S(1)} %collective-permute-done.8.refs_2_, ...), custom_call_target="tpu_custom_call" | custom-call | flops 805306368 | bytes 9437196 | tf_op jit(solution)/shard_map/pallas_call | solution.py:22
  43.5 4.3 %collective-permute-start.10 = (f32[4,64,256]{2,1,0:T(8,128)S(1)}, f32[4,64,256]{2,1,0:T(8,128)S(1)}, u32[]{:S(2)}, u32[]{:S(2)}) collective-permute-start(f32[4,64,256]{2,1,0:T(8,128)S(1)} %get-tuple-element.44), channel_id=1, source_target_pairs={{0,1},{1,0},{2,3},{3,2},{4,5},{5,4},{6,7},{7,6},{8,9},{9,8},{10,11... | collective-permute-start | bytes 786440 | tf_op jit(solution)/shard_map/ppermute | solution.py:221
  48.5 2.4 %shard_map.123 = (f32[16,64,256]{2,1,0:T(8,128)S(1)}, f32[16,64,256]{2,1,0:T(8,128)S(1)}, f32[4,64,256]{2,1,0:T(8,128)S(1)}, f32[4,64,256]{2,1,0:T(8,128)S(1)}) custom-call(s32[3]{0:T(128)S(1)} %pad_add_fusion.info, s32[1,3]{1,0:T(1,128)S(1)} %copy-done.7, f32[1,4]{1,0:T(1,128)S(1)} %copy-done.9, f32[16,64,256]{2,1,0:T(8,128)S(1)} %get-tuple-element.32.refs_0_.refs_1_, ...), custom_call_target="tpu_custom_call" | custom-call | flops 805306368 | bytes 6291496 | tf_op jit(solution)/shard_map/pallas_call | solution.py:22
  51.0 4.3 %collective-permute-start.4 = (f32[4,64,256]{2,1,0:T(8,128)S(1)}, f32[4,64,256]{2,1,0:T(8,128)S(1)}, u32[]{:S(2)}, u32[]{:S(2)}) collective-permute-start(f32[4,64,256]{2,1,0:T(8,128)S(1)} %get-tuple-element.36), channel_id=1, source_target_pairs={{0,1},{1,0},{2,3},{3,2},{4,5},{5,4},{6,7},{7,6},{8,9},{9,8},{10,11... | collective-permute-start | bytes 786440 | tf_op jit(solution)/shard_map/ppermute | solution.py:221
  56.2 9.6 %collective-permute-done.10.refs_2_ = f32[4,64,256]{2,1,0:T(8,128)S(1)} collective-permute-done((f32[4,64,256]{2,1,0:T(8,128)S(1)}, f32[4,64,256]{2,1,0:T(8,128)S(1)}, u32[]{:S(2)}, u32[]{:S(2)}) %collective-permute-start.10) | collective-permute-done | bytes 262176 | tf_op jit(solution)/shard_map/ppermute | solution.py:221
  65.8 2.4 %shard_map.127 = (f32[16,64,256]{2,1,0:T(8,128)S(1)}, f32[4,64,256]{2,1,0:T(8,128)S(1)}, f32[4,64,256]{2,1,0:T(8,128)S(1)}) custom-call(s32[3]{0:T(128)S(1)} %pad_add_fusion.info, f32[16,64,256]{2,1,0:T(8,128)S(1)} %get-tuple-element.43.refs_0_.refs_1_, f32[16,64,256]{2,1,0:T(8,128)S(1)} %bitcast.21, f32[4,64,256]{2,1,0:T(8,128)S(1)} %collective-permute-done.10.refs_2_, ...), custom_call_target="tpu_custom_call" | custom-call | flops 805306368 | bytes 9437196 | tf_op jit(solution)/shard_map/pallas_call | solution.py:22
  68.3 2.5 %collective-permute-start.12 = (f32[4,64,256]{2,1,0:T(8,128)S(1)}, f32[4,64,256]{2,1,0:T(8,128)S(1)}, u32[]{:S(2)}, u32[]{:S(2)}) collective-permute-start(f32[4,64,256]{2,1,0:T(8,128)S(1)} %get-tuple-element.47), channel_id=1, source_target_pairs={{0,1},{1,0},{2,3},{3,2},{4,5},{5,4},{6,7},{7,6},{8,9},{9,8},{10,11... | collective-permute-start | bytes 786440 | tf_op jit(solution)/shard_map/ppermute | solution.py:221
  71.5 2.6 %collective-permute-done.4.refs_2_ = f32[4,64,256]{2,1,0:T(8,128)S(1)} collective-permute-done((f32[4,64,256]{2,1,0:T(8,128)S(1)}, f32[4,64,256]{2,1,0:T(8,128)S(1)}, u32[]{:S(2)}, u32[]{:S(2)}) %collective-permute-start.4) | collective-permute-done | bytes 262176 | tf_op jit(solution)/shard_map/ppermute | solution.py:221
  74.1 2.4 %shard_map.124 = (f32[16,64,256]{2,1,0:T(8,128)S(1)}, f32[16,64,256]{2,1,0:T(8,128)S(1)}, f32[4,64,256]{2,1,0:T(8,128)S(1)}, f32[4,64,256]{2,1,0:T(8,128)S(1)}) custom-call(s32[3]{0:T(128)S(1)} %pad_add_fusion.info, s32[1,3]{1,0:T(1,128)S(1)} %copy-done.7, f32[1,4]{1,0:T(1,128)S(1)} %copy-done.9, f32[16,64,256]{2,1,0:T(8,128)S(1)} %get-tuple-element.35.refs_0_.refs_1_, ...), custom_call_target="tpu_custom_call" | custom-call | flops 805306368 | bytes 6291496 | tf_op jit(solution)/shard_map/pallas_call | solution.py:22
  76.6 2.7 %collective-permute-start.6 = (f32[4,64,256]{2,1,0:T(8,128)S(1)}, f32[4,64,256]{2,1,0:T(8,128)S(1)}, u32[]{:S(2)}, u32[]{:S(2)}) collective-permute-start(f32[4,64,256]{2,1,0:T(8,128)S(1)} %get-tuple-element.39), channel_id=1, source_target_pairs={{0,1},{1,0},{2,3},{3,2},{4,5},{5,4},{6,7},{7,6},{8,9},{9,8},{10,11... | collective-permute-start | bytes 786440 | tf_op jit(solution)/shard_map/ppermute | solution.py:221
  79.9 8.4 %collective-permute-done.12.refs_2_ = f32[4,64,256]{2,1,0:T(8,128)S(1)} collective-permute-done((f32[4,64,256]{2,1,0:T(8,128)S(1)}, f32[4,64,256]{2,1,0:T(8,128)S(1)}, u32[]{:S(2)}, u32[]{:S(2)}) %collective-permute-start.12) | collective-permute-done | bytes 262176 | tf_op jit(solution)/shard_map/ppermute | solution.py:221
  88.3 2.6 %shard_map.128 = (f32[16,64,256]{2,1,0:T(8,128)S(1)}, f32[4,64,256]{2,1,0:T(8,128)S(1)}, f32[4,64,256]{2,1,0:T(8,128)S(1)}, f32[16,64,256]{2,1,0:T(8,128)S(1)}) custom-call(s32[3]{0:T(128)S(1)} %pad_add_fusion.info, f32[16,64,256]{2,1,0:T(8,128)S(1)} %get-tuple-element.46.refs_0_.refs_1_, f32[16,64,256]{2,1,0:T(8,128)S(1)} %get-tuple-element.43.refs_0_.refs_1_, ...), custom_call_target="tpu_custom_call" | custom-call | flops 805306368 | bytes 13631500 | tf_op jit(solution)/shard_map/pallas_call | solution.py:22
  92.3 3.5 %shard_map.129 = (f32[16,64,256]{2,1,0:T(8,128)}, f32[8,64,256]{2,1,0:T(8,128)S(1)}, f32[8,64,256]{2,1,0:T(8,128)S(1)}) custom-call(s32[3]{0:T(128)S(1)} %pad_add_fusion.info, s32[1,3]{1,0:T(1,128)S(1)} %copy-done.7, f32[1,4]{1,0:T(1,128)S(1)} %copy-done.9, f32[16,64,256]{2,1,0:T(8,128)S(1)} %get-tuple-element.38.refs_0_, ...), custom_call_target="tpu_custom_call" | custom-call | flops 805306368 | bytes 7864360 | tf_op jit(solution)/shard_map/pallas_call | solution.py:22
  95.8 1.9 %collective-permute-done.16 = f32[8,64,256]{2,1,0:T(8,128)S(1)} collective-permute-done((f32[8,64,256]{2,1,0:T(8,128)S(1)}, f32[8,64,256]{2,1,0:T(8,128)S(1)}, u32[]{:S(2)}, u32[]{:S(2)}) %collective-permute-start.16) | collective-permute-done | bytes 524320 | tf_op jit(solution)/shard_map/ppermute | solution.py:331
  99.4 12.4 %collective-permute-done.17 = f32[8,64,256]{2,1,0:T(8,128)S(1)} collective-permute-done((f32[8,64,256]{2,1,0:T(8,128)S(1)}, f32[8,64,256]{2,1,0:T(8,128)S(1)}, u32[]{:S(2)}, u32[]{:S(2)}) %collective-permute-start.17) | collective-permute-done | bytes 524320 | tf_op jit(solution)/shard_map/ppermute | solution.py:332
  112.0 2.5 %collective-permute-start.14 = (f32[4,64,256]{2,1,0:T(8,128)S(1)}, f32[4,64,256]{2,1,0:T(8,128)S(1)}, u32[]{:S(2)}, u32[]{:S(2)}) collective-permute-start(f32[4,64,256]{2,1,0:T(8,128)S(1)} %get-tuple-element.55), channel_id=1, source_target_pairs={{0,1},{1,0},{2,3},{3,2},{4,5},{5,4},{6,7},{7,6},{8,9},{9,8},{10,11... | collective-permute-start | bytes 786440 | tf_op jit(solution)/shard_map/ppermute | solution.py:221
  115.2 11.1 %collective-permute-done.14.refs_2_ = f32[4,64,256]{2,1,0:T(8,128)S(1)} collective-permute-done((f32[4,64,256]{2,1,0:T(8,128)S(1)}, f32[4,64,256]{2,1,0:T(8,128)S(1)}, u32[]{:S(2)}, u32[]{:S(2)}) %collective-permute-start.14) | collective-permute-done | bytes 262176 | tf_op jit(solution)/shard_map/ppermute | solution.py:221
  126.3 3.4 %shard_map.130 = f32[16,64,256]{2,1,0:T(8,128)} custom-call(s32[3]{0:T(128)S(1)} %pad_add_fusion.info, f32[16,64,256]{2,1,0:T(8,128)S(1)} %get-tuple-element.54.refs_0_, f32[16,64,256]{2,1,0:T(8,128)S(1)} %get-tuple-element.46.refs_0_.refs_1_, f32[4,64,256]{2,1,0:T(8,128)S(1)} %collective-permute-done.14.refs_2_, ...), custom_call_target="tpu_custom_call" | custom-call | flops 805306368 | bytes 8912908 | tf_op jit(solution)/shard_map/pallas_call | solution.py:22
  (54 shorter events, 19.1 us)
Async XLA Ops:
  0.6 33.1 %copy-start.11 = (f32[1,4,1024]{2,1,0:T(4,128)S(1)}, f32[1,4,1024]{2,1,0:T(4,128)}, u32[]{:S(2)}) copy-start(f32[1,4,1024]{2,1,0:T(4,128)} %param.19) | copy-start | bytes 49156
  1.7 12.7 %collective-permute-start.1 = (f32[4,64,256]{2,1,0:T(8,128)S(1)}, f32[4,64,256]{2,1,0:T(8,128)S(1)}, u32[]{:S(2)}, u32[]{:S(2)}) collective-permute-start(f32[4,64,256]{2,1,0:T(8,128)S(1)} %get-tuple-element.59), channel_id=1, source_target_pairs={{1,2},{3,4},{5,6},{2,1},{4,3},{6,5},{9,10},{11,12},{13,14},{10,9},... | collective-permute-start | bytes 786440 | tf_op jit(solution)/shard_map/ppermute | solution.py:222
  2.4 21.9 %collective-permute-start = (f32[4,64,256]{2,1,0:T(8,128)S(1)}, f32[4,64,256]{2,1,0:T(8,128)S(1)}, u32[]{:S(2)}, u32[]{:S(2)}) collective-permute-start(f32[4,64,256]{2,1,0:T(8,128)S(1)} %get-tuple-element.60), channel_id=1, source_target_pairs={{0,1},{1,0},{2,3},{3,2},{4,5},{5,4},{6,7},{7,6},{8,9},{9,8},{10,11... | collective-permute-start | bytes 786440 | tf_op jit(solution)/shard_map/ppermute | solution.py:221
  13.0 28.0 %collective-permute-start.8 = (f32[4,64,256]{2,1,0:T(8,128)S(1)}, f32[4,64,256]{2,1,0:T(8,128)S(1)}, u32[]{:S(2)}, u32[]{:S(2)}) collective-permute-start(f32[4,64,256]{2,1,0:T(8,128)S(1)} %get-tuple-element.41), channel_id=1, source_target_pairs={{0,1},{1,0},{2,3},{3,2},{4,5},{5,4},{6,7},{7,6},{8,9},{9,8},{10,11... | collective-permute-start | bytes 786440 | tf_op jit(solution)/shard_map/ppermute | solution.py:221
  13.1 27.9 %collective-permute-start.9 = (f32[4,64,256]{2,1,0:T(8,128)S(1)}, f32[4,64,256]{2,1,0:T(8,128)S(1)}, u32[]{:S(2)}, u32[]{:S(2)}) collective-permute-start(f32[4,64,256]{2,1,0:T(8,128)S(1)} %get-tuple-element.42), channel_id=1, source_target_pairs={{1,2},{3,4},{5,6},{2,1},{4,3},{6,5},{9,10},{11,12},{13,14},{10,9},... | collective-permute-start | bytes 786440 | tf_op jit(solution)/shard_map/ppermute | solution.py:222
  30.5 18.0 %collective-permute-start.2 = (f32[4,64,256]{2,1,0:T(8,128)S(1)}, f32[4,64,256]{2,1,0:T(8,128)S(1)}, u32[]{:S(2)}, u32[]{:S(2)}) collective-permute-start(f32[4,64,256]{2,1,0:T(8,128)S(1)} %get-tuple-element.33), channel_id=1, source_target_pairs={{0,1},{1,0},{2,3},{3,2},{4,5},{5,4},{6,7},{7,6},{8,9},{9,8},{10,11... | collective-permute-start | bytes 786440 | tf_op jit(solution)/shard_map/ppermute | solution.py:221
  33.0 15.5 %collective-permute-start.3 = (f32[4,64,256]{2,1,0:T(8,128)S(1)}, f32[4,64,256]{2,1,0:T(8,128)S(1)}, u32[]{:S(2)}, u32[]{:S(2)}) collective-permute-start(f32[4,64,256]{2,1,0:T(8,128)S(1)} %get-tuple-element.34), channel_id=1, source_target_pairs={{1,2},{3,4},{5,6},{2,1},{4,3},{6,5},{9,10},{11,12},{13,14},{10,9},... | collective-permute-start | bytes 786440 | tf_op jit(solution)/shard_map/ppermute | solution.py:222
  33.7 7.3 %copy-start.1 = (f32[1,16,64,256]{3,2,1,0:T(8,128)S(1)}, f32[1,16,64,256]{3,2,1,0:T(8,128)}, u32[]{:S(2)}) copy-start(f32[1,16,64,256]{3,2,1,0:T(8,128)} %param.13) | copy-start | bytes 3145732
  33.7 7.3 %copy-start.5 = (f32[1,16,64,256]{3,2,1,0:T(8,128)S(1)}, f32[1,16,64,256]{3,2,1,0:T(8,128)}, u32[]{:S(2)}) copy-start(f32[1,16,64,256]{3,2,1,0:T(8,128)} %param.12) | copy-start | bytes 3145732
  41.0 7.6 %copy-start.3 = (f32[1,16,64,256]{3,2,1,0:T(8,128)S(1)}, f32[1,16,64,256]{3,2,1,0:T(8,128)}, u32[]{:S(2)}) copy-start(f32[1,16,64,256]{3,2,1,0:T(8,128)} %param.11) | copy-start | bytes 3145732
  41.0 7.5 %copy-start.9 = (f32[1,4]{1,0:T(1,128)S(1)}, f32[1,4]{1,0:T(1,128)}, u32[]{:S(2)}) copy-start(f32[1,4]{1,0:T(1,128)} %wavelet.7) | copy-start | bytes 52
  43.5 22.3 %collective-permute-start.10 = (f32[4,64,256]{2,1,0:T(8,128)S(1)}, f32[4,64,256]{2,1,0:T(8,128)S(1)}, u32[]{:S(2)}, u32[]{:S(2)}) collective-permute-start(f32[4,64,256]{2,1,0:T(8,128)S(1)} %get-tuple-element.44), channel_id=1, source_target_pairs={{0,1},{1,0},{2,3},{3,2},{4,5},{5,4},{6,7},{7,6},{8,9},{9,8},{10,11... | collective-permute-start | bytes 786440 | tf_op jit(solution)/shard_map/ppermute | solution.py:221
  47.8 18.0 %collective-permute-start.11 = (f32[4,64,256]{2,1,0:T(8,128)S(1)}, f32[4,64,256]{2,1,0:T(8,128)S(1)}, u32[]{:S(2)}, u32[]{:S(2)}) collective-permute-start(f32[4,64,256]{2,1,0:T(8,128)S(1)} %get-tuple-element.45), channel_id=1, source_target_pairs={{1,2},{3,4},{5,6},{2,1},{4,3},{6,5},{9,10},{11,12},{13,14},{10,9},... | collective-permute-start | bytes 786440 | tf_op jit(solution)/shard_map/ppermute | solution.py:222
  51.0 23.1 %collective-permute-start.4 = (f32[4,64,256]{2,1,0:T(8,128)S(1)}, f32[4,64,256]{2,1,0:T(8,128)S(1)}, u32[]{:S(2)}, u32[]{:S(2)}) collective-permute-start(f32[4,64,256]{2,1,0:T(8,128)S(1)} %get-tuple-element.36), channel_id=1, source_target_pairs={{0,1},{1,0},{2,3},{3,2},{4,5},{5,4},{6,7},{7,6},{8,9},{9,8},{10,11... | collective-permute-start | bytes 786440 | tf_op jit(solution)/shard_map/ppermute | solution.py:221
  55.3 18.8 %collective-permute-start.5 = (f32[4,64,256]{2,1,0:T(8,128)S(1)}, f32[4,64,256]{2,1,0:T(8,128)S(1)}, u32[]{:S(2)}, u32[]{:S(2)}) collective-permute-start(f32[4,64,256]{2,1,0:T(8,128)S(1)} %get-tuple-element.37), channel_id=1, source_target_pairs={{1,2},{3,4},{5,6},{2,1},{4,3},{6,5},{9,10},{11,12},{13,14},{10,9},... | collective-permute-start | bytes 786440 | tf_op jit(solution)/shard_map/ppermute | solution.py:222
  68.3 20.0 %collective-permute-start.12 = (f32[4,64,256]{2,1,0:T(8,128)S(1)}, f32[4,64,256]{2,1,0:T(8,128)S(1)}, u32[]{:S(2)}, u32[]{:S(2)}) collective-permute-start(f32[4,64,256]{2,1,0:T(8,128)S(1)} %get-tuple-element.47), channel_id=1, source_target_pairs={{0,1},{1,0},{2,3},{3,2},{4,5},{5,4},{6,7},{7,6},{8,9},{9,8},{10,11... | collective-permute-start | bytes 786440 | tf_op jit(solution)/shard_map/ppermute | solution.py:221
  70.8 17.5 %collective-permute-start.13 = (f32[4,64,256]{2,1,0:T(8,128)S(1)}, f32[4,64,256]{2,1,0:T(8,128)S(1)}, u32[]{:S(2)}, u32[]{:S(2)}) collective-permute-start(f32[4,64,256]{2,1,0:T(8,128)S(1)} %get-tuple-element.48), channel_id=1, source_target_pairs={{1,2},{3,4},{5,6},{2,1},{4,3},{6,5},{9,10},{11,12},{13,14},{10,9},... | collective-permute-start | bytes 786440 | tf_op jit(solution)/shard_map/ppermute | solution.py:222
  76.6 15.7 %collective-permute-start.6 = (f32[4,64,256]{2,1,0:T(8,128)S(1)}, f32[4,64,256]{2,1,0:T(8,128)S(1)}, u32[]{:S(2)}, u32[]{:S(2)}) collective-permute-start(f32[4,64,256]{2,1,0:T(8,128)S(1)} %get-tuple-element.39), channel_id=1, source_target_pairs={{0,1},{1,0},{2,3},{3,2},{4,5},{5,4},{6,7},{7,6},{8,9},{9,8},{10,11... | collective-permute-start | bytes 786440 | tf_op jit(solution)/shard_map/ppermute | solution.py:221
  79.2 13.0 %collective-permute-start.7 = (f32[4,64,256]{2,1,0:T(8,128)S(1)}, f32[4,64,256]{2,1,0:T(8,128)S(1)}, u32[]{:S(2)}, u32[]{:S(2)}) collective-permute-start(f32[4,64,256]{2,1,0:T(8,128)S(1)} %get-tuple-element.40), channel_id=1, source_target_pairs={{1,2},{3,4},{5,6},{2,1},{4,3},{6,5},{9,10},{11,12},{13,14},{10,9},... | collective-permute-start | bytes 786440 | tf_op jit(solution)/shard_map/ppermute | solution.py:222
  95.8 1.9 %collective-permute-start.16 = (f32[8,64,256]{2,1,0:T(8,128)S(1)}, f32[8,64,256]{2,1,0:T(8,128)S(1)}, u32[]{:S(2)}, u32[]{:S(2)}) collective-permute-start(f32[8,64,256]{2,1,0:T(8,128)S(1)} %get-tuple-element.58), channel_id=1, source_target_pairs={{0,8},{8,0},{16,24},{24,16},{1,9},{9,1},{17,25},{25,17},{2,10},{10... | collective-permute-start | bytes 1572872 | tf_op jit(solution)/shard_map/ppermute | solution.py:331
  97.8 14.0 %collective-permute-start.17 = (f32[8,64,256]{2,1,0:T(8,128)S(1)}, f32[8,64,256]{2,1,0:T(8,128)S(1)}, u32[]{:S(2)}, u32[]{:S(2)}) collective-permute-start(f32[8,64,256]{2,1,0:T(8,128)S(1)} %add.21), channel_id=1, source_target_pairs={{0,16},{8,24},{16,0},{24,8},{1,17},{9,25},{17,1},{25,9},{2,18},{10... | collective-permute-start | bytes 1572872 | tf_op jit(solution)/shard_map/ppermute | solution.py:332
  111.9 17.8 %collective-permute-start.18 = (f32[8,64,256]{2,1,0:T(8,128)S(1)}, f32[8,64,256]{2,1,0:T(8,128)S(1)}, u32[]{:S(2)}, u32[]{:S(2)}) collective-permute-start(f32[8,64,256]{2,1,0:T(8,128)S(1)} %add.22.kept), channel_id=1, source_target_pairs={{0,8},{8,0},{16,24},{24,16},{1,9},{9,1},{17,25},{25,17},{2,10},{10... | collective-permute-start | bytes 1572872 | tf_op jit(solution)/shard_map/ppermute | solution.py:333
  112.0 14.3 %collective-permute-start.14 = (f32[4,64,256]{2,1,0:T(8,128)S(1)}, f32[4,64,256]{2,1,0:T(8,128)S(1)}, u32[]{:S(2)}, u32[]{:S(2)}) collective-permute-start(f32[4,64,256]{2,1,0:T(8,128)S(1)} %get-tuple-element.55), channel_id=1, source_target_pairs={{0,1},{1,0},{2,3},{3,2},{4,5},{5,4},{6,7},{7,6},{8,9},{9,8},{10,11... | collective-permute-start | bytes 786440 | tf_op jit(solution)/shard_map/ppermute | solution.py:221
  114.5 11.8 %collective-permute-start.15 = (f32[4,64,256]{2,1,0:T(8,128)S(1)}, f32[4,64,256]{2,1,0:T(8,128)S(1)}, u32[]{:S(2)}, u32[]{:S(2)}) collective-permute-start(f32[4,64,256]{2,1,0:T(8,128)S(1)} %get-tuple-element.56), channel_id=1, source_target_pairs={{1,2},{3,4},{5,6},{2,1},{4,3},{6,5},{9,10},{11,12},{13,14},{10,9},... | collective-permute-start | bytes 786440 | tf_op jit(solution)/shard_map/ppermute | solution.py:222
  (7 other events, 6.9 us)

commit v2 on v1

v2 whole, which is shorter than its diff:
```python
import functools

import jax
import jax.numpy as jnp
from jax import lax
from jax.experimental import pallas as pl
from jax.experimental.pallas import tpu as pltpu
from jax.sharding import PartitionSpec as P

centre_coef = -205.0 / 72.0
side_coefs = (8.0 / 5.0, -1.0 / 5.0, 8.0 / 315.0, -1.0 / 560.0)
unit = 5040.0
side_units = (8064.0, -1008.0, 128.0, -9.0)
halo = 4

vmem = pl.BlockSpec(memory_space=pltpu.VMEM)
smem = pl.BlockSpec(memory_space=pltpu.SMEM)
hbm = pl.BlockSpec(memory_space=pltpu.HBM)


def call(kernel, args, in_specs, outs, scratch=(), aliases={}):
    return pl.pallas_call(
        kernel,
        out_shape=[shape for shape, _ in outs],
        in_specs=in_specs,
        out_specs=[spec for _, spec in outs],
        scratch_shapes=list(scratch),
        input_output_aliases=aliases,
        compiler_params=pltpu.CompilerParams(vmem_limit_bytes=24 * 1024 * 1024),
        cost_estimate=pl.CostEstimate(flops=1024, bytes_accessed=1024, transcendentals=0),
    )(*args)


def f32(*shape):
    return jax.ShapeDtypeStruct(shape, jnp.float32)


def band(size, block):
    row = lax.broadcasted_iota(jnp.int32, (size, size), 0)
    col = lax.broadcasted_iota(jnp.int32, (size, size), 1)
    apart = jnp.abs(row - col)
    value = jnp.zeros((size, size), jnp.float32)
    for k in range(1, 5):
        value = jnp.where(apart == k, side_units[k - 1], value)
    if block != size:
        value = jnp.where(lax.div(row, block) == lax.div(col, block), value, 0.0)
    return value.astype(jnp.bfloat16)


def pieces(value):
    high = value.astype(jnp.bfloat16)
    rest = value - high.astype(jnp.float32)
    middle = rest.astype(jnp.bfloat16)
    low = (rest - middle.astype(jnp.float32)).astype(jnp.bfloat16)
    return high, middle, low


def dot(a, b):
    return lax.dot_general(a, b, (((1,), (0,)), ((), ())), preferred_element_type=jnp.float32)


def laplacian(field, at, along_y, along_z):
    _, nz, ny = field.shape
    centre = field[pl.ds(at, halo)]
    high, middle, low = pieces(centre.reshape(halo * nz, ny))
    across = dot(low, along_y) + dot(along_z, low)
    across = across + (dot(middle, along_y) + dot(along_z, middle))
    across = across + (dot(high, along_y) + dot(along_z, high))
    result = 3.0 * centre_coef * centre + across.reshape(halo, nz, ny) * (1.0 / unit)
    for k in range(1, 5):
        result = result + side_coefs[k - 1] * (
            field[pl.ds(at + k, halo)] + field[pl.ds(at - k, halo)]
        )
    return result


def bands(field):
    _, nz, ny = field.shape
    return band(ny, ny), band(halo * nz, nz)


def place(ext, info, near, far):
    planes = ext.shape[0] - 2 * halo
    odd = info[0]
    spot = jnp.where(odd == 1, 0, planes + halo)
    ext[pl.ds(spot, halo)] = near[...]
    ext[pl.ds(planes + halo - spot, halo)] = far[...]


def edge_spots(info, planes):
    odd = info[0]
    near = jnp.where(odd == 1, 0, planes - halo)
    return near, planes - halo - near


def add_source(field, first, info, source, value):
    count, _, ny = field.shape
    x = source[0, 0] - info[1] - first
    z = source[0, 1]
    y = source[0, 2]

    @pl.when((x >= 0) & (x < count))
    def _():
        base = pl.multiple_of(lax.div(z, 8) * 8, 8)
        rows = lax.broadcasted_iota(jnp.int32, (8, ny), 0)
        cols = lax.broadcasted_iota(jnp.int32, (8, ny), 1)
        hit = (rows == z - base) & (cols == y)
        tile = field[x, pl.ds(base, 8), :]
        field[x, pl.ds(base, 8), :] = tile + jnp.where(hit, value, 0.0)


def prepare_kernel(
    info, table, labels, near_field, *refs
):
    sources, refs = refs[:3], refs[3:]
    rate, near_edge, far_edge, field, *targets = refs[:7]
    label, sems = refs[7:]
    planes = labels.shape[0]
    first = pltpu.make_async_copy(labels, label, sems.at[0])
    second = pltpu.make_async_copy(near_field, field, sems.at[1])
    first.start()
    second.start()
    others = []
    for n in range(3):
        others.append(pltpu.make_async_copy(sources[n], targets[n], sems.at[2 + n]))
        others[n].start()
    first.wait()
    for part in range(planes // halo):
        here = pl.ds(part * halo, halo)
        known = label[here]
        value = jnp.zeros(known.shape, jnp.float32)
        for region in range(table.shape[0]):
            value = jnp.where(known == region, table[region], value)
        rate[here] = value
    second.wait()
    near, far = edge_spots(info, planes)
    near_edge[...] = rate[pl.ds(near, halo)] * field[pl.ds(near, halo)]
    far_edge[...] = rate[pl.ds(far, halo)] * field[pl.ds(far, halo)]
    for copy in others:
        copy.wait()


def receivers_kernel(info, index, values, injected):
    steps, planes, nz, ny = injected.shape
    count = index.shape[1]
    local = index[0:1, :] - info[1]
    cell = jnp.where((local >= 0) & (local < planes), local * nz + index[1:2, :], -1)
    at_y = lax.broadcasted_iota(jnp.int32, (ny, count), 0) == index[2:3, :]
    parts = []
    for step in range(steps):
        for piece in pieces(values[step : step + 1, :]):
            spread = jnp.where(at_y, piece.astype(jnp.float32), 0.0)
            parts.append(spread.astype(jnp.bfloat16))
    group = halo
    rows = group * nz
    for part in range(planes // group):
        at_cell = lax.broadcasted_iota(jnp.int32, (rows, count), 0) + part * rows == cell
        picked = jnp.where(at_cell, 1.0, 0.0).astype(jnp.bfloat16)
        for step in range(steps):
            total = None
            for piece in reversed(parts[3 * step : 3 * step + 3]):
                term = lax.dot_general(
                    picked, piece, (((1,), (1,)), ((), ())), preferred_element_type=jnp.float32
                )
                total = term if total is None else total + term
            injected[step, pl.ds(part * group, group)] = total.reshape(group, nz, ny)


def forward_kernel(step, info, source, wavelet, *refs):
    current, previous, near, far, rate, upcoming, lap, near_edge, far_edge, ext = refs
    planes = current.shape[0]
    place(ext, info, near, far)
    ext[pl.ds(halo, planes)] = current[...]
    along_y, along_z = bands(current)
    for first in range(0, planes, halo):
        here = pl.ds(first, halo)
        value = laplacian(ext, first + halo, along_y, along_z)
        lap[here] = value
        upcoming[here] = 2.0 * current[here] - previous[here] + rate[here] * value
    add_source(upcoming, 0, info, source, wavelet[0, step])
    near_at, far_at = edge_spots(info, planes)
    near_edge[...] = upcoming[pl.ds(near_at, halo)]
    far_edge[...] = upcoming[pl.ds(far_at, halo)]


def adjoint_kernel(step, info, *refs):
    current, later, near, far, rate, injected, earlier, near_edge, far_edge, ext = refs
    planes = current.shape[0]
    place(ext, info, near, far)
    ext[pl.ds(halo, planes)] = rate[...] * current[...]
    along_y, along_z = bands(current)
    for first in range(0, planes, halo):
        here = pl.ds(first, halo)
        value = laplacian(ext, first + halo, along_y, along_z)
        earlier[here] = 2.0 * current[here] - later[here] + value + injected[step, here]
    near_at, far_at = edge_spots(info, planes)
    near_edge[...] = rate[pl.ds(near_at, halo)] * earlier[pl.ds(near_at, halo)]
    far_edge[...] = rate[pl.ds(far_at, halo)] * earlier[pl.ds(far_at, halo)]


def turn_kernel(forward_step, step, info, source, wavelet, *refs):
    (current, later, near, far, rate, injected, lap1, lap2, lap3, wave, before, a5,
     earlier, near_edge, far_edge, rest, keep, send, final, ext, stage, grad, sem) = refs
    planes = current.shape[0]
    place(ext, info, near, far)
    ext[pl.ds(halo, planes)] = rate[...] * current[...]
    along_y, along_z = bands(current)
    for first in range(0, planes, halo):
        here = pl.ds(first, halo)
        value = laplacian(ext, first + halo, along_y, along_z)
        value = 2.0 * current[here] - later[here] + value + injected[step, here]
        earlier[here] = value
        partial = later[here] * lap3[here] + current[here] * lap2[here] + value * lap1[here]
        if first == 0:
            rest[0] = partial
        elif first == planes - halo:
            rest[1] = partial
        else:
            value = laplacian(wave, first, along_y, along_z)
            inner = pl.ds(first - halo, halo)
            stage[inner] = 2.0 * wave[here] - before[here] + rate[here] * value
            grad[inner] = partial + a5[here] * value
    add_source(stage, halo, info, source, wavelet[0, forward_step])
    copy = pltpu.make_async_copy(stage, final.at[pl.ds(halo, planes - 2 * halo)], sem)
    copy.start()
    near_at, far_at = edge_spots(info, planes)
    near_edge[...] = rate[pl.ds(near_at, halo)] * earlier[pl.ds(near_at, halo)]
    far_edge[...] = rate[pl.ds(far_at, halo)] * earlier[pl.ds(far_at, halo)]
    half = keep.shape[0]
    mine = info[2] * half
    keep[...] = grad[pl.ds(mine, half)]
    send[...] = grad[pl.ds(half - mine, half)]
    copy.wait()


def forward_outer_kernel(step, info, source, wavelet, *refs):
    (current, previous, near, far, rate, rest, a5, _,
     keep, send, final, ext, stage, grad, sems) = refs
    planes = current.shape[0]
    place(ext, info, near, far)
    ext[pl.ds(halo, planes)] = current[...]
    along_y, along_z = bands(current)
    copies = []
    for side, first in enumerate((0, planes - halo)):
        here = pl.ds(first, halo)
        value = laplacian(ext, first + halo, along_y, along_z)
        stage[side] = 2.0 * current[here] - previous[here] + rate[here] * value
        grad[side] = rest[side] + a5[here] * value
        add_source(stage.at[side], first, info, source, wavelet[0, step])
        copies.append(pltpu.make_async_copy(stage.at[side], final.at[here], sems.at[side]))
        copies[side].start()
    keep[...] = grad[info[2]]
    send[...] = grad[1 - info[2]]
    for copy in copies:
        copy.wait()


def adjoint_inner_kernel(step, info, current, later, rate, injected, first_adjoint, ext, stage, sem):
    planes = current.shape[0]
    ext[...] = rate[...] * current[...]
    along_y, along_z = bands(current)
    for first in range(halo, planes - halo, halo):
        here = pl.ds(first, halo)
        value = laplacian(ext, first, along_y, along_z)
        stage[pl.ds(first - halo, halo)] = (
            2.0 * current[here] - later[here] + value + injected[step, here]
        )
    copy = pltpu.make_async_copy(stage, first_adjoint.at[pl.ds(halo, planes - 2 * halo)], sem)
    copy.start()
    copy.wait()


def adjoint_outer_kernel(step, info, *refs):
    current, later, near, far, rate, injected, _, first_adjoint, ext, stage, sems = refs
    planes = current.shape[0]
    place(ext, info, near, far)
    ext[pl.ds(halo, planes)] = rate[...] * current[...]
    along_y, along_z = bands(current)
    copies = []
    for side, first in enumerate((0, planes - halo)):
        here = pl.ds(first, halo)
        value = laplacian(ext, first + halo, along_y, along_z)
        stage[side] = 2.0 * current[here] - later[here] + value + injected[step, here]
        copies.append(pltpu.make_async_copy(stage.at[side], first_adjoint.at[here], sems.at[side]))
        copies[side].start()
    for copy in copies:
        copy.wait()


def assemble_kernel(info, inner_kept, inner_got, kept, got, total, sems):
    planes = total.shape[0]
    half = inner_kept.shape[0]
    mine = info[2] * half
    side = info[2] * (planes - halo)
    spots = (
        (inner_kept, halo + mine, half),
        (inner_got, halo + half - mine, half),
        (kept, side, halo),
        (got, planes - halo - side, halo),
    )
    copies = []
    for n, (piece, at, count) in enumerate(spots):
        copies.append(pltpu.make_async_copy(piece, total.at[pl.ds(at, count)], sems.at[n]))
        copies[n].start()
    for copy in copies:
        copy.wait()


def swap(near_edge, far_edge):
    count = lax.axis_size("dom")
    near_pairs = [(i, i ^ 1) for i in range(count) if i ^ 1 < count]
    far_pairs = [(i, i + 1) for i in range(1, count - 1, 2)]
    far_pairs = far_pairs + [(b, a) for a, b in far_pairs]
    return (
        lax.ppermute(near_edge, "dom", near_pairs),
        lax.ppermute(far_edge, "dom", far_pairs),
    )


def summed(keep, send):
    shots = lax.axis_size("shot")
    pairs = [(i, i ^ 1) for i in range(shots)]
    across = [(i, i ^ 2) for i in range(shots)]
    kept = keep + lax.ppermute(send, "shot", pairs)
    kept = kept + lax.ppermute(kept, "shot", across)
    return kept, lax.ppermute(kept, "shot", pairs)


def per_device(
    wave_before,
    wave_current,
    adjoint_far,
    adjoint_near,
    labels,
    table,
    source_index,
    wavelet,
    receiver_index,
    residual,
):
    planes, nz, ny = wave_current.shape[1:]
    steps = wavelet.shape[1]
    place_x = lax.axis_index("dom")
    odd = place_x % 2
    info = jnp.stack([odd, place_x * planes, lax.axis_index("shot") % 2]).astype(jnp.int32)
    u0, u1 = wave_before[0], wave_current[0]
    a6, a5 = adjoint_far[0], adjoint_near[0]
    whole = f32(planes, nz, ny)
    block = (whole, vmem)
    edge = (f32(halo, nz, ny), vmem)
    inner = planes - 2 * halo
    quarter = (f32(inner // 2, nz, ny), vmem)
    ext = pltpu.VMEM((planes + 2 * halo, nz, ny), jnp.float32)
    within = pltpu.VMEM((inner, nz, ny), jnp.float32)
    outer = pltpu.VMEM((2, halo, nz, ny), jnp.float32)

    near_at = jnp.where(odd == 1, 0, planes - halo)
    near_edge = lax.dynamic_slice_in_dim(u1, near_at, halo, axis=0)
    far_edge = lax.dynamic_slice_in_dim(u1, planes - halo - near_at, halo, axis=0)
    u_halo = swap(near_edge, far_edge)

    rate, near_edge, far_edge, a5, u1, u0, a6 = call(
        prepare_kernel,
        (info, table, labels, a5, u1, u0, a6),
        [smem, smem] + [hbm] * 5,
        [block, edge, edge] + [block] * 4,
        [pltpu.VMEM((planes, nz, ny), jnp.int32), pltpu.SemaphoreType.DMA((5,))],
    )
    a_halo = swap(near_edge, far_edge)

    (injected,) = call(
        receivers_kernel,
        (info, receiver_index[0].T, residual[0]),
        [smem, vmem, vmem],
        [(f32(steps, planes, nz, ny), vmem)],
    )

    laps = []
    previous, current = u0, u1
    later, adjoint = a6, a5
    for n in range(steps - 1):
        upcoming, lap, near_edge, far_edge = call(
            functools.partial(forward_kernel, n),
            (info, source_index, wavelet, current, previous, *u_halo, rate),
            [smem] * 3 + [vmem] * 5,
            [block, block, edge, edge],
            [ext],
        )
        laps.append(lap)
        u_halo = swap(near_edge, far_edge)
        previous, current = current, upcoming
        step = steps - 1 - n
        if n < steps - 2:
            earlier, near_edge, far_edge = call(
                functools.partial(adjoint_kernel, step),
                (info, adjoint, later, *a_halo, rate, injected),
                [smem] + [vmem] * 6,
                [block, edge, edge],
                [ext],
            )
        else:
            earlier, near_edge, far_edge, rest, keep, send, final = call(
                functools.partial(turn_kernel, steps - 1, step),
                (info, source_index, wavelet, adjoint, later, *a_halo, rate, injected, *laps,
                 current, previous, a5),
                [smem] * 3 + [vmem] * 12,
                [block, edge, edge, (f32(2, halo, nz, ny), vmem), quarter, quarter, (whole, hbm)],
                [ext, within, within, pltpu.SemaphoreType.DMA],
            )
        a_halo = swap(near_edge, far_edge)
        later, adjoint = adjoint, earlier

    inner_kept, inner_got = summed(keep, send)
    keep, send, final = call(
        functools.partial(forward_outer_kernel, steps - 1),
        (info, source_index, wavelet, current, previous, *u_halo, rate, rest, a5, final),
        [smem] * 3 + [vmem] * 7 + [hbm],
        [edge, edge, (whole, hbm)],
        [ext, outer, outer, pltpu.SemaphoreType.DMA((2,))],
        {10: 2},
    )
    kept, got = summed(keep, send)
    (first_adjoint,) = call(
        functools.partial(adjoint_inner_kernel, 0),
        (info, adjoint, later, rate, injected),
        [smem] + [vmem] * 4,
        [(whole, hbm)],
        [pltpu.VMEM((planes, nz, ny), jnp.float32), within, pltpu.SemaphoreType.DMA],
    )
    (first_adjoint,) = call(
        functools.partial(adjoint_outer_kernel, 0),
        (info, adjoint, later, *a_halo, rate, injected, first_adjoint),
        [smem] + [vmem] * 6 + [hbm],
        [(whole, hbm)],
        [ext, outer, pltpu.SemaphoreType.DMA((2,))],
        {7: 0},
    )
    (total,) = call(
        assemble_kernel,
        (info, inner_kept, inner_got, kept, got),
        [smem] + [vmem] * 4,
        [(whole, hbm)],
        [pltpu.SemaphoreType.DMA((4,))],
    )
    return (final[None], first_adjoint[None], total)


def solution(mesh):
    placed = (
        P("shot", "dom", None, None),
        P("shot", "dom", None, None),
        P("shot", "dom", None, None),
        P("shot", "dom", None, None),
        P("dom", None, None),
        P(),
        P("shot", None),
        P("shot", None),
        P("shot", None, None),
        P("shot", None, None),
    )
    return jax.shard_map(
        per_device,
        mesh=mesh,
        in_specs=placed,
        out_specs=(
            P("shot", "dom", None, None),
            P("shot", "dom", None, None),
            P("dom", None, None),
        ),
        check_vma=False,
    )
```

time: 132 us -> 111 us (0.84)
  waiting for transfers between devices: 57.4 us -> 33 us
  starting transfers between devices: 32.1 us -> 34.2 us
  Pallas kernels: 32.1 us -> 33.9 us
    ppermute x8, waiting for transfers between devices: 43 us -> 24.9 us  [swap(): lax.ppermute(near_edge, 'dom', near_pairs)]
    ppermute x3 -> x6, waiting for transfers between devices: 14.4 us -> 8.04 us  [the longest x2 8.03 us: summed(): kept = kept + lax.ppermute(kept, 'shot', across)]
    pallas_call x11 -> x12, Pallas kernels: 32.1 us -> 33.9 us  [call(): pl.pallas_call(kernel, out_shape=[shape for shape, _ in outs], in_specs=i...]
    ppermute x3 -> x6, starting transfers between devices: 1.66 us -> 3.34 us  [the longest x2 2.97 us: summed(): kept = kept + lax.ppermute(kept, 'shot', across)]
    unnamed x25 -> x21, local copies, waits for them, and re-layouts: 7.61 us -> 6.8 us
  transfers between devices with their start and end apart: 19 -> 22, of which waited for: 8 -> 8; matrix products, arithmetic and copies ran while one was open for 1% -> 0% of each run, Pallas kernels for 21% -> 29%
where the time goes in v2:
time: 111 us; the launch traced here: 110 us
  starting transfers between devices  34.2 us (31%)
  Pallas kernels  33.9 us (31%)
  waiting for transfers between devices  33 us (30%)
  local copies, waits for them, and re-layouts  7.88 us (7%)
    pallas_call x12, Pallas kernels, call(): pl.pallas_call(kernel, out_shape=[shape for shape, _ in outs], in_specs=i...  33.9 us
    ppermute x8, starting transfers between devices, swap(): lax.ppermute(near_edge, 'dom', near_pairs)  25.4 us
    ppermute x8, waiting for transfers between devices, swap(): lax.ppermute(near_edge, 'dom', near_pairs)  24.9 us
    ppermute x2, waiting for transfers between devices, summed(): kept = kept + lax.ppermute(kept, 'shot', across)  8.03 us
    unnamed x21, local copies, waits for them, and re-layouts  6.8 us
    ppermute x8, starting transfers between devices, swap(): lax.ppermute(far_edge, 'dom', far_pairs)  5.51 us
    ppermute x2, starting transfers between devices, summed(): kept = kept + lax.ppermute(kept, 'shot', across)  2.97 us
  transfers between devices with their start and end apart: 22, of which 8 were waited for; matrix products, arithmetic and copies ran while one was open for 0% of the time, Pallas kernels for 29%

profile of v2, /device:TPU:0, one launch (start us, length us, event | category | flops | bytes accessed | tf_op | source)
XLA Modules:
  0.0 110.3 jit_solution(15999406770886656664)
XLA Ops:
  2.4 5.8 %collective-permute-start = (f32[4,64,256]{2,1,0:T(8,128)S(1)}, f32[4,64,256]{2,1,0:T(8,128)S(1)}, u32[]{:S(2)}, u32[]{:S(2)}) collective-permute-start(f32[4,64,256]{2,1,0:T(8,128)S(1)} %get-tuple-element.74), channel_id=1, source_target_pairs={{0,1},{1,0},{2,3},{3,2},{4,5},{5,4},{6,7},{7,6},{8,9},{9,8},{10,11... | collective-permute-start | bytes 786440 | tf_op jit(solution)/shard_map/ppermute | solution.py:315
  15.1 1.6 %shard_map.121 = (f32[16,64,256]{2,1,0:T(8,128)S(1)}, f32[4,64,256]{2,1,0:T(8,128)S(1)}, f32[4,64,256]{2,1,0:T(8,128)S(1)}, f32[16,64,256]{2,1,0:T(8,128)S(1)}, ...) custom-call(s32[3]{0:T(128)S(1)} %pad_add_fusion.info, f32[8]{0:T(128)S(1)} %copy-done.8, ...), custom_call_target="tpu_custom_call" | custom-call | flops 1024 | bytes 1024 | tf_op jit(solution)/shard_map/pallas_call | solution.py:22
  18.8 2.3 %shard_map.122 = (f32[16,64,256]{2,1,0:T(8,128)S(1)}, f32[16,64,256]{2,1,0:T(8,128)S(1)}, f32[4,64,256]{2,1,0:T(8,128)S(1)}, f32[4,64,256]{2,1,0:T(8,128)S(1)}) custom-call(s32[3]{0:T(128)S(1)} %pad_add_fusion.info, s32[1,3]{1,0:T(1,128)S(1)} %copy-done.6, f32[1,4]{1,0:T(1,128)S(1)} %copy-done.7, f32[16,64,256]{2,1,0:T(8,128)S(1)} %get-tuple-element.38.refs_0_.refs_1_, ...), custom_call_target="tpu_custom_call" | custom-call | flops 1024 | bytes 1024 | tf_op jit(solution)/shard_map/pallas_call | solution.py:22
  21.1 3.4 %collective-permute-start.2 = (f32[4,64,256]{2,1,0:T(8,128)S(1)}, f32[4,64,256]{2,1,0:T(8,128)S(1)}, u32[]{:S(2)}, u32[]{:S(2)}) collective-permute-start(f32[4,64,256]{2,1,0:T(8,128)S(1)} %get-tuple-element.42), channel_id=1, source_target_pairs={{0,1},{1,0},{2,3},{3,2},{4,5},{5,4},{6,7},{7,6},{8,9},{9,8},{10,11... | collective-permute-start | bytes 786440 | tf_op jit(solution)/shard_map/ppermute | solution.py:315
  25.2 7.2 %shard_map.125.refs_5_.injected = f32[4,16,64,256]{3,2,1,0:T(8,128)S(1)} custom-call(s32[3]{0:T(128)S(1)} %pad_add_fusion.info, s32[3,1024]{1,0:T(4,128)S(1)} %bitcast.23, f32[4,1024]{1,0:T(4,128)S(1)} %bitcast.24), custom_call_target="tpu_custom_call" | custom-call | flops 1024 | bytes 1024 | tf_op jit(solution)/shard_map/pallas_call | solution.py:22
  32.4 3.2 %collective-permute-done.8.refs_2_ = f32[4,64,256]{2,1,0:T(8,128)S(1)} collective-permute-done((f32[4,64,256]{2,1,0:T(8,128)S(1)}, f32[4,64,256]{2,1,0:T(8,128)S(1)}, u32[]{:S(2)}, u32[]{:S(2)}) %collective-permute-start.8) | collective-permute-done | bytes 262176 | tf_op jit(solution)/shard_map/ppermute | solution.py:315
  35.6 2.4 %shard_map.126 = (f32[16,64,256]{2,1,0:T(8,128)S(1)}, f32[4,64,256]{2,1,0:T(8,128)S(1)}, f32[4,64,256]{2,1,0:T(8,128)S(1)}) custom-call(s32[3]{0:T(128)S(1)} %pad_add_fusion.info, f32[16,64,256]{2,1,0:T(8,128)S(1)} %get-tuple-element.50.refs_0_.refs_1_.refs_11_.refs_6_, f32[16,64,256]{2,1,0:T(8,128)S(1)} %get-tuple-element.51.refs_1_, ...), custom_call_target="tpu_custom_call" | custom-call | flops 1024 | bytes 1024 | tf_op jit(solution)/shard_map/pallas_call | solution.py:22
  38.0 2.5 %collective-permute-start.10 = (f32[4,64,256]{2,1,0:T(8,128)S(1)}, f32[4,64,256]{2,1,0:T(8,128)S(1)}, u32[]{:S(2)}, u32[]{:S(2)}) collective-permute-start(f32[4,64,256]{2,1,0:T(8,128)S(1)} %get-tuple-element.55), channel_id=1, source_target_pairs={{0,1},{1,0},{2,3},{3,2},{4,5},{5,4},{6,7},{7,6},{8,9},{9,8},{10,11... | collective-permute-start | bytes 786440 | tf_op jit(solution)/shard_map/ppermute | solution.py:315
  41.3 2.3 %shard_map.123 = (f32[16,64,256]{2,1,0:T(8,128)S(1)}, f32[16,64,256]{2,1,0:T(8,128)S(1)}, f32[4,64,256]{2,1,0:T(8,128)S(1)}, f32[4,64,256]{2,1,0:T(8,128)S(1)}) custom-call(s32[3]{0:T(128)S(1)} %pad_add_fusion.info, s32[1,3]{1,0:T(1,128)S(1)} %copy-done.6, f32[1,4]{1,0:T(1,128)S(1)} %copy-done.7, f32[16,64,256]{2,1,0:T(8,128)S(1)} %get-tuple-element.41.refs_0_.refs_1_, ...), custom_call_target="tpu_custom_call" | custom-call | flops 1024 | bytes 1024 | tf_op jit(solution)/shard_map/pallas_call | solution.py:22
  43.5 4.3 %collective-permute-start.4 = (f32[4,64,256]{2,1,0:T(8,128)S(1)}, f32[4,64,256]{2,1,0:T(8,128)S(1)}, u32[]{:S(2)}, u32[]{:S(2)}) collective-permute-start(f32[4,64,256]{2,1,0:T(8,128)S(1)} %get-tuple-element.45), channel_id=1, source_target_pairs={{0,1},{1,0},{2,3},{3,2},{4,5},{5,4},{6,7},{7,6},{8,9},{9,8},{10,11... | collective-permute-start | bytes 786440 | tf_op jit(solution)/shard_map/ppermute | solution.py:315
  48.7 9.9 %collective-permute-done.10.refs_2_ = f32[4,64,256]{2,1,0:T(8,128)S(1)} collective-permute-done((f32[4,64,256]{2,1,0:T(8,128)S(1)}, f32[4,64,256]{2,1,0:T(8,128)S(1)}, u32[]{:S(2)}, u32[]{:S(2)}) %collective-permute-start.10) | collective-permute-done | bytes 262176 | tf_op jit(solution)/shard_map/ppermute | solution.py:315
  58.6 2.3 %shard_map.127 = (f32[16,64,256]{2,1,0:T(8,128)S(1)}, f32[4,64,256]{2,1,0:T(8,128)S(1)}, f32[4,64,256]{2,1,0:T(8,128)S(1)}) custom-call(s32[3]{0:T(128)S(1)} %pad_add_fusion.info, f32[16,64,256]{2,1,0:T(8,128)S(1)} %get-tuple-element.54.refs_0_.refs_1_, f32[16,64,256]{2,1,0:T(8,128)S(1)} %get-tuple-element.50.refs_0_.refs_1_.refs_11_.refs_6_, ...), custom_call_target="tpu_custom_call" | custom-call | flops 1024 | bytes 1024 | tf_op jit(solution)/shard_map/pallas_call | solution.py:22
  60.9 2.5 %collective-permute-start.12 = (f32[4,64,256]{2,1,0:T(8,128)S(1)}, f32[4,64,256]{2,1,0:T(8,128)S(1)}, u32[]{:S(2)}, u32[]{:S(2)}) collective-permute-start(f32[4,64,256]{2,1,0:T(8,128)S(1)} %get-tuple-element.58), channel_id=1, source_target_pairs={{0,1},{1,0},{2,3},{3,2},{4,5},{5,4},{6,7},{7,6},{8,9},{9,8},{10,11... | collective-permute-start | bytes 786440 | tf_op jit(solution)/shard_map/ppermute | solution.py:315
  64.2 2.3 %shard_map.124 = (f32[16,64,256]{2,1,0:T(8,128)S(1)}, f32[16,64,256]{2,1,0:T(8,128)S(1)}, f32[4,64,256]{2,1,0:T(8,128)S(1)}, f32[4,64,256]{2,1,0:T(8,128)S(1)}) custom-call(s32[3]{0:T(128)S(1)} %pad_add_fusion.info, s32[1,3]{1,0:T(1,128)S(1)} %copy-done.6, f32[1,4]{1,0:T(1,128)S(1)} %copy-done.7, ...), custom_call_target="tpu_custom_call" | custom-call | flops 1024 | bytes 1024 | tf_op jit(solution)/shard_map/pallas_call | solution.py:22
  66.5 4.2 %collective-permute-start.6 = (f32[4,64,256]{2,1,0:T(8,128)S(1)}, f32[4,64,256]{2,1,0:T(8,128)S(1)}, u32[]{:S(2)}, u32[]{:S(2)}) collective-permute-start(f32[4,64,256]{2,1,0:T(8,128)S(1)} %get-tuple-element.48), channel_id=1, source_target_pairs={{0,1},{1,0},{2,3},{3,2},{4,5},{5,4},{6,7},{7,6},{8,9},{9,8},{10,11... | collective-permute-start | bytes 786440 | tf_op jit(solution)/shard_map/ppermute | solution.py:315
  71.4 10.0 %collective-permute-done.12.refs_2_ = f32[4,64,256]{2,1,0:T(8,128)S(1)} collective-permute-done((f32[4,64,256]{2,1,0:T(8,128)S(1)}, f32[4,64,256]{2,1,0:T(8,128)S(1)}, u32[]{:S(2)}, u32[]{:S(2)}) %collective-permute-start.12) | collective-permute-done | bytes 262176 | tf_op jit(solution)/shard_map/ppermute | solution.py:315
  81.4 4.2 %shard_map.128 = (f32[16,64,256]{2,1,0:T(8,128)S(1)}, f32[4,64,256]{2,1,0:T(8,128)S(1)}, f32[4,64,256]{2,1,0:T(8,128)S(1)}, f32[2,4,64,256]{3,2,1,0:T(8,128)S(1)...) custom-call(s32[3]{0:T(128)S(1)} %pad_add_fusion.info, s32[1,3]{1,0:T(1,128)S(1)} %copy-done.6, ...), custom_call_target="tpu_custom_call" | custom-call | flops 1024 | bytes 1024 | tf_op jit(solution)/shard_map/pallas_call | solution.py:22
  86.1 2.9 %shard_map.129 = (f32[4,64,256]{2,1,0:T(8,128)S(1)}, f32[4,64,256]{2,1,0:T(8,128)S(1)}, f32[16,64,256]{2,1,0:T(8,128)}) custom-call(s32[3]{0:T(128)S(1)} %pad_add_fusion.info, s32[1,3]{1,0:T(1,128)S(1)} %copy-done.6, f32[1,4]{1,0:T(1,128)S(1)} %copy-done.7, f32[16,64,256]{2,1,0:T(8,128)S(1)} %get-tuple-element.47.refs_9_.refs_0_, ...), custom_call_target="tpu_custom_call", output_to_operand_aliasing={{2}: (10, {})} | custom-call | flops 1024 | bytes 1024 | tf_op jit(solution)/shard_map/pallas_call | solution.py:22
  89.2 1.6 %collective-permute-start.17 = (f32[4,64,256]{2,1,0:T(8,128)S(1)}, f32[4,64,256]{2,1,0:T(8,128)S(1)}, u32[]{:S(2)}, u32[]{:S(2)}) collective-permute-start(f32[4,64,256]{2,1,0:T(8,128)S(1)} %add.27), channel_id=1, source_target_pairs={{0,16},{8,24},{16,0},{24,8},{1,17},{9,25},{17,1},{25,9},{2,18},{10... | collective-permute-start | bytes 786440 | tf_op jit(solution)/shard_map/ppermute | solution.py:325
  92.2 2.5 %collective-permute-start.14 = (f32[4,64,256]{2,1,0:T(8,128)S(1)}, f32[4,64,256]{2,1,0:T(8,128)S(1)}, u32[]{:S(2)}, u32[]{:S(2)}) collective-permute-start(f32[4,64,256]{2,1,0:T(8,128)S(1)} %get-tuple-element.67), channel_id=1, source_target_pairs={{0,1},{1,0},{2,3},{3,2},{4,5},{5,4},{6,7},{7,6},{8,9},{9,8},{10,11... | collective-permute-start | bytes 786440 | tf_op jit(solution)/shard_map/ppermute | solution.py:315
  95.4 3.0 %collective-permute-done.17 = f32[4,64,256]{2,1,0:T(8,128)S(1)} collective-permute-done((f32[4,64,256]{2,1,0:T(8,128)S(1)}, f32[4,64,256]{2,1,0:T(8,128)S(1)}, u32[]{:S(2)}, u32[]{:S(2)}) %collective-permute-start.17) | collective-permute-done | bytes 262176 | tf_op jit(solution)/shard_map/ppermute | solution.py:325
  98.5 5.0 %collective-permute-done.20 = f32[4,64,256]{2,1,0:T(8,128)S(1)} collective-permute-done((f32[4,64,256]{2,1,0:T(8,128)S(1)}, f32[4,64,256]{2,1,0:T(8,128)S(1)}, u32[]{:S(2)}, u32[]{:S(2)}) %collective-permute-start.20) | collective-permute-done | bytes 262176 | tf_op jit(solution)/shard_map/ppermute | solution.py:325
  103.6 2.4 %shard_map.130.refs_6_ = f32[16,64,256]{2,1,0:T(8,128)} custom-call(s32[3]{0:T(128)S(1)} %pad_add_fusion.info, f32[16,64,256]{2,1,0:T(8,128)S(1)} %get-tuple-element.66.current.refs_0_, f32[16,64,256]{2,1,0:T(8,128)S(1)} %get-tuple-element.57.refs_0_.later.refs_1_, f32[16,64,256]{2,1,0:T(8,128)S(1)} %get-tuple-element.40.refs_4_.rate, ...), custom_call_target="tpu_custom_call" | custom-call | flops 1024 | bytes 1024 | tf_op jit(solution)/shard_map/pallas_call | solution.py:22
  106.1 2.5 %shard_map.131 = f32[16,64,256]{2,1,0:T(8,128)} custom-call(s32[3]{0:T(128)S(1)} %pad_add_fusion.info, f32[16,64,256]{2,1,0:T(8,128)S(1)} %get-tuple-element.66.current.refs_0_, f32[16,64,256]{2,1,0:T(8,128)S(1)} %get-tuple-element.57.refs_0_.later.refs_1_, f32[4,64,256]{2,1,0:T(8,128)S(1)} %collective-permute-done.14.refs_2_, ...), custom_call_target="tpu_custom_call", output_to_operand_aliasing={{}: (7, {})} | custom-call | flops 1024 | bytes 1024 | tf_op jit(solution)/shard_map/pallas_call | solution.py:22
  (59 shorter events, 18.9 us)
Async XLA Ops:
  0.6 18.1 %copy-start.7 = (f32[1,4]{1,0:T(1,128)S(1)}, f32[1,4]{1,0:T(1,128)}, u32[]{:S(2)}) copy-start(f32[1,4]{1,0:T(1,128)} %wavelet.9) | copy-start | bytes 52
  0.6 18.1 %copy-start.6 = (s32[1,3]{1,0:T(1,128)S(1)}, s32[1,3]{1,0:T(1,128)}, u32[]{:S(2)}) copy-start(s32[1,3]{1,0:T(1,128)} %source.9) | copy-start | bytes 40
  1.8 15.7 %collective-permute-start.1 = (f32[4,64,256]{2,1,0:T(8,128)S(1)}, f32[4,64,256]{2,1,0:T(8,128)S(1)}, u32[]{:S(2)}, u32[]{:S(2)}) collective-permute-start(f32[4,64,256]{2,1,0:T(8,128)S(1)} %get-tuple-element.73), channel_id=1, source_target_pairs={{1,2},{3,4},{5,6},{2,1},{4,3},{6,5},{9,10},{11,12},{13,14},{10,9},... | collective-permute-start | bytes 786440 | tf_op jit(solution)/shard_map/ppermute | solution.py:316
  2.4 16.3 %collective-permute-start = (f32[4,64,256]{2,1,0:T(8,128)S(1)}, f32[4,64,256]{2,1,0:T(8,128)S(1)}, u32[]{:S(2)}, u32[]{:S(2)}) collective-permute-start(f32[4,64,256]{2,1,0:T(8,128)S(1)} %get-tuple-element.74), channel_id=1, source_target_pairs={{0,1},{1,0},{2,3},{3,2},{4,5},{5,4},{6,7},{7,6},{8,9},{9,8},{10,11... | collective-permute-start | bytes 786440 | tf_op jit(solution)/shard_map/ppermute | solution.py:315
  16.6 19.0 %collective-permute-start.8 = (f32[4,64,256]{2,1,0:T(8,128)S(1)}, f32[4,64,256]{2,1,0:T(8,128)S(1)}, u32[]{:S(2)}, u32[]{:S(2)}) collective-permute-start(f32[4,64,256]{2,1,0:T(8,128)S(1)} %get-tuple-element.52), channel_id=1, source_target_pairs={{0,1},{1,0},{2,3},{3,2},{4,5},{5,4},{6,7},{7,6},{8,9},{9,8},{10,11... | collective-permute-start | bytes 786440 | tf_op jit(solution)/shard_map/ppermute | solution.py:315
  16.7 18.9 %collective-permute-start.9 = (f32[4,64,256]{2,1,0:T(8,128)S(1)}, f32[4,64,256]{2,1,0:T(8,128)S(1)}, u32[]{:S(2)}, u32[]{:S(2)}) collective-permute-start(f32[4,64,256]{2,1,0:T(8,128)S(1)} %get-tuple-element.53), channel_id=1, source_target_pairs={{1,2},{3,4},{5,6},{2,1},{4,3},{6,5},{9,10},{11,12},{13,14},{10,9},... | collective-permute-start | bytes 786440 | tf_op jit(solution)/shard_map/ppermute | solution.py:316
  21.1 20.1 %collective-permute-start.2 = (f32[4,64,256]{2,1,0:T(8,128)S(1)}, f32[4,64,256]{2,1,0:T(8,128)S(1)}, u32[]{:S(2)}, u32[]{:S(2)}) collective-permute-start(f32[4,64,256]{2,1,0:T(8,128)S(1)} %get-tuple-element.42), channel_id=1, source_target_pairs={{0,1},{1,0},{2,3},{3,2},{4,5},{5,4},{6,7},{7,6},{8,9},{9,8},{10,11... | collective-permute-start | bytes 786440 | tf_op jit(solution)/shard_map/ppermute | solution.py:315
  24.5 16.8 %collective-permute-start.3 = (f32[4,64,256]{2,1,0:T(8,128)S(1)}, f32[4,64,256]{2,1,0:T(8,128)S(1)}, u32[]{:S(2)}, u32[]{:S(2)}) collective-permute-start(f32[4,64,256]{2,1,0:T(8,128)S(1)} %get-tuple-element.43), channel_id=1, source_target_pairs={{1,2},{3,4},{5,6},{2,1},{4,3},{6,5},{9,10},{11,12},{13,14},{10,9},... | collective-permute-start | bytes 786440 | tf_op jit(solution)/shard_map/ppermute | solution.py:316
  38.0 20.5 %collective-permute-start.10 = (f32[4,64,256]{2,1,0:T(8,128)S(1)}, f32[4,64,256]{2,1,0:T(8,128)S(1)}, u32[]{:S(2)}, u32[]{:S(2)}) collective-permute-start(f32[4,64,256]{2,1,0:T(8,128)S(1)} %get-tuple-element.55), channel_id=1, source_target_pairs={{0,1},{1,0},{2,3},{3,2},{4,5},{5,4},{6,7},{7,6},{8,9},{9,8},{10,11... | collective-permute-start | bytes 786440 | tf_op jit(solution)/shard_map/ppermute | solution.py:315
  40.6 18.0 %collective-permute-start.11 = (f32[4,64,256]{2,1,0:T(8,128)S(1)}, f32[4,64,256]{2,1,0:T(8,128)S(1)}, u32[]{:S(2)}, u32[]{:S(2)}) collective-permute-start(f32[4,64,256]{2,1,0:T(8,128)S(1)} %get-tuple-element.56), channel_id=1, source_target_pairs={{1,2},{3,4},{5,6},{2,1},{4,3},{6,5},{9,10},{11,12},{13,14},{10,9},... | collective-permute-start | bytes 786440 | tf_op jit(solution)/shard_map/ppermute | solution.py:316
  43.5 20.7 %collective-permute-start.4 = (f32[4,64,256]{2,1,0:T(8,128)S(1)}, f32[4,64,256]{2,1,0:T(8,128)S(1)}, u32[]{:S(2)}, u32[]{:S(2)}) collective-permute-start(f32[4,64,256]{2,1,0:T(8,128)S(1)} %get-tuple-element.45), channel_id=1, source_target_pairs={{0,1},{1,0},{2,3},{3,2},{4,5},{5,4},{6,7},{7,6},{8,9},{9,8},{10,11... | collective-permute-start | bytes 786440 | tf_op jit(solution)/shard_map/ppermute | solution.py:315
  47.8 16.3 %collective-permute-start.5 = (f32[4,64,256]{2,1,0:T(8,128)S(1)}, f32[4,64,256]{2,1,0:T(8,128)S(1)}, u32[]{:S(2)}, u32[]{:S(2)}) collective-permute-start(f32[4,64,256]{2,1,0:T(8,128)S(1)} %get-tuple-element.46), channel_id=1, source_target_pairs={{1,2},{3,4},{5,6},{2,1},{4,3},{6,5},{9,10},{11,12},{13,14},{10,9},... | collective-permute-start | bytes 786440 | tf_op jit(solution)/shard_map/ppermute | solution.py:316
  60.9 20.5 %collective-permute-start.12 = (f32[4,64,256]{2,1,0:T(8,128)S(1)}, f32[4,64,256]{2,1,0:T(8,128)S(1)}, u32[]{:S(2)}, u32[]{:S(2)}) collective-permute-start(f32[4,64,256]{2,1,0:T(8,128)S(1)} %get-tuple-element.58), channel_id=1, source_target_pairs={{0,1},{1,0},{2,3},{3,2},{4,5},{5,4},{6,7},{7,6},{8,9},{9,8},{10,11... | collective-permute-start | bytes 786440 | tf_op jit(solution)/shard_map/ppermute | solution.py:315
  63.4 18.0 %collective-permute-start.13 = (f32[4,64,256]{2,1,0:T(8,128)S(1)}, f32[4,64,256]{2,1,0:T(8,128)S(1)}, u32[]{:S(2)}, u32[]{:S(2)}) collective-permute-start(f32[4,64,256]{2,1,0:T(8,128)S(1)} %get-tuple-element.59), channel_id=1, source_target_pairs={{1,2},{3,4},{5,6},{2,1},{4,3},{6,5},{9,10},{11,12},{13,14},{10,9},... | collective-permute-start | bytes 786440 | tf_op jit(solution)/shard_map/ppermute | solution.py:316
  66.5 19.6 %collective-permute-start.6 = (f32[4,64,256]{2,1,0:T(8,128)S(1)}, f32[4,64,256]{2,1,0:T(8,128)S(1)}, u32[]{:S(2)}, u32[]{:S(2)}) collective-permute-start(f32[4,64,256]{2,1,0:T(8,128)S(1)} %get-tuple-element.48), channel_id=1, source_target_pairs={{0,1},{1,0},{2,3},{3,2},{4,5},{5,4},{6,7},{7,6},{8,9},{9,8},{10,11... | collective-permute-start | bytes 786440 | tf_op jit(solution)/shard_map/ppermute | solution.py:315
  70.7 15.4 %collective-permute-start.7 = (f32[4,64,256]{2,1,0:T(8,128)S(1)}, f32[4,64,256]{2,1,0:T(8,128)S(1)}, u32[]{:S(2)}, u32[]{:S(2)}) collective-permute-start(f32[4,64,256]{2,1,0:T(8,128)S(1)} %get-tuple-element.49), channel_id=1, source_target_pairs={{1,2},{3,4},{5,6},{2,1},{4,3},{6,5},{9,10},{11,12},{13,14},{10,9},... | collective-permute-start | bytes 786440 | tf_op jit(solution)/shard_map/ppermute | solution.py:316
  85.6 3.6 %collective-permute-start.16 = (f32[4,64,256]{2,1,0:T(8,128)S(1)}, f32[4,64,256]{2,1,0:T(8,128)S(1)}, u32[]{:S(2)}, u32[]{:S(2)}) collective-permute-start(f32[4,64,256]{2,1,0:T(8,128)S(1)} %get-tuple-element.70), channel_id=1, source_target_pairs={{0,8},{8,0},{16,24},{24,16},{1,9},{9,1},{17,25},{25,17},{2,10},{10... | collective-permute-start | bytes 786440 | tf_op jit(solution)/shard_map/ppermute | solution.py:324
  89.0 1.8 %collective-permute-start.19 = (f32[4,64,256]{2,1,0:T(8,128)S(1)}, f32[4,64,256]{2,1,0:T(8,128)S(1)}, u32[]{:S(2)}, u32[]{:S(2)}) collective-permute-start(f32[4,64,256]{2,1,0:T(8,128)S(1)} %get-tuple-element.72), channel_id=1, source_target_pairs={{0,8},{8,0},{16,24},{24,16},{1,9},{9,1},{17,25},{25,17},{2,10},{10... | collective-permute-start | bytes 786440 | tf_op jit(solution)/shard_map/ppermute | solution.py:324
  89.2 9.2 %collective-permute-start.17 = (f32[4,64,256]{2,1,0:T(8,128)S(1)}, f32[4,64,256]{2,1,0:T(8,128)S(1)}, u32[]{:S(2)}, u32[]{:S(2)}) collective-permute-start(f32[4,64,256]{2,1,0:T(8,128)S(1)} %add.27), channel_id=1, source_target_pairs={{0,16},{8,24},{16,0},{24,8},{1,17},{9,25},{17,1},{25,9},{2,18},{10... | collective-permute-start | bytes 786440 | tf_op jit(solution)/shard_map/ppermute | solution.py:325
  90.8 12.7 %collective-permute-start.20 = (f32[4,64,256]{2,1,0:T(8,128)S(1)}, f32[4,64,256]{2,1,0:T(8,128)S(1)}, u32[]{:S(2)}, u32[]{:S(2)}) collective-permute-start(f32[4,64,256]{2,1,0:T(8,128)S(1)} %add.29), channel_id=1, source_target_pairs={{0,16},{8,24},{16,0},{24,8},{1,17},{9,25},{17,1},{25,9},{2,18},{10... | collective-permute-start | bytes 786440 | tf_op jit(solution)/shard_map/ppermute | solution.py:325
  92.2 13.8 %collective-permute-start.14 = (f32[4,64,256]{2,1,0:T(8,128)S(1)}, f32[4,64,256]{2,1,0:T(8,128)S(1)}, u32[]{:S(2)}, u32[]{:S(2)}) collective-permute-start(f32[4,64,256]{2,1,0:T(8,128)S(1)} %get-tuple-element.67), channel_id=1, source_target_pairs={{0,1},{1,0},{2,3},{3,2},{4,5},{5,4},{6,7},{7,6},{8,9},{9,8},{10,11... | collective-permute-start | bytes 786440 | tf_op jit(solution)/shard_map/ppermute | solution.py:315
  94.7 11.4 %collective-permute-start.15 = (f32[4,64,256]{2,1,0:T(8,128)S(1)}, f32[4,64,256]{2,1,0:T(8,128)S(1)}, u32[]{:S(2)}, u32[]{:S(2)}) collective-permute-start(f32[4,64,256]{2,1,0:T(8,128)S(1)} %get-tuple-element.68), channel_id=1, source_target_pairs={{1,2},{3,4},{5,6},{2,1},{4,3},{6,5},{9,10},{11,12},{13,14},{10,9},... | collective-permute-start | bytes 786440 | tf_op jit(solution)/shard_map/ppermute | solution.py:316
  98.4 10.2 %collective-permute-start.18 = (f32[4,64,256]{2,1,0:T(8,128)S(1)}, f32[4,64,256]{2,1,0:T(8,128)S(1)}, u32[]{:S(2)}, u32[]{:S(2)}) collective-permute-start(f32[4,64,256]{2,1,0:T(8,128)S(1)} %add.28.inner_kept), channel_id=1, source_target_pairs={{0,8},{8,0},{16,24},{24,16},{1,9},{9,1},{17,25},{25,17},{2,10},{10... | collective-permute-start | bytes 786440 | tf_op jit(solution)/shard_map/ppermute | solution.py:326
  103.6 5.0 %collective-permute-start.21 = (f32[4,64,256]{2,1,0:T(8,128)S(1)}, f32[4,64,256]{2,1,0:T(8,128)S(1)}, u32[]{:S(2)}, u32[]{:S(2)}) collective-permute-start(f32[4,64,256]{2,1,0:T(8,128)S(1)} %add.30.kept), channel_id=1, source_target_pairs={{0,8},{8,0},{16,24},{24,16},{1,9},{9,1},{17,25},{25,17},{2,10},{10... | collective-permute-start | bytes 786440 | tf_op jit(solution)/shard_map/ppermute | solution.py:326
  (8 other events, 26.9 us)

commit v3 on v2

--- a/solution.py
+++ b/solution.py
@@ -14,20 +14,22 @@
 halo = 4
 
 vmem = pl.BlockSpec(memory_space=pltpu.VMEM)
-smem = pl.BlockSpec(memory_space=pltpu.SMEM)
 hbm = pl.BlockSpec(memory_space=pltpu.HBM)
-
-
-def call(kernel, args, in_specs, outs, scratch=(), aliases={}):
+wherever = pl.BlockSpec(memory_space=pl.ANY)
+
+
+def call(kernel, args, in_specs, outs, scratch=(), aliases={}, limit=24, cost=1024):
     return pl.pallas_call(
         kernel,
-        out_shape=[shape for shape, _ in outs],
+        out_shape=[
+            pltpu.VMEM(shape.shape, shape.dtype) if spec is vmem else shape for shape, spec in outs
+        ],
         in_specs=in_specs,
         out_specs=[spec for _, spec in outs],
         scratch_shapes=list(scratch),
         input_output_aliases=aliases,
-        compiler_params=pltpu.CompilerParams(vmem_limit_bytes=24 * 1024 * 1024),
-        cost_estimate=pl.CostEstimate(flops=1024, bytes_accessed=1024, transcendentals=0),
+        compiler_params=pltpu.CompilerParams(vmem_limit_bytes=limit * 1024 * 1024),
+        cost_estimate=pl.CostEstimate(flops=cost, bytes_accessed=1024, transcendentals=0),
     )(*args)
 
 
@@ -79,23 +81,27 @@
     return band(ny, ny), band(halo * nz, nz)
 
 
-def place(ext, info, near, far):
+def core():
+    return lax.axis_index("shot") % 2
+
+
+def place(ext, near, far):
     planes = ext.shape[0] - 2 * halo
-    odd = info[0]
+    odd = lax.axis_index("dom") % 2
     spot = jnp.where(odd == 1, 0, planes + halo)
     ext[pl.ds(spot, halo)] = near[...]
     ext[pl.ds(planes + halo - spot, halo)] = far[...]
 
 
-def edge_spots(info, planes):
-    odd = info[0]
+def edge_spots(planes):
+    odd = lax.axis_index("dom") % 2
     near = jnp.where(odd == 1, 0, planes - halo)
     return near, planes - halo - near
 
 
-def add_source(field, first, info, source, value):
+def add_source(field, first, planes, source, value):
     count, _, ny = field.shape
-    x = source[0, 0] - info[1] - first
+    x = source[0, 0] - lax.axis_index("dom") * planes - first
     z = source[0, 1]
     y = source[0, 2]
 
@@ -110,7 +116,7 @@
 
 
 def prepare_kernel(
-    info, table, labels, near_field, *refs
+    table, labels, near_field, *refs
 ):
     sources, refs = refs[:3], refs[3:]
     rate, near_edge, far_edge, field, *targets = refs[:7]
@@ -133,17 +139,17 @@
             value = jnp.where(known == region, table[region], value)
         rate[here] = value
     second.wait()
-    near, far = edge_spots(info, planes)
+    near, far = edge_spots(planes)
     near_edge[...] = rate[pl.ds(near, halo)] * field[pl.ds(near, halo)]
     far_edge[...] = rate[pl.ds(far, halo)] * field[pl.ds(far, halo)]
     for copy in others:
         copy.wait()
 
 
-def receivers_kernel(info, index, values, injected):
+def receivers_kernel(index, values, _, injected):
     steps, planes, nz, ny = injected.shape
     count = index.shape[1]
-    local = index[0:1, :] - info[1]
+    local = index[0:1, :] - lax.axis_index("dom") * planes
     cell = jnp.where((local >= 0) & (local < planes), local * nz + index[1:2, :], -1)
     at_y = lax.broadcasted_iota(jnp.int32, (ny, count), 0) == index[2:3, :]
     parts = []
@@ -166,10 +172,10 @@
             injected[step, pl.ds(part * group, group)] = total.reshape(group, nz, ny)
 
 
-def forward_kernel(step, info, source, wavelet, *refs):
-    current, previous, near, far, rate, upcoming, lap, near_edge, far_edge, ext = refs
+def forward_kernel(step, source, wavelet, *refs):
+    current, previous, near, far, rate, _, upcoming, lap, near_edge, far_edge, ext = refs
     planes = current.shape[0]
-    place(ext, info, near, far)
+    place(ext, near, far)
     ext[pl.ds(halo, planes)] = current[...]
     along_y, along_z = bands(current)
     for first in range(0, planes, halo):
@@ -177,32 +183,32 @@
         value = laplacian(ext, first + halo, along_y, along_z)
         lap[here] = value
         upcoming[here] = 2.0 * current[here] - previous[here] + rate[here] * value
-    add_source(upcoming, 0, info, source, wavelet[0, step])
-    near_at, far_at = edge_spots(info, planes)
+    add_source(upcoming, 0, planes, source, wavelet[0, step])
+    near_at, far_at = edge_spots(planes)
     near_edge[...] = upcoming[pl.ds(near_at, halo)]
     far_edge[...] = upcoming[pl.ds(far_at, halo)]
 
 
-def adjoint_kernel(step, info, *refs):
+def adjoint_kernel(step, *refs):
     current, later, near, far, rate, injected, earlier, near_edge, far_edge, ext = refs
     planes = current.shape[0]
-    place(ext, info, near, far)
+    place(ext, near, far)
     ext[pl.ds(halo, planes)] = rate[...] * current[...]
     along_y, along_z = bands(current)
     for first in range(0, planes, halo):
         here = pl.ds(first, halo)
         value = laplacian(ext, first + halo, along_y, along_z)
         earlier[here] = 2.0 * current[here] - later[here] + value + injected[step, here]
-    near_at, far_at = edge_spots(info, planes)
+    near_at, far_at = edge_spots(planes)
     near_edge[...] = rate[pl.ds(near_at, halo)] * earlier[pl.ds(near_at, halo)]
     far_edge[...] = rate[pl.ds(far_at, halo)] * earlier[pl.ds(far_at, halo)]
 
 
-def turn_kernel(forward_step, step, info, source, wavelet, *refs):
+def turn_kernel(forward_step, step, source, wavelet, *refs):
     (current, later, near, far, rate, injected, lap1, lap2, lap3, wave, before, a5,
-     earlier, near_edge, far_edge, rest, keep, send, final, ext, stage, grad, sem) = refs
+     earlier, near_edge, far_edge, rest, keep, send, inner, ext, grad) = refs
     planes = current.shape[0]
-    place(ext, info, near, far)
+    place(ext, near, far)
     ext[pl.ds(halo, planes)] = rate[...] * current[...]
     along_y, along_z = bands(current)
     for first in range(0, planes, halo):
@@ -217,46 +223,42 @@
             rest[1] = partial
         else:
             value = laplacian(wave, first, along_y, along_z)
-            inner = pl.ds(first - halo, halo)
-            stage[inner] = 2.0 * wave[here] - before[here] + rate[here] * value
-            grad[inner] = partial + a5[here] * value
-    add_source(stage, halo, info, source, wavelet[0, forward_step])
-    copy = pltpu.make_async_copy(stage, final.at[pl.ds(halo, planes - 2 * halo)], sem)
-    copy.start()
-    near_at, far_at = edge_spots(info, planes)
+            within = pl.ds(first - halo, halo)
+            inner[within] = 2.0 * wave[here] - before[here] + rate[here] * value
+            grad[within] = partial + a5[here] * value
+    add_source(inner, halo, planes, source, wavelet[0, forward_step])
+    near_at, far_at = edge_spots(planes)
     near_edge[...] = rate[pl.ds(near_at, halo)] * earlier[pl.ds(near_at, halo)]
     far_edge[...] = rate[pl.ds(far_at, halo)] * earlier[pl.ds(far_at, halo)]
     half = keep.shape[0]
-    mine = info[2] * half
+    mine = core() * half
     keep[...] = grad[pl.ds(mine, half)]
     send[...] = grad[pl.ds(half - mine, half)]
-    copy.wait()
-
-
-def forward_outer_kernel(step, info, source, wavelet, *refs):
-    (current, previous, near, far, rate, rest, a5, _,
-     keep, send, final, ext, stage, grad, sems) = refs
+
+
+def forward_outer_kernel(step, source, wavelet, *refs):
+    current, previous, near, far, rate, rest, a5, keep, send, outer, ext, grad = refs
     planes = current.shape[0]
-    place(ext, info, near, far)
+    place(ext, near, far)
     ext[pl.ds(halo, planes)] = current[...]
     along_y, along_z = bands(current)
-    copies = []
     for side, first in enumerate((0, planes - halo)):
         here = pl.ds(first, halo)
         value = laplacian(ext, first + halo, along_y, along_z)
-        stage[side] = 2.0 * current[here] - previous[here] + rate[here] * value
+        outer[side] = 2.0 * current[here] - previous[here] + rate[here] * value
         grad[side] = rest[side] + a5[here] * value
-        add_source(stage.at[side], first, info, source, wavelet[0, step])
-        copies.append(pltpu.make_async_copy(stage.at[side], final.at[here], sems.at[side]))
-        copies[side].start()
-    keep[...] = grad[info[2]]
-    send[...] = grad[1 - info[2]]
-    for copy in copies:
-        copy.wait()
-
-
-def adjoint_inner_kernel(step, info, current, later, rate, injected, first_adjoint, ext, stage, sem):
+        add_source(outer.at[side], first, planes, source, wavelet[0, step])
+    keep[...] = grad[core()]
+    send[...] = grad[1 - core()]
+
+
+def adjoint_inner_kernel(step, *refs):
+    (current, later, rate, injected, inner, near_in, far_in, _,
+     first_adjoint, final, near_edge, far_edge, ext, stage, sems) = refs
     planes = current.shape[0]
+    within = pl.ds(halo, planes - 2 * halo)
+    wave_copy = pltpu.make_async_copy(inner, final.at[within], sems.at[0])
+    wave_copy.start()
     ext[...] = rate[...] * current[...]
     along_y, along_z = bands(current)
     for first in range(halo, planes - halo, halo):
@@ -265,33 +267,44 @@
         stage[pl.ds(first - halo, halo)] = (
             2.0 * current[here] - later[here] + value + injected[step, here]
         )
-    copy = pltpu.make_async_copy(stage, first_adjoint.at[pl.ds(halo, planes - 2 * halo)], sem)
+    copy = pltpu.make_async_copy(stage, first_adjoint.at[within], sems.at[1])
     copy.start()
+    near_edge[...] = near_in[...]
+    far_edge[...] = far_in[...]
+    wave_copy.wait()
     copy.wait()
 
 
-def adjoint_outer_kernel(step, info, *refs):
-    current, later, near, far, rate, injected, _, first_adjoint, ext, stage, sems = refs
+def adjoint_outer_kernel(step, *refs):
+    (current, later, near, far, rate, injected, outer, _, _,
+     first_adjoint, final, token, ext, stage, sems) = refs
     planes = current.shape[0]
-    place(ext, info, near, far)
+    copies = []
+    for side, first in enumerate((0, planes - halo)):
+        here = pl.ds(first, halo)
+        copies.append(pltpu.make_async_copy(outer.at[side], final.at[here], sems.at[side]))
+        copies[-1].start()
+    place(ext, near, far)
     ext[pl.ds(halo, planes)] = rate[...] * current[...]
     along_y, along_z = bands(current)
-    copies = []
     for side, first in enumerate((0, planes - halo)):
         here = pl.ds(first, halo)
         value = laplacian(ext, first + halo, along_y, along_z)
         stage[side] = 2.0 * current[here] - later[here] + value + injected[step, here]
-        copies.append(pltpu.make_async_copy(stage.at[side], first_adjoint.at[here], sems.at[side]))
-        copies[side].start()
+        copies.append(
+            pltpu.make_async_copy(stage.at[side], first_adjoint.at[here], sems.at[2 + side])
+        )
+        copies[-1].start()
+    token[...] = jnp.zeros_like(token)
     for copy in copies:
         copy.wait()
 
 
-def assemble_kernel(info, inner_kept, inner_got, kept, got, total, sems):
+def assemble_kernel(inner_kept, inner_got, kept, got, total, sems):
     planes = total.shape[0]
     half = inner_kept.shape[0]
-    mine = info[2] * half
-    side = info[2] * (planes - halo)
+    mine = core() * half
+    side = core() * (planes - halo)
     spots = (
         (inner_kept, halo + mine, half),
         (inner_got, halo + half - mine, half),
@@ -317,12 +330,42 @@
     )
 
 
-def summed(keep, send):
+def parts_kernel(keep, *refs):
+    parts, total = refs[:-2], refs[-1]
+    size = parts[0].shape[0]
+    for n, part in enumerate(parts):
+        here = pl.ds(n * size, size)
+        total[here] = keep[here] + part[...]
+
+
+def add_kernel(a, b, _, total):
+    total[...] = a[...] + b[...]
+
+
+def first_sum(keep, send, after, count):
     shots = lax.axis_size("shot")
     pairs = [(i, i ^ 1) for i in range(shots)]
     across = [(i, i ^ 2) for i in range(shots)]
-    kept = keep + lax.ppermute(send, "shot", pairs)
-    kept = kept + lax.ppermute(kept, "shot", across)
+    size = send.shape[0] // count
+    got = [lax.ppermute(send[n * size : (n + 1) * size], "shot", pairs) for n in range(count)]
+    (kept,) = call(
+        parts_kernel,
+        (keep, *got, after),
+        [vmem] * (1 + count) + [wherever],
+        [(jax.ShapeDtypeStruct(keep.shape, jnp.float32), vmem)],
+    )
+    return kept, lax.ppermute(kept, "shot", across)
+
+
+def second_sum(kept, got, after):
+    shots = lax.axis_size("shot")
+    pairs = [(i, i ^ 1) for i in range(shots)]
+    (kept,) = call(
+        add_kernel,
+        (kept, got, after),
+        [vmem, vmem, wherever],
+        [(jax.ShapeDtypeStruct(kept.shape, jnp.float32), vmem)],
+    )
     return kept, lax.ppermute(kept, "shot", pairs)
 
 
@@ -340,29 +383,31 @@
 ):
     planes, nz, ny = wave_current.shape[1:]
     steps = wavelet.shape[1]
-    place_x = lax.axis_index("dom")
-    odd = place_x % 2
-    info = jnp.stack([odd, place_x * planes, lax.axis_index("shot") % 2]).astype(jnp.int32)
+    odd = lax.axis_index("dom") % 2
     u0, u1 = wave_before[0], wave_current[0]
     a6, a5 = adjoint_far[0], adjoint_near[0]
+    u0, u1, a6, a5, labels = (
+        pltpu.with_memory_space_constraint(x, pltpu.HBM) for x in (u0, u1, a6, a5, labels)
+    )
     whole = f32(planes, nz, ny)
     block = (whole, vmem)
     edge = (f32(halo, nz, ny), vmem)
     inner = planes - 2 * halo
     quarter = (f32(inner // 2, nz, ny), vmem)
+    pair = (f32(2, halo, nz, ny), vmem)
     ext = pltpu.VMEM((planes + 2 * halo, nz, ny), jnp.float32)
     within = pltpu.VMEM((inner, nz, ny), jnp.float32)
     outer = pltpu.VMEM((2, halo, nz, ny), jnp.float32)
 
     near_at = jnp.where(odd == 1, 0, planes - halo)
-    near_edge = lax.dynamic_slice_in_dim(u1, near_at, halo, axis=0)
-    far_edge = lax.dynamic_slice_in_dim(u1, planes - halo - near_at, halo, axis=0)
+    near_edge = lax.dynamic_slice_in_dim(wave_current[0], near_at, halo, axis=0)
+    far_edge = lax.dynamic_slice_in_dim(wave_current[0], planes - halo - near_at, halo, axis=0)
     u_halo = swap(near_edge, far_edge)
 
     rate, near_edge, far_edge, a5, u1, u0, a6 = call(
         prepare_kernel,
-        (info, table, labels, a5, u1, u0, a6),
-        [smem, smem] + [hbm] * 5,
+        (table, labels, a5, u1, u0, a6),
+        [vmem] + [hbm] * 5,
         [block, edge, edge] + [block] * 4,
         [pltpu.VMEM((planes, nz, ny), jnp.int32), pltpu.SemaphoreType.DMA((5,))],
     )
@@ -370,8 +415,8 @@
 
     (injected,) = call(
         receivers_kernel,
-        (info, receiver_index[0].T, residual[0]),
-        [smem, vmem, vmem],
+        (receiver_index[0].T, residual[0], rate),
+        [vmem, vmem, wherever],
         [(f32(steps, planes, nz, ny), vmem)],
     )
 
@@ -381,8 +426,8 @@
     for n in range(steps - 1):
         upcoming, lap, near_edge, far_edge = call(
             functools.partial(forward_kernel, n),
-            (info, source_index, wavelet, current, previous, *u_halo, rate),
-            [smem] * 3 + [vmem] * 5,
+            (source_index, wavelet, current, previous, *u_halo, rate, injected),
+            [vmem] * 7 + [wherever],
             [block, block, edge, edge],
             [ext],
         )
@@ -393,52 +438,56 @@
         if n < steps - 2:
             earlier, near_edge, far_edge = call(
                 functools.partial(adjoint_kernel, step),
-                (info, adjoint, later, *a_halo, rate, injected),
-                [smem] + [vmem] * 6,
+                (adjoint, later, *a_halo, rate, injected),
+                [vmem] * 6,
                 [block, edge, edge],
                 [ext],
             )
         else:
-            earlier, near_edge, far_edge, rest, keep, send, final = call(
+            earlier, near_edge, far_edge, rest, keep, send, inner_wave = call(
                 functools.partial(turn_kernel, steps - 1, step),
-                (info, source_index, wavelet, adjoint, later, *a_halo, rate, injected, *laps,
+                (source_index, wavelet, adjoint, later, *a_halo, rate, injected, *laps,
                  current, previous, a5),
-                [smem] * 3 + [vmem] * 12,
-                [block, edge, edge, (f32(2, halo, nz, ny), vmem), quarter, quarter, (whole, hbm)],
-                [ext, within, within, pltpu.SemaphoreType.DMA],
+                [vmem] * 14,
+                [block, edge, edge, pair, quarter, quarter, (f32(inner, nz, ny), vmem)],
+                [ext, within],
             )
-        a_halo = swap(near_edge, far_edge)
+        if n < steps - 2:
+            a_halo = swap(near_edge, far_edge)
         later, adjoint = adjoint, earlier
 
-    inner_kept, inner_got = summed(keep, send)
-    keep, send, final = call(
+    inner_sum = first_sum(keep, send, keep, 4)
+    first_adjoint, final, near_edge, far_edge = call(
+        functools.partial(adjoint_inner_kernel, 0),
+        (adjoint, later, rate, injected, inner_wave, near_edge, far_edge, inner_sum[0]),
+        [vmem] * 7 + [wherever],
+        [(whole, hbm), (whole, hbm), edge, edge],
+        [pltpu.VMEM((planes, nz, ny), jnp.float32), within, pltpu.SemaphoreType.DMA((2,))],
+    )
+    a_halo = swap(near_edge, far_edge)
+    keep, send, outer_wave = call(
         functools.partial(forward_outer_kernel, steps - 1),
-        (info, source_index, wavelet, current, previous, *u_halo, rate, rest, a5, final),
-        [smem] * 3 + [vmem] * 7 + [hbm],
-        [edge, edge, (whole, hbm)],
-        [ext, outer, outer, pltpu.SemaphoreType.DMA((2,))],
-        {10: 2},
-    )
-    kept, got = summed(keep, send)
-    (first_adjoint,) = call(
-        functools.partial(adjoint_inner_kernel, 0),
-        (info, adjoint, later, rate, injected),
-        [smem] + [vmem] * 4,
-        [(whole, hbm)],
-        [pltpu.VMEM((planes, nz, ny), jnp.float32), within, pltpu.SemaphoreType.DMA],
-    )
-    (first_adjoint,) = call(
+        (source_index, wavelet, current, previous, *u_halo, rate, rest, a5),
+        [vmem] * 9,
+        [edge, edge, pair],
+        [ext, outer],
+    )
+    outer_sum = first_sum(keep, send, inner_sum[1], 2)
+    first_adjoint, final, token = call(
         functools.partial(adjoint_outer_kernel, 0),
-        (info, adjoint, later, *a_halo, rate, injected, first_adjoint),
-        [smem] + [vmem] * 6 + [hbm],
-        [(whole, hbm)],
-        [ext, outer, pltpu.SemaphoreType.DMA((2,))],
-        {7: 0},
-    )
+        (adjoint, later, *a_halo, rate, injected, outer_wave, first_adjoint, final),
+        [vmem] * 7 + [hbm] * 2,
+        [(whole, hbm), (whole, hbm), (f32(8, 128), vmem)],
+        [ext, outer, pltpu.SemaphoreType.DMA((4,))],
+        {7: 0, 8: 1},
+        cost=2000000000,
+    )
+    inner_kept, inner_got = second_sum(*inner_sum, token)
+    kept, got = second_sum(*outer_sum, token)
     (total,) = call(
         assemble_kernel,
-        (info, inner_kept, inner_got, kept, got),
-        [smem] + [vmem] * 4,
+        (inner_kept, inner_got, kept, got),
+        [vmem] * 4,
         [(whole, hbm)],
         [pltpu.SemaphoreType.DMA((4,))],
     )

time: 111 us -> 105 us (0.946)
  Pallas kernels: 33.9 us -> 27.7 us
  local copies, waits for them, and re-layouts: 7.88 us -> 1.78 us
  waiting for transfers between devices: 33 us -> 38.8 us
    ppermute x8, waiting for transfers between devices: 24.9 us -> 34.7 us  [swap(): lax.ppermute(near_edge, 'dom', near_pairs)]
    pallas_call x12 -> x16, Pallas kernels: 33.9 us -> 27.7 us  [call(): pl.pallas_call(kernel, out_shape=[pltpu.VMEM(shape.shape, shape.dtype) if...]
    unnamed x21 -> x11, local copies, waits for them, and re-layouts: 6.8 us -> 0.68 us
    ppermute x6 -> x10, waiting for transfers between devices: 8.04 us -> 4.08 us  [the longest x6 2.78 us: first_sum(): lax.ppermute(send[n * size:(n + 1) * size], 'shot', pairs)]
    ppermute x6 -> x10, starting transfers between devices: 3.34 us -> 4.15 us  [the longest x2 2.15 us: first_sum(): return (kept, lax.ppermute(kept, 'shot', across))]
  transfers between devices with their start and end apart: 22 -> 26, of which waited for: 8 -> 14; matrix products, arithmetic and copies ran while one was open for 0% -> 0% of each run, Pallas kernels for 29% -> 26%
where the time goes in v3:
time: 105 us; the launch traced here: 104 us
  waiting for transfers between devices  38.8 us (37%)
  starting transfers between devices  34.5 us (33%)
  Pallas kernels  27.7 us (26%)
  local copies, waits for them, and re-layouts  1.78 us (2%)
  between operations  1.08 us (1%)
    ppermute x8, waiting for transfers between devices, swap(): lax.ppermute(near_edge, 'dom', near_pairs)  34.7 us
    pallas_call x16, Pallas kernels, call(): pl.pallas_call(kernel, out_shape=[pltpu.VMEM(shape.shape, shape.dtype) if...  27.7 us
    ppermute x8, starting transfers between devices, swap(): lax.ppermute(near_edge, 'dom', near_pairs)  24.8 us
    ppermute x8, starting transfers between devices, swap(): lax.ppermute(far_edge, 'dom', far_pairs)  5.52 us
    ppermute x6, waiting for transfers between devices, first_sum(): lax.ppermute(send[n * size:(n + 1) * size], 'shot', pairs)  2.78 us
    ppermute x2, starting transfers between devices, first_sum(): return (kept, lax.ppermute(kept, 'shot', across))  2.15 us
  transfers between devices with their start and end apart: 26, of which 14 were waited for; matrix products, arithmetic and copies ran while one was open for 0% of the time, Pallas kernels for 26%

profile of v3, /device:TPU:0, one launch (start us, length us, event | category | flops | bytes accessed | tf_op | source)
XLA Modules:
  0.0 103.8 jit_solution(9263471509169048231)
XLA Ops:
  0.7 1.1 %dynamic-slice_bitcast_fusion = (f32[4,64,256]{2,1,0:T(8,128)S(1)}, f32[4,64,256]{2,1,0:T(8,128)S(1)}) fusion(f32[1,16,64,256]{3,2,1,0:T(8,128)} %param.11, s32[]{:T(128)S(6)} %select_n.17, s32[]{:T(128)S(6)} %select_n.16), kind=kLoop, calls=%fused_computation | loop fusion | bytes 1048584 | tf_op jit(solution)/shard_map/dynamic_slice | solution.py:404
  2.4 5.8 %collective-permute-start.6 = (f32[4,64,256]{2,1,0:T(8,128)S(1)}, f32[4,64,256]{2,1,0:T(8,128)S(1)}, u32[]{:S(2)}, u32[]{:S(2)}) collective-permute-start(f32[4,64,256]{2,1,0:T(8,128)S(1)} %get-tuple-element.88), channel_id=1, source_target_pairs={{0,1},{1,0},{2,3},{3,2},{4,5},{5,4},{6,7},{7,6},{8,9},{9,8},{10,11... | collective-permute-start | bytes 786440 | tf_op jit(solution)/shard_map/ppermute | solution.py:328
  8.9 2.6 %shard_map.121 = (f32[16,64,256]{2,1,0:T(8,128)S(1)}, f32[4,64,256]{2,1,0:T(8,128)S(1)}, f32[4,64,256]{2,1,0:T(8,128)S(1)}, f32[16,64,256]{2,1,0:T(8,128)S(1)}, ...) custom-call(f32[8]{0:T(128)S(1)} %copy-done.3, s32[16,64,256]{2,1,0:T(8,128)} %labels.1, ...), custom_call_target="tpu_custom_call" | custom-call | flops 1024 | bytes 1024 | tf_op jit(solution)/shard_map/pallas_call | solution.py:22
  12.3 6.7 %shard_map.122.refs_5_.refs_3_ = f32[4,16,64,256]{3,2,1,0:T(8,128)S(1)} custom-call(s32[3,1024]{1,0:T(4,128)S(1)} %bitcast.16, f32[4,1024]{1,0:T(4,128)S(1)} %bitcast.17, f32[16,64,256]{2,1,0:T(8,128)S(1)} %get-tuple-element.49._.refs_4_.refs_2_), custom_call_target="tpu_custom_call" | custom-call | flops 1024 | bytes 1024 | tf_op jit(solution)/shard_map/pallas_call | solution.py:22
  19.0 5.3 %collective-permute-done.6.refs_2_ = f32[4,64,256]{2,1,0:T(8,128)S(1)} collective-permute-done((f32[4,64,256]{2,1,0:T(8,128)S(1)}, f32[4,64,256]{2,1,0:T(8,128)S(1)}, u32[]{:S(2)}, u32[]{:S(2)}) %collective-permute-start.6) | collective-permute-done | bytes 262176 | tf_op jit(solution)/shard_map/ppermute | solution.py:328
  24.4 1.8 %shard_map.125 = (f32[16,64,256]{2,1,0:T(8,128)S(1)}, f32[16,64,256]{2,1,0:T(8,128)S(1)}, f32[4,64,256]{2,1,0:T(8,128)S(1)}, f32[4,64,256]{2,1,0:T(8,128)S(1)}) custom-call(s32[1,3]{1,0:T(1,128)S(1)} %copy-done.1, f32[1,4]{1,0:T(1,128)S(1)} %copy-done.2, f32[16,64,256]{2,1,0:T(8,128)S(1)} %get-tuple-element.56.refs_0_.refs_1_, ...), custom_call_target="tpu_custom_call" | custom-call | flops 1024 | bytes 1024 | tf_op jit(solution)/shard_map/pallas_call | solution.py:22
  26.2 2.5 %collective-permute-start.8 = (f32[4,64,256]{2,1,0:T(8,128)S(1)}, f32[4,64,256]{2,1,0:T(8,128)S(1)}, u32[]{:S(2)}, u32[]{:S(2)}) collective-permute-start(f32[4,64,256]{2,1,0:T(8,128)S(1)} %get-tuple-element.60), channel_id=1, source_target_pairs={{0,1},{1,0},{2,3},{3,2},{4,5},{5,4},{6,7},{7,6},{8,9},{9,8},{10,11... | collective-permute-start | bytes 786440 | tf_op jit(solution)/shard_map/ppermute | solution.py:328
  30.0 1.9 %shard_map.123 = (f32[16,64,256]{2,1,0:T(8,128)S(1)}, f32[4,64,256]{2,1,0:T(8,128)S(1)}, f32[4,64,256]{2,1,0:T(8,128)S(1)}) custom-call(f32[16,64,256]{2,1,0:T(8,128)S(1)} %get-tuple-element.45.refs_0_.refs_1_.refs_11_.refs_6_, f32[16,64,256]{2,1,0:T(8,128)S(1)} %get-tuple-element.46.refs_1_, f32[4,64,256]{2,1,0:T(8,128)S(1)} %collective-permute-done.refs_2_, ...), custom_call_target="tpu_custom_call" | custom-call | flops 1024 | bytes 1024 | tf_op jit(solution)/shard_map/pallas_call | solution.py:22
  31.9 3.8 %collective-permute-start.2 = (f32[4,64,256]{2,1,0:T(8,128)S(1)}, f32[4,64,256]{2,1,0:T(8,128)S(1)}, u32[]{:S(2)}, u32[]{:S(2)}) collective-permute-start(f32[4,64,256]{2,1,0:T(8,128)S(1)} %get-tuple-element.51), channel_id=1, source_target_pairs={{0,1},{1,0},{2,3},{3,2},{4,5},{5,4},{6,7},{7,6},{8,9},{9,8},{10,11... | collective-permute-start | bytes 786440 | tf_op jit(solution)/shard_map/ppermute | solution.py:328
  36.3 10.5 %collective-permute-done.8.refs_2_ = f32[4,64,256]{2,1,0:T(8,128)S(1)} collective-permute-done((f32[4,64,256]{2,1,0:T(8,128)S(1)}, f32[4,64,256]{2,1,0:T(8,128)S(1)}, u32[]{:S(2)}, u32[]{:S(2)}) %collective-permute-start.8) | collective-permute-done | bytes 262176 | tf_op jit(solution)/shard_map/ppermute | solution.py:328
  46.8 1.7 %shard_map.126 = (f32[16,64,256]{2,1,0:T(8,128)S(1)}, f32[16,64,256]{2,1,0:T(8,128)S(1)}, f32[4,64,256]{2,1,0:T(8,128)S(1)}, f32[4,64,256]{2,1,0:T(8,128)S(1)}) custom-call(s32[1,3]{1,0:T(1,128)S(1)} %copy-done.1, f32[1,4]{1,0:T(1,128)S(1)} %copy-done.2, f32[16,64,256]{2,1,0:T(8,128)S(1)} %get-tuple-element.59.refs_0_.refs_1_, ...), custom_call_target="tpu_custom_call" | custom-call | flops 1024 | bytes 1024 | tf_op jit(solution)/shard_map/pallas_call | solution.py:22
  48.6 2.5 %collective-permute-start.10 = (f32[4,64,256]{2,1,0:T(8,128)S(1)}, f32[4,64,256]{2,1,0:T(8,128)S(1)}, u32[]{:S(2)}, u32[]{:S(2)}) collective-permute-start(f32[4,64,256]{2,1,0:T(8,128)S(1)} %get-tuple-element.64), channel_id=1, source_target_pairs={{0,1},{1,0},{2,3},{3,2},{4,5},{5,4},{6,7},{7,6},{8,9},{9,8},{10,11... | collective-permute-start | bytes 786440 | tf_op jit(solution)/shard_map/ppermute | solution.py:328
  52.5 1.8 %shard_map.124 = (f32[16,64,256]{2,1,0:T(8,128)S(1)}, f32[4,64,256]{2,1,0:T(8,128)S(1)}, f32[4,64,256]{2,1,0:T(8,128)S(1)}) custom-call(f32[16,64,256]{2,1,0:T(8,128)S(1)} %get-tuple-element.50.refs_0_.refs_1_, f32[16,64,256]{2,1,0:T(8,128)S(1)} %get-tuple-element.45.refs_0_.refs_1_.refs_11_.refs_6_, f32[4,64,256]{2,1,0:T(8,128)S(1)} %collective-permute-done.2.refs_2_, ...), custom_call_target="tpu_custom_call" | custom-call | flops 1024 | bytes 1024 | tf_op jit(solution)/shard_map/pallas_call | solution.py:22
  54.3 3.9 %collective-permute-start.4 = (f32[4,64,256]{2,1,0:T(8,128)S(1)}, f32[4,64,256]{2,1,0:T(8,128)S(1)}, u32[]{:S(2)}, u32[]{:S(2)}) collective-permute-start(f32[4,64,256]{2,1,0:T(8,128)S(1)} %get-tuple-element.54), channel_id=1, source_target_pairs={{0,1},{1,0},{2,3},{3,2},{4,5},{5,4},{6,7},{7,6},{8,9},{9,8},{10,11... | collective-permute-start | bytes 786440 | tf_op jit(solution)/shard_map/ppermute | solution.py:328
  58.8 10.5 %collective-permute-done.10.refs_2_ = f32[4,64,256]{2,1,0:T(8,128)S(1)} collective-permute-done((f32[4,64,256]{2,1,0:T(8,128)S(1)}, f32[4,64,256]{2,1,0:T(8,128)S(1)}, u32[]{:S(2)}, u32[]{:S(2)}) %collective-permute-start.10) | collective-permute-done | bytes 262176 | tf_op jit(solution)/shard_map/ppermute | solution.py:328
  69.3 1.7 %shard_map.127 = (f32[16,64,256]{2,1,0:T(8,128)S(1)}, f32[16,64,256]{2,1,0:T(8,128)S(1)}, f32[4,64,256]{2,1,0:T(8,128)S(1)}, f32[4,64,256]{2,1,0:T(8,128)S(1)}) custom-call(s32[1,3]{1,0:T(1,128)S(1)} %copy-done.1, f32[1,4]{1,0:T(1,128)S(1)} %copy-done.2, f32[16,64,256]{2,1,0:T(8,128)S(1)} %get-tuple-element.63.refs_0_.refs_10_.refs_1_, ...), custom_call_target="tpu_custom_call" | custom-call | flops 1024 | bytes 1024 | tf_op jit(solution)/shard_map/pallas_call | solution.py:22
  71.0 2.5 %collective-permute-start.18 = (f32[4,64,256]{2,1,0:T(8,128)S(1)}, f32[4,64,256]{2,1,0:T(8,128)S(1)}, u32[]{:S(2)}, u32[]{:S(2)}) collective-permute-start(f32[4,64,256]{2,1,0:T(8,128)S(1)} %get-tuple-element.76), channel_id=1, source_target_pairs={{0,1},{1,0},{2,3},{3,2},{4,5},{5,4},{6,7},{7,6},{8,9},{9,8},{10,11... | collective-permute-start | bytes 786440 | tf_op jit(solution)/shard_map/ppermute | solution.py:328
  74.9 2.7 %shard_map.128 = (f32[16,64,256]{2,1,0:T(8,128)S(1)}, f32[4,64,256]{2,1,0:T(8,128)S(1)}, f32[4,64,256]{2,1,0:T(8,128)S(1)}, f32[2,4,64,256]{3,2,1,0:T(8,128)S(1)...) custom-call(s32[1,3]{1,0:T(1,128)S(1)} %copy-done.1, f32[1,4]{1,0:T(1,128)S(1)} %copy-done.2, ...), custom_call_target="tpu_custom_call" | custom-call | flops 1024 | bytes 1024 | tf_op jit(solution)/shard_map/pallas_call | solution.py:22
  80.3 1.6 %collective-permute-start.20 = (f32[4,64,256]{2,1,0:T(8,128)S(1)}, f32[4,64,256]{2,1,0:T(8,128)S(1)}, u32[]{:S(2)}, u32[]{:S(2)}) collective-permute-start(f32[4,64,256]{2,1,0:T(8,128)S(1)} %shard_map.129.refs_7_.a), channel_id=1, source_target_pairs={{0,16},{8,24},{16,0},{24,8},{1,17},{9,25},{17,1},{25,9},{2,18},{10... | collective-permute-start | bytes 786440 | tf_op jit(solution)/shard_map/ppermute | solution.py:357
  81.9 1.9 %shard_map.130 = (f32[16,64,256]{2,1,0:T(8,128)}, f32[16,64,256]{2,1,0:T(8,128)}, f32[4,64,256]{2,1,0:T(8,128)S(1)}, f32[4,64,256]{2,1,0:T(8,128)S(1)}) custom-call(f32[16,64,256]{2,1,0:T(8,128)S(1)} %get-tuple-element.68.refs_0_, f32[16,64,256]{2,1,0:T(8,128)S(1)} %get-tuple-element.53.refs_0_.refs_1_, ...), custom_call_target="tpu_custom_call" | custom-call | flops 1024 | bytes 1024 | tf_op jit(solution)/shard_map/pallas_call | solution.py:22
  83.8 3.7 %collective-permute-start.16 = (f32[4,64,256]{2,1,0:T(8,128)S(1)}, f32[4,64,256]{2,1,0:T(8,128)S(1)}, u32[]{:S(2)}, u32[]{:S(2)}) collective-permute-start(f32[4,64,256]{2,1,0:T(8,128)S(1)} %get-tuple-element.74), channel_id=1, source_target_pairs={{0,1},{1,0},{2,3},{3,2},{4,5},{5,4},{6,7},{7,6},{8,9},{9,8},{10,11... | collective-permute-start | bytes 786440 | tf_op jit(solution)/shard_map/ppermute | solution.py:328
  88.2 1.7 %shard_map.131 = (f32[4,64,256]{2,1,0:T(8,128)S(1)}, f32[4,64,256]{2,1,0:T(8,128)S(1)}, f32[2,4,64,256]{3,2,1,0:T(8,128)S(1)}) custom-call(s32[1,3]{1,0:T(1,128)S(1)} %copy-done.1, f32[1,4]{1,0:T(1,128)S(1)} %copy-done.2, f32[16,64,256]{2,1,0:T(8,128)S(1)} %get-tuple-element.67.refs_9_.refs_0_, ...), custom_call_target="tpu_custom_call" | custom-call | flops 1024 | bytes 1024 | tf_op jit(solution)/shard_map/pallas_call | solution.py:22
  92.1 6.6 %collective-permute-done.16.refs_2_ = f32[4,64,256]{2,1,0:T(8,128)S(1)} collective-permute-done((f32[4,64,256]{2,1,0:T(8,128)S(1)}, f32[4,64,256]{2,1,0:T(8,128)S(1)}, u32[]{:S(2)}, u32[]{:S(2)}) %collective-permute-start.16) | collective-permute-done | bytes 262176 | tf_op jit(solution)/shard_map/ppermute | solution.py:328
  98.7 1.9 %shard_map.132 = (f32[16,64,256]{2,1,0:T(8,128)}, f32[16,64,256]{2,1,0:T(8,128)}, f32[8,128]{1,0:T(8,128)S(1)}) custom-call(f32[16,64,256]{2,1,0:T(8,128)S(1)} %get-tuple-element.68.refs_0_, f32[16,64,256]{2,1,0:T(8,128)S(1)} %get-tuple-element.53.refs_0_.refs_1_, ...), custom_call_target="tpu_custom_call", output_to_operand_aliasing={{0}: (7, {}), {1}: (8, {})} | custom-call | flops 2000000000 | bytes 1024 | tf_op jit(solution)/shard_map/pallas_call | solution.py:22
  (58 shorter events, 15.9 us)
Async XLA Ops:
  1.7 17.3 %collective-permute-start.7 = (f32[4,64,256]{2,1,0:T(8,128)S(1)}, f32[4,64,256]{2,1,0:T(8,128)S(1)}, u32[]{:S(2)}, u32[]{:S(2)}) collective-permute-start(f32[4,64,256]{2,1,0:T(8,128)S(1)} %get-tuple-element.87), channel_id=1, source_target_pairs={{1,2},{3,4},{5,6},{2,1},{4,3},{6,5},{9,10},{11,12},{13,14},{10,9},... | collective-permute-start | bytes 786440 | tf_op jit(solution)/shard_map/ppermute | solution.py:329
  2.4 21.9 %collective-permute-start.6 = (f32[4,64,256]{2,1,0:T(8,128)S(1)}, f32[4,64,256]{2,1,0:T(8,128)S(1)}, u32[]{:S(2)}, u32[]{:S(2)}) collective-permute-start(f32[4,64,256]{2,1,0:T(8,128)S(1)} %get-tuple-element.88), channel_id=1, source_target_pairs={{0,1},{1,0},{2,3},{3,2},{4,5},{5,4},{6,7},{7,6},{8,9},{9,8},{10,11... | collective-permute-start | bytes 786440 | tf_op jit(solution)/shard_map/ppermute | solution.py:328
  11.5 18.5 %collective-permute-start = (f32[4,64,256]{2,1,0:T(8,128)S(1)}, f32[4,64,256]{2,1,0:T(8,128)S(1)}, u32[]{:S(2)}, u32[]{:S(2)}) collective-permute-start(f32[4,64,256]{2,1,0:T(8,128)S(1)} %get-tuple-element.47), channel_id=1, source_target_pairs={{0,1},{1,0},{2,3},{3,2},{4,5},{5,4},{6,7},{7,6},{8,9},{9,8},{10,11... | collective-permute-start | bytes 786440 | tf_op jit(solution)/shard_map/ppermute | solution.py:328
  11.6 18.4 %collective-permute-start.1 = (f32[4,64,256]{2,1,0:T(8,128)S(1)}, f32[4,64,256]{2,1,0:T(8,128)S(1)}, u32[]{:S(2)}, u32[]{:S(2)}) collective-permute-start(f32[4,64,256]{2,1,0:T(8,128)S(1)} %get-tuple-element.48), channel_id=1, source_target_pairs={{1,2},{3,4},{5,6},{2,1},{4,3},{6,5},{9,10},{11,12},{13,14},{10,9},... | collective-permute-start | bytes 786440 | tf_op jit(solution)/shard_map/ppermute | solution.py:329
  26.2 20.7 %collective-permute-start.8 = (f32[4,64,256]{2,1,0:T(8,128)S(1)}, f32[4,64,256]{2,1,0:T(8,128)S(1)}, u32[]{:S(2)}, u32[]{:S(2)}) collective-permute-start(f32[4,64,256]{2,1,0:T(8,128)S(1)} %get-tuple-element.60), channel_id=1, source_target_pairs={{0,1},{1,0},{2,3},{3,2},{4,5},{5,4},{6,7},{7,6},{8,9},{9,8},{10,11... | collective-permute-start | bytes 786440 | tf_op jit(solution)/shard_map/ppermute | solution.py:328
  28.7 18.1 %collective-permute-start.9 = (f32[4,64,256]{2,1,0:T(8,128)S(1)}, f32[4,64,256]{2,1,0:T(8,128)S(1)}, u32[]{:S(2)}, u32[]{:S(2)}) collective-permute-start(f32[4,64,256]{2,1,0:T(8,128)S(1)} %get-tuple-element.61), channel_id=1, source_target_pairs={{1,2},{3,4},{5,6},{2,1},{4,3},{6,5},{9,10},{11,12},{13,14},{10,9},... | collective-permute-start | bytes 786440 | tf_op jit(solution)/shard_map/ppermute | solution.py:329
  31.9 20.6 %collective-permute-start.2 = (f32[4,64,256]{2,1,0:T(8,128)S(1)}, f32[4,64,256]{2,1,0:T(8,128)S(1)}, u32[]{:S(2)}, u32[]{:S(2)}) collective-permute-start(f32[4,64,256]{2,1,0:T(8,128)S(1)} %get-tuple-element.51), channel_id=1, source_target_pairs={{0,1},{1,0},{2,3},{3,2},{4,5},{5,4},{6,7},{7,6},{8,9},{9,8},{10,11... | collective-permute-start | bytes 786440 | tf_op jit(solution)/shard_map/ppermute | solution.py:328
  35.6 16.8 %collective-permute-start.3 = (f32[4,64,256]{2,1,0:T(8,128)S(1)}, f32[4,64,256]{2,1,0:T(8,128)S(1)}, u32[]{:S(2)}, u32[]{:S(2)}) collective-permute-start(f32[4,64,256]{2,1,0:T(8,128)S(1)} %get-tuple-element.52), channel_id=1, source_target_pairs={{1,2},{3,4},{5,6},{2,1},{4,3},{6,5},{9,10},{11,12},{13,14},{10,9},... | collective-permute-start | bytes 786440 | tf_op jit(solution)/shard_map/ppermute | solution.py:329
  48.6 20.7 %collective-permute-start.10 = (f32[4,64,256]{2,1,0:T(8,128)S(1)}, f32[4,64,256]{2,1,0:T(8,128)S(1)}, u32[]{:S(2)}, u32[]{:S(2)}) collective-permute-start(f32[4,64,256]{2,1,0:T(8,128)S(1)} %get-tuple-element.64), channel_id=1, source_target_pairs={{0,1},{1,0},{2,3},{3,2},{4,5},{5,4},{6,7},{7,6},{8,9},{9,8},{10,11... | collective-permute-start | bytes 786440 | tf_op jit(solution)/shard_map/ppermute | solution.py:328
  51.1 18.2 %collective-permute-start.11 = (f32[4,64,256]{2,1,0:T(8,128)S(1)}, f32[4,64,256]{2,1,0:T(8,128)S(1)}, u32[]{:S(2)}, u32[]{:S(2)}) collective-permute-start(f32[4,64,256]{2,1,0:T(8,128)S(1)} %get-tuple-element.65), channel_id=1, source_target_pairs={{1,2},{3,4},{5,6},{2,1},{4,3},{6,5},{9,10},{11,12},{13,14},{10,9},... | collective-permute-start | bytes 786440 | tf_op jit(solution)/shard_map/ppermute | solution.py:329
  54.3 20.6 %collective-permute-start.4 = (f32[4,64,256]{2,1,0:T(8,128)S(1)}, f32[4,64,256]{2,1,0:T(8,128)S(1)}, u32[]{:S(2)}, u32[]{:S(2)}) collective-permute-start(f32[4,64,256]{2,1,0:T(8,128)S(1)} %get-tuple-element.54), channel_id=1, source_target_pairs={{0,1},{1,0},{2,3},{3,2},{4,5},{5,4},{6,7},{7,6},{8,9},{9,8},{10,11... | collective-permute-start | bytes 786440 | tf_op jit(solution)/shard_map/ppermute | solution.py:328
  58.2 16.8 %collective-permute-start.5 = (f32[4,64,256]{2,1,0:T(8,128)S(1)}, f32[4,64,256]{2,1,0:T(8,128)S(1)}, u32[]{:S(2)}, u32[]{:S(2)}) collective-permute-start(f32[4,64,256]{2,1,0:T(8,128)S(1)} %get-tuple-element.55), channel_id=1, source_target_pairs={{1,2},{3,4},{5,6},{2,1},{4,3},{6,5},{9,10},{11,12},{13,14},{10,9},... | collective-permute-start | bytes 786440 | tf_op jit(solution)/shard_map/ppermute | solution.py:329
  71.0 17.1 %collective-permute-start.18 = (f32[4,64,256]{2,1,0:T(8,128)S(1)}, f32[4,64,256]{2,1,0:T(8,128)S(1)}, u32[]{:S(2)}, u32[]{:S(2)}) collective-permute-start(f32[4,64,256]{2,1,0:T(8,128)S(1)} %get-tuple-element.76), channel_id=1, source_target_pairs={{0,1},{1,0},{2,3},{3,2},{4,5},{5,4},{6,7},{7,6},{8,9},{9,8},{10,11... | collective-permute-start | bytes 786440 | tf_op jit(solution)/shard_map/ppermute | solution.py:328
  73.6 14.6 %collective-permute-start.19 = (f32[4,64,256]{2,1,0:T(8,128)S(1)}, f32[4,64,256]{2,1,0:T(8,128)S(1)}, u32[]{:S(2)}, u32[]{:S(2)}) collective-permute-start(f32[4,64,256]{2,1,0:T(8,128)S(1)} %get-tuple-element.77), channel_id=1, source_target_pairs={{1,2},{3,4},{5,6},{2,1},{4,3},{6,5},{9,10},{11,12},{13,14},{10,9},... | collective-permute-start | bytes 786440 | tf_op jit(solution)/shard_map/ppermute | solution.py:329
  77.7 1.3 %collective-permute-start.15 = (f32[1,64,256]{2,1,0:T(8,128)S(1)}, f32[1,64,256]{2,1,0:T(8,128)S(1)}, u32[]{:S(2)}, u32[]{:S(2)}) collective-permute-start(f32[1,64,256]{2,1,0:T(8,128)S(1)} %get-tuple-element.91), channel_id=1, source_target_pairs={{0,8},{8,0},{16,24},{24,16},{1,9},{9,1},{17,25},{25,17},{2,10},{10... | collective-permute-start | bytes 196616 | tf_op jit(solution)/shard_map/ppermute | solution.py:350
  77.8 1.4 %collective-permute-start.14 = (f32[1,64,256]{2,1,0:T(8,128)S(1)}, f32[1,64,256]{2,1,0:T(8,128)S(1)}, u32[]{:S(2)}, u32[]{:S(2)}) collective-permute-start(f32[1,64,256]{2,1,0:T(8,128)S(1)} %get-tuple-element.92), channel_id=1, source_target_pairs={{0,8},{8,0},{16,24},{24,16},{1,9},{9,1},{17,25},{25,17},{2,10},{10... | collective-permute-start | bytes 196616 | tf_op jit(solution)/shard_map/ppermute | solution.py:350
  80.3 10.1 %collective-permute-start.20 = (f32[4,64,256]{2,1,0:T(8,128)S(1)}, f32[4,64,256]{2,1,0:T(8,128)S(1)}, u32[]{:S(2)}, u32[]{:S(2)}) collective-permute-start(f32[4,64,256]{2,1,0:T(8,128)S(1)} %shard_map.129.refs_7_.a), channel_id=1, source_target_pairs={{0,16},{8,24},{16,0},{24,8},{1,17},{9,25},{17,1},{25,9},{2,18},{10... | collective-permute-start | bytes 786440 | tf_op jit(solution)/shard_map/ppermute | solution.py:357
  83.8 14.9 %collective-permute-start.16 = (f32[4,64,256]{2,1,0:T(8,128)S(1)}, f32[4,64,256]{2,1,0:T(8,128)S(1)}, u32[]{:S(2)}, u32[]{:S(2)}) collective-permute-start(f32[4,64,256]{2,1,0:T(8,128)S(1)} %get-tuple-element.74), channel_id=1, source_target_pairs={{0,1},{1,0},{2,3},{3,2},{4,5},{5,4},{6,7},{7,6},{8,9},{9,8},{10,11... | collective-permute-start | bytes 786440 | tf_op jit(solution)/shard_map/ppermute | solution.py:328
  87.5 11.2 %collective-permute-start.17 = (f32[4,64,256]{2,1,0:T(8,128)S(1)}, f32[4,64,256]{2,1,0:T(8,128)S(1)}, u32[]{:S(2)}, u32[]{:S(2)}) collective-permute-start(f32[4,64,256]{2,1,0:T(8,128)S(1)} %get-tuple-element.75), channel_id=1, source_target_pairs={{1,2},{3,4},{5,6},{2,1},{4,3},{6,5},{9,10},{11,12},{13,14},{10,9},... | collective-permute-start | bytes 786440 | tf_op jit(solution)/shard_map/ppermute | solution.py:329
  89.9 1.4 %collective-permute-start.23 = (f32[2,64,256]{2,1,0:T(8,128)S(1)}, f32[2,64,256]{2,1,0:T(8,128)S(1)}, u32[]{:S(2)}, u32[]{:S(2)}) collective-permute-start(f32[2,64,256]{2,1,0:T(8,128)S(1)} %get-tuple-element.89), channel_id=1, source_target_pairs={{0,8},{8,0},{16,24},{24,16},{1,9},{9,1},{17,25},{25,17},{2,10},{10... | collective-permute-start | bytes 393224 | tf_op jit(solution)/shard_map/ppermute | solution.py:350
  90.0 1.5 %collective-permute-start.22 = (f32[2,64,256]{2,1,0:T(8,128)S(1)}, f32[2,64,256]{2,1,0:T(8,128)S(1)}, u32[]{:S(2)}, u32[]{:S(2)}) collective-permute-start(f32[2,64,256]{2,1,0:T(8,128)S(1)} %get-tuple-element.90), channel_id=1, source_target_pairs={{0,8},{8,0},{16,24},{24,16},{1,9},{9,1},{17,25},{25,17},{2,10},{10... | collective-permute-start | bytes 393224 | tf_op jit(solution)/shard_map/ppermute | solution.py:350
  91.5 9.2 %collective-permute-start.24 = (f32[4,64,256]{2,1,0:T(8,128)S(1)}, f32[4,64,256]{2,1,0:T(8,128)S(1)}, u32[]{:S(2)}, u32[]{:S(2)}) collective-permute-start(f32[4,64,256]{2,1,0:T(8,128)S(1)} %shard_map.134.a), channel_id=1, source_target_pairs={{0,16},{8,24},{16,0},{24,8},{1,17},{9,25},{17,1},{25,9},{2,18},{10... | collective-permute-start | bytes 786440 | tf_op jit(solution)/shard_map/ppermute | solution.py:357
  100.7 1.6 %collective-permute-start.21 = (f32[4,64,256]{2,1,0:T(8,128)S(1)}, f32[4,64,256]{2,1,0:T(8,128)S(1)}, u32[]{:S(2)}, u32[]{:S(2)}) collective-permute-start(f32[4,64,256]{2,1,0:T(8,128)S(1)} %shard_map.133.inner_kept), channel_id=1, source_target_pairs={{0,8},{8,0},{16,24},{24,16},{1,9},{9,1},{17,25},{25,17},{2,10},{10... | collective-permute-start | bytes 786440 | tf_op jit(solution)/shard_map/ppermute | solution.py:369
  100.8 1.8 %collective-permute-start.25 = (f32[4,64,256]{2,1,0:T(8,128)S(1)}, f32[4,64,256]{2,1,0:T(8,128)S(1)}, u32[]{:S(2)}, u32[]{:S(2)}) collective-permute-start(f32[4,64,256]{2,1,0:T(8,128)S(1)} %shard_map.135.kept), channel_id=1, source_target_pairs={{0,8},{8,0},{16,24},{24,16},{1,9},{9,1},{17,25},{25,17},{2,10},{10... | collective-permute-start | bytes 786440 | tf_op jit(solution)/shard_map/ppermute | solution.py:369
  (7 other events, 57.5 us)

commit v4 on v3

--- a/solution.py
+++ b/solution.py
@@ -173,7 +173,7 @@
 
 
 def forward_kernel(step, source, wavelet, *refs):
-    current, previous, near, far, rate, _, upcoming, lap, near_edge, far_edge, ext = refs
+    current, previous, far, near, rate, _, upcoming, lap, near_edge, far_edge, ext = refs
     planes = current.shape[0]
     place(ext, near, far)
     ext[pl.ds(halo, planes)] = current[...]
@@ -237,7 +237,7 @@
 
 
 def forward_outer_kernel(step, source, wavelet, *refs):
-    current, previous, near, far, rate, rest, a5, keep, send, outer, ext, grad = refs
+    current, previous, far, near, rate, rest, a5, keep, send, outer, ext, grad = refs
     planes = current.shape[0]
     place(ext, near, far)
     ext[pl.ds(halo, planes)] = current[...]
@@ -257,6 +257,8 @@
      first_adjoint, final, near_edge, far_edge, ext, stage, sems) = refs
     planes = current.shape[0]
     within = pl.ds(halo, planes - 2 * halo)
+    near_edge[...] = near_in[...]
+    far_edge[...] = far_in[...]
     wave_copy = pltpu.make_async_copy(inner, final.at[within], sems.at[0])
     wave_copy.start()
     ext[...] = rate[...] * current[...]
@@ -269,51 +271,49 @@
         )
     copy = pltpu.make_async_copy(stage, first_adjoint.at[within], sems.at[1])
     copy.start()
-    near_edge[...] = near_in[...]
-    far_edge[...] = far_in[...]
     wave_copy.wait()
     copy.wait()
 
 
 def adjoint_outer_kernel(step, *refs):
-    (current, later, near, far, rate, injected, outer, _, _,
-     first_adjoint, final, token, ext, stage, sems) = refs
+    (current, later, near, far, rate, injected, outer_wave, _,
+     outer, final, ext, sems) = refs
     planes = current.shape[0]
     copies = []
     for side, first in enumerate((0, planes - halo)):
-        here = pl.ds(first, halo)
-        copies.append(pltpu.make_async_copy(outer.at[side], final.at[here], sems.at[side]))
-        copies[-1].start()
+        copies.append(
+            pltpu.make_async_copy(
+                outer_wave.at[side], final.at[pl.ds(first, halo)], sems.at[side]
+            )
+        )
+        copies[side].start()
     place(ext, near, far)
     ext[pl.ds(halo, planes)] = rate[...] * current[...]
     along_y, along_z = bands(current)
     for side, first in enumerate((0, planes - halo)):
         here = pl.ds(first, halo)
         value = laplacian(ext, first + halo, along_y, along_z)
-        stage[side] = 2.0 * current[here] - later[here] + value + injected[step, here]
-        copies.append(
-            pltpu.make_async_copy(stage.at[side], first_adjoint.at[here], sems.at[2 + side])
-        )
-        copies[-1].start()
-    token[...] = jnp.zeros_like(token)
+        outer[side] = 2.0 * current[here] - later[here] + value + injected[step, here]
     for copy in copies:
         copy.wait()
 
 
-def assemble_kernel(inner_kept, inner_got, kept, got, total, sems):
+def finish_kernel(inner_kept, inner_got, kept, got, outer, _, first_adjoint, total, sems):
     planes = total.shape[0]
     half = inner_kept.shape[0]
     mine = core() * half
     side = core() * (planes - halo)
     spots = (
-        (inner_kept, halo + mine, half),
-        (inner_got, halo + half - mine, half),
-        (kept, side, halo),
-        (got, planes - halo - side, halo),
+        (inner_kept, total, halo + mine, half),
+        (inner_got, total, halo + half - mine, half),
+        (kept, total, side, halo),
+        (got, total, planes - halo - side, halo),
+        (outer.at[0], first_adjoint, 0, halo),
+        (outer.at[1], first_adjoint, planes - halo, halo),
     )
     copies = []
-    for n, (piece, at, count) in enumerate(spots):
-        copies.append(pltpu.make_async_copy(piece, total.at[pl.ds(at, count)], sems.at[n]))
+    for n, (piece, target, at, count) in enumerate(spots):
+        copies.append(pltpu.make_async_copy(piece, target.at[pl.ds(at, count)], sems.at[n]))
         copies[n].start()
     for copy in copies:
         copy.wait()
@@ -324,10 +324,8 @@
     near_pairs = [(i, i ^ 1) for i in range(count) if i ^ 1 < count]
     far_pairs = [(i, i + 1) for i in range(1, count - 1, 2)]
     far_pairs = far_pairs + [(b, a) for a, b in far_pairs]
-    return (
-        lax.ppermute(near_edge, "dom", near_pairs),
-        lax.ppermute(far_edge, "dom", far_pairs),
-    )
+    far = lax.ppermute(far_edge, "dom", far_pairs)
+    return lax.ppermute(near_edge, "dom", near_pairs), far
 
 
 def parts_kernel(keep, *refs):
@@ -426,7 +424,7 @@
     for n in range(steps - 1):
         upcoming, lap, near_edge, far_edge = call(
             functools.partial(forward_kernel, n),
-            (source_index, wavelet, current, previous, *u_halo, rate, injected),
+            (source_index, wavelet, current, previous, *u_halo[::-1], rate, injected),
             [vmem] * 7 + [wherever],
             [block, block, edge, edge],
             [ext],
@@ -467,29 +465,30 @@
     a_halo = swap(near_edge, far_edge)
     keep, send, outer_wave = call(
         functools.partial(forward_outer_kernel, steps - 1),
-        (source_index, wavelet, current, previous, *u_halo, rate, rest, a5),
+        (source_index, wavelet, current, previous, *u_halo[::-1], rate, rest, a5),
         [vmem] * 9,
         [edge, edge, pair],
         [ext, outer],
     )
     outer_sum = first_sum(keep, send, inner_sum[1], 2)
-    first_adjoint, final, token = call(
+    last_outer, final = call(
         functools.partial(adjoint_outer_kernel, 0),
-        (adjoint, later, *a_halo, rate, injected, outer_wave, first_adjoint, final),
-        [vmem] * 7 + [hbm] * 2,
-        [(whole, hbm), (whole, hbm), (f32(8, 128), vmem)],
-        [ext, outer, pltpu.SemaphoreType.DMA((4,))],
-        {7: 0, 8: 1},
+        (adjoint, later, *a_halo, rate, injected, outer_wave, final),
+        [vmem] * 7 + [hbm],
+        [pair, (whole, hbm)],
+        [ext, pltpu.SemaphoreType.DMA((2,))],
+        {7: 1},
         cost=2000000000,
     )
-    inner_kept, inner_got = second_sum(*inner_sum, token)
-    kept, got = second_sum(*outer_sum, token)
-    (total,) = call(
-        assemble_kernel,
-        (inner_kept, inner_got, kept, got),
-        [vmem] * 4,
-        [(whole, hbm)],
-        [pltpu.SemaphoreType.DMA((4,))],
+    inner_kept, inner_got = second_sum(*inner_sum, last_outer)
+    kept, got = second_sum(*outer_sum, last_outer)
+    first_adjoint, total = call(
+        finish_kernel,
+        (inner_kept, inner_got, kept, got, last_outer, first_adjoint),
+        [vmem] * 5 + [hbm],
+        [(whole, hbm), (whole, hbm)],
+        [pltpu.SemaphoreType.DMA((6,))],
+        {5: 0},
     )
     return (final[None], first_adjoint[None], total)
 

time: 105 us -> 102 us (0.971)
  waiting for transfers between devices: 38.8 us -> 37.2 us
    ppermute x16, waiting for transfers between devices: 34.7 us -> 33.1 us  [the longest x8 33.1 us: swap(): return (lax.ppermute(near_edge, 'dom', near_pairs), far)]
    ppermute x16, starting transfers between devices: 30.3 us -> 29.2 us  [the longest x8 23.7 us: swap(): return (lax.ppermute(near_edge, 'dom', near_pairs), far)]
  transfers between devices with their start and end apart: 26 -> 26, of which waited for: 14 -> 13; matrix products, arithmetic and copies ran while one was open for 0% -> 0% of each run, Pallas kernels for 26% -> 26%
where the time goes in v4:
time: 102 us
  waiting for transfers between devices  37.2 us (36%)
  starting transfers between devices  34.4 us (34%)
  Pallas kernels  27.4 us (27%)
  local copies, waits for them, and re-layouts  1.78 us (2%)
  between operations  1.07 us (1%)
    ppermute x8, waiting for transfers between devices, swap(): return (lax.ppermute(near_edge, 'dom', near_pairs), far)  33.1 us
    pallas_call x16, Pallas kernels, call(): pl.pallas_call(kernel, out_shape=[pltpu.VMEM(shape.shape, shape.dtype) if...  27.4 us
    ppermute x8, starting transfers between devices, swap(): return (lax.ppermute(near_edge, 'dom', near_pairs), far)  23.7 us
    ppermute x8, starting transfers between devices, swap(): far = lax.ppermute(far_edge, 'dom', far_pairs)  5.55 us
    ppermute x2, starting transfers between devices, first_sum(): return (kept, lax.ppermute(kept, 'shot', across))  3.17 us
    ppermute x6, waiting for transfers between devices, first_sum(): lax.ppermute(send[n * size:(n + 1) * size], 'shot', pairs)  2.11 us
  transfers between devices with their start and end apart: 26, of which 13 were waited for; matrix products, arithmetic and copies ran while one was open for 0% of the time, Pallas kernels for 26%

profile of v4, /device:TPU:0, one launch (start us, length us, event | category | flops | bytes accessed | tf_op | source)
XLA Modules:
  0.0 101.8 jit_solution(1914968662408543546)
XLA Ops:
  0.7 1.1 %dynamic-slice_bitcast_fusion = (f32[4,64,256]{2,1,0:T(8,128)S(1)}, f32[4,64,256]{2,1,0:T(8,128)S(1)}) fusion(f32[1,16,64,256]{3,2,1,0:T(8,128)} %param.11, s32[]{:T(128)S(6)} %select_n.16, s32[]{:T(128)S(6)} %select_n.17), kind=kLoop, calls=%fused_computation | loop fusion | bytes 1048584 | tf_op jit(solution)/shard_map/dynamic_slice | solution.py:401
  1.7 3.0 %collective-permute-start.7 = (f32[4,64,256]{2,1,0:T(8,128)S(1)}, f32[4,64,256]{2,1,0:T(8,128)S(1)}, u32[]{:S(2)}, u32[]{:S(2)}) collective-permute-start(f32[4,64,256]{2,1,0:T(8,128)S(1)} %get-tuple-element.89), channel_id=1, source_target_pairs={{0,1},{1,0},{2,3},{3,2},{4,5},{5,4},{6,7},{7,6},{8,9},{9,8},{10,11... | collective-permute-start | bytes 786440 | tf_op jit(solution)/shard_map/ppermute | solution.py:328
  6.1 2.6 %shard_map.121 = (f32[16,64,256]{2,1,0:T(8,128)S(1)}, f32[4,64,256]{2,1,0:T(8,128)S(1)}, f32[4,64,256]{2,1,0:T(8,128)S(1)}, f32[16,64,256]{2,1,0:T(8,128)S(1)}, ...) custom-call(f32[8]{0:T(128)S(1)} %copy-done.3, s32[16,64,256]{2,1,0:T(8,128)} %labels.1, ...), custom_call_target="tpu_custom_call" | custom-call | flops 1024 | bytes 1024 | tf_op jit(solution)/shard_map/pallas_call | solution.py:22
  8.7 4.3 %collective-permute-start = (f32[4,64,256]{2,1,0:T(8,128)S(1)}, f32[4,64,256]{2,1,0:T(8,128)S(1)}, u32[]{:S(2)}, u32[]{:S(2)}) collective-permute-start(f32[4,64,256]{2,1,0:T(8,128)S(1)} %get-tuple-element.48), channel_id=1, source_target_pairs={{0,1},{1,0},{2,3},{3,2},{4,5},{5,4},{6,7},{7,6},{8,9},{9,8},{10,11... | collective-permute-start | bytes 786440 | tf_op jit(solution)/shard_map/ppermute | solution.py:328
  13.8 6.7 %shard_map.122.refs_5_.refs_3_ = f32[4,16,64,256]{3,2,1,0:T(8,128)S(1)} custom-call(s32[3,1024]{1,0:T(4,128)S(1)} %bitcast.16, f32[4,1024]{1,0:T(4,128)S(1)} %bitcast.17, f32[16,64,256]{2,1,0:T(8,128)S(1)} %get-tuple-element.50._.refs_4_.refs_2_), custom_call_target="tpu_custom_call" | custom-call | flops 1024 | bytes 1024 | tf_op jit(solution)/shard_map/pallas_call | solution.py:22
  20.5 2.2 %collective-permute-done.7.refs_3_ = f32[4,64,256]{2,1,0:T(8,128)S(1)} collective-permute-done((f32[4,64,256]{2,1,0:T(8,128)S(1)}, f32[4,64,256]{2,1,0:T(8,128)S(1)}, u32[]{:S(2)}, u32[]{:S(2)}) %collective-permute-start.7) | collective-permute-done | bytes 262176 | tf_op jit(solution)/shard_map/ppermute | solution.py:328
  22.7 1.8 %shard_map.125 = (f32[16,64,256]{2,1,0:T(8,128)S(1)}, f32[16,64,256]{2,1,0:T(8,128)S(1)}, f32[4,64,256]{2,1,0:T(8,128)S(1)}, f32[4,64,256]{2,1,0:T(8,128)S(1)}) custom-call(s32[1,3]{1,0:T(1,128)S(1)} %copy-done.1, f32[1,4]{1,0:T(1,128)S(1)} %copy-done.2, f32[16,64,256]{2,1,0:T(8,128)S(1)} %get-tuple-element.57.refs_0_.refs_1_, ...), custom_call_target="tpu_custom_call" | custom-call | flops 1024 | bytes 1024 | tf_op jit(solution)/shard_map/pallas_call | solution.py:22
  25.2 5.3 %collective-permute-start.9 = (f32[4,64,256]{2,1,0:T(8,128)S(1)}, f32[4,64,256]{2,1,0:T(8,128)S(1)}, u32[]{:S(2)}, u32[]{:S(2)}) collective-permute-start(f32[4,64,256]{2,1,0:T(8,128)S(1)} %get-tuple-element.62), channel_id=1, source_target_pairs={{0,1},{1,0},{2,3},{3,2},{4,5},{5,4},{6,7},{7,6},{8,9},{9,8},{10,11... | collective-permute-start | bytes 786440 | tf_op jit(solution)/shard_map/ppermute | solution.py:328
  30.5 1.9 %shard_map.123 = (f32[16,64,256]{2,1,0:T(8,128)S(1)}, f32[4,64,256]{2,1,0:T(8,128)S(1)}, f32[4,64,256]{2,1,0:T(8,128)S(1)}) custom-call(f32[16,64,256]{2,1,0:T(8,128)S(1)} %get-tuple-element.46.refs_0_.refs_1_.refs_11_.refs_6_, f32[16,64,256]{2,1,0:T(8,128)S(1)} %get-tuple-element.47.refs_1_, f32[4,64,256]{2,1,0:T(8,128)S(1)} %collective-permute-done.refs_2_, ...), custom_call_target="tpu_custom_call" | custom-call | flops 1024 | bytes 1024 | tf_op jit(solution)/shard_map/pallas_call | solution.py:22
  33.2 12.0 %collective-permute-done.9.refs_3_ = f32[4,64,256]{2,1,0:T(8,128)S(1)} collective-permute-done((f32[4,64,256]{2,1,0:T(8,128)S(1)}, f32[4,64,256]{2,1,0:T(8,128)S(1)}, u32[]{:S(2)}, u32[]{:S(2)}) %collective-permute-start.9) | collective-permute-done | bytes 262176 | tf_op jit(solution)/shard_map/ppermute | solution.py:328
  45.2 1.7 %shard_map.126 = (f32[16,64,256]{2,1,0:T(8,128)S(1)}, f32[16,64,256]{2,1,0:T(8,128)S(1)}, f32[4,64,256]{2,1,0:T(8,128)S(1)}, f32[4,64,256]{2,1,0:T(8,128)S(1)}) custom-call(s32[1,3]{1,0:T(1,128)S(1)} %copy-done.1, f32[1,4]{1,0:T(1,128)S(1)} %copy-done.2, f32[16,64,256]{2,1,0:T(8,128)S(1)} %get-tuple-element.60.refs_0_.refs_1_, ...), custom_call_target="tpu_custom_call" | custom-call | flops 1024 | bytes 1024 | tf_op jit(solution)/shard_map/pallas_call | solution.py:22
  47.8 5.2 %collective-permute-start.11 = (f32[4,64,256]{2,1,0:T(8,128)S(1)}, f32[4,64,256]{2,1,0:T(8,128)S(1)}, u32[]{:S(2)}, u32[]{:S(2)}) collective-permute-start(f32[4,64,256]{2,1,0:T(8,128)S(1)} %get-tuple-element.66), channel_id=1, source_target_pairs={{0,1},{1,0},{2,3},{3,2},{4,5},{5,4},{6,7},{7,6},{8,9},{9,8},{10,11... | collective-permute-start | bytes 786440 | tf_op jit(solution)/shard_map/ppermute | solution.py:328
  53.0 1.8 %shard_map.124 = (f32[16,64,256]{2,1,0:T(8,128)S(1)}, f32[4,64,256]{2,1,0:T(8,128)S(1)}, f32[4,64,256]{2,1,0:T(8,128)S(1)}) custom-call(f32[16,64,256]{2,1,0:T(8,128)S(1)} %get-tuple-element.51.refs_0_.refs_1_, f32[16,64,256]{2,1,0:T(8,128)S(1)} %get-tuple-element.46.refs_0_.refs_1_.refs_11_.refs_6_, f32[4,64,256]{2,1,0:T(8,128)S(1)} %collective-permute-done.2.refs_2_, ...), custom_call_target="tpu_custom_call" | custom-call | flops 1024 | bytes 1024 | tf_op jit(solution)/shard_map/pallas_call | solution.py:22
  55.6 11.9 %collective-permute-done.11.refs_3_ = f32[4,64,256]{2,1,0:T(8,128)S(1)} collective-permute-done((f32[4,64,256]{2,1,0:T(8,128)S(1)}, f32[4,64,256]{2,1,0:T(8,128)S(1)}, u32[]{:S(2)}, u32[]{:S(2)}) %collective-permute-start.11) | collective-permute-done | bytes 262176 | tf_op jit(solution)/shard_map/ppermute | solution.py:328
  67.5 1.7 %shard_map.127 = (f32[16,64,256]{2,1,0:T(8,128)S(1)}, f32[16,64,256]{2,1,0:T(8,128)S(1)}, f32[4,64,256]{2,1,0:T(8,128)S(1)}, f32[4,64,256]{2,1,0:T(8,128)S(1)}) custom-call(s32[1,3]{1,0:T(1,128)S(1)} %copy-done.1, f32[1,4]{1,0:T(1,128)S(1)} %copy-done.2, f32[16,64,256]{2,1,0:T(8,128)S(1)} %get-tuple-element.64.refs_0_.refs_10_.refs_1_, ...), custom_call_target="tpu_custom_call" | custom-call | flops 1024 | bytes 1024 | tf_op jit(solution)/shard_map/pallas_call | solution.py:22
  69.9 5.1 %collective-permute-start.19 = (f32[4,64,256]{2,1,0:T(8,128)S(1)}, f32[4,64,256]{2,1,0:T(8,128)S(1)}, u32[]{:S(2)}, u32[]{:S(2)}) collective-permute-start(f32[4,64,256]{2,1,0:T(8,128)S(1)} %get-tuple-element.78), channel_id=1, source_target_pairs={{0,1},{1,0},{2,3},{3,2},{4,5},{5,4},{6,7},{7,6},{8,9},{9,8},{10,11... | collective-permute-start | bytes 786440 | tf_op jit(solution)/shard_map/ppermute | solution.py:328
  75.0 2.7 %shard_map.128 = (f32[16,64,256]{2,1,0:T(8,128)S(1)}, f32[4,64,256]{2,1,0:T(8,128)S(1)}, f32[4,64,256]{2,1,0:T(8,128)S(1)}, f32[2,4,64,256]{3,2,1,0:T(8,128)S(1)...) custom-call(s32[1,3]{1,0:T(1,128)S(1)} %copy-done.1, f32[1,4]{1,0:T(1,128)S(1)} %copy-done.2, ...), custom_call_target="tpu_custom_call" | custom-call | flops 1024 | bytes 1024 | tf_op jit(solution)/shard_map/pallas_call | solution.py:22
  80.4 1.6 %collective-permute-start.20 = (f32[4,64,256]{2,1,0:T(8,128)S(1)}, f32[4,64,256]{2,1,0:T(8,128)S(1)}, u32[]{:S(2)}, u32[]{:S(2)}) collective-permute-start(f32[4,64,256]{2,1,0:T(8,128)S(1)} %shard_map.129.refs_7_.a), channel_id=1, source_target_pairs={{0,16},{8,24},{16,0},{24,8},{1,17},{9,25},{17,1},{25,9},{2,18},{10... | collective-permute-start | bytes 786440 | tf_op jit(solution)/shard_map/ppermute | solution.py:355
  82.0 1.9 %shard_map.130 = (f32[16,64,256]{2,1,0:T(8,128)}, f32[16,64,256]{2,1,0:T(8,128)}, f32[4,64,256]{2,1,0:T(8,128)S(1)}, f32[4,64,256]{2,1,0:T(8,128)S(1)}) custom-call(f32[16,64,256]{2,1,0:T(8,128)S(1)} %get-tuple-element.69.refs_0_, f32[16,64,256]{2,1,0:T(8,128)S(1)} %get-tuple-element.54.refs_0_.refs_1_, ...), custom_call_target="tpu_custom_call" | custom-call | flops 1024 | bytes 1024 | tf_op jit(solution)/shard_map/pallas_call | solution.py:22
  85.8 1.7 %shard_map.131 = (f32[4,64,256]{2,1,0:T(8,128)S(1)}, f32[4,64,256]{2,1,0:T(8,128)S(1)}, f32[2,4,64,256]{3,2,1,0:T(8,128)S(1)}) custom-call(s32[1,3]{1,0:T(1,128)S(1)} %copy-done.1, f32[1,4]{1,0:T(1,128)S(1)} %copy-done.2, f32[16,64,256]{2,1,0:T(8,128)S(1)} %get-tuple-element.68.refs_9_.refs_0_, ...), custom_call_target="tpu_custom_call" | custom-call | flops 1024 | bytes 1024 | tf_op jit(solution)/shard_map/pallas_call | solution.py:22
  89.2 1.6 %collective-permute-start.24 = (f32[4,64,256]{2,1,0:T(8,128)S(1)}, f32[4,64,256]{2,1,0:T(8,128)S(1)}, u32[]{:S(2)}, u32[]{:S(2)}) collective-permute-start(f32[4,64,256]{2,1,0:T(8,128)S(1)} %shard_map.134.a), channel_id=1, source_target_pairs={{0,16},{8,24},{16,0},{24,8},{1,17},{9,25},{17,1},{25,9},{2,18},{10... | collective-permute-start | bytes 786440 | tf_op jit(solution)/shard_map/ppermute | solution.py:355
  90.8 6.2 %collective-permute-done.16.refs_2_ = f32[4,64,256]{2,1,0:T(8,128)S(1)} collective-permute-done((f32[4,64,256]{2,1,0:T(8,128)S(1)}, f32[4,64,256]{2,1,0:T(8,128)S(1)}, u32[]{:S(2)}, u32[]{:S(2)}) %collective-permute-start.16) | collective-permute-done | bytes 262176 | tf_op jit(solution)/shard_map/ppermute | solution.py:328
  97.0 1.5 %shard_map.132 = (f32[2,4,64,256]{3,2,1,0:T(8,128)S(1)}, f32[16,64,256]{2,1,0:T(8,128)}) custom-call(f32[16,64,256]{2,1,0:T(8,128)S(1)} %get-tuple-element.69.refs_0_, f32[16,64,256]{2,1,0:T(8,128)S(1)} %get-tuple-element.54.refs_0_.refs_1_, f32[4,64,256]{2,1,0:T(8,128)S(1)} %collective-permute-done.16.refs_2_, ...), custom_call_target="tpu_custom_call", output_to_operand_aliasing={{1}: (7, {})} | custom-call | flops 2000000000 | bytes 1024 | tf_op jit(solution)/shard_map/pallas_call | solution.py:22
  100.5 1.2 %shard_map.136 = (f32[16,64,256]{2,1,0:T(8,128)}, f32[16,64,256]{2,1,0:T(8,128)}) custom-call(f32[4,64,256]{2,1,0:T(8,128)S(1)} %shard_map.133.inner_kept, f32[4,64,256]{2,1,0:T(8,128)S(1)} %collective-permute-done.21.inner_got, f32[4,64,256]{2,1,0:T(8,128)S(1)} %shard_map.135.kept, ...), custom_call_target="tpu_custom_call", output_to_operand_aliasing={{0}: (5, {})} | custom-call | flops 1024 | bytes 1024 | tf_op jit(solution)/shard_map/pallas_call | solution.py:22
  (58 shorter events, 14.0 us)
Async XLA Ops:
  1.7 21.0 %collective-permute-start.7 = (f32[4,64,256]{2,1,0:T(8,128)S(1)}, f32[4,64,256]{2,1,0:T(8,128)S(1)}, u32[]{:S(2)}, u32[]{:S(2)}) collective-permute-start(f32[4,64,256]{2,1,0:T(8,128)S(1)} %get-tuple-element.89), channel_id=1, source_target_pairs={{0,1},{1,0},{2,3},{3,2},{4,5},{5,4},{6,7},{7,6},{8,9},{9,8},{10,11... | collective-permute-start | bytes 786440 | tf_op jit(solution)/shard_map/ppermute | solution.py:328
  4.7 17.9 %collective-permute-start.6 = (f32[4,64,256]{2,1,0:T(8,128)S(1)}, f32[4,64,256]{2,1,0:T(8,128)S(1)}, u32[]{:S(2)}, u32[]{:S(2)}) collective-permute-start(f32[4,64,256]{2,1,0:T(8,128)S(1)} %get-tuple-element.90), channel_id=1, source_target_pairs={{1,2},{3,4},{5,6},{2,1},{4,3},{6,5},{9,10},{11,12},{13,14},{10,9},... | collective-permute-start | bytes 786440 | tf_op jit(solution)/shard_map/ppermute | solution.py:327
  8.7 21.8 %collective-permute-start = (f32[4,64,256]{2,1,0:T(8,128)S(1)}, f32[4,64,256]{2,1,0:T(8,128)S(1)}, u32[]{:S(2)}, u32[]{:S(2)}) collective-permute-start(f32[4,64,256]{2,1,0:T(8,128)S(1)} %get-tuple-element.48), channel_id=1, source_target_pairs={{0,1},{1,0},{2,3},{3,2},{4,5},{5,4},{6,7},{7,6},{8,9},{9,8},{10,11... | collective-permute-start | bytes 786440 | tf_op jit(solution)/shard_map/ppermute | solution.py:328
  13.1 17.5 %collective-permute-start.1 = (f32[4,64,256]{2,1,0:T(8,128)S(1)}, f32[4,64,256]{2,1,0:T(8,128)S(1)}, u32[]{:S(2)}, u32[]{:S(2)}) collective-permute-start(f32[4,64,256]{2,1,0:T(8,128)S(1)} %get-tuple-element.49), channel_id=1, source_target_pairs={{1,2},{3,4},{5,6},{2,1},{4,3},{6,5},{9,10},{11,12},{13,14},{10,9},... | collective-permute-start | bytes 786440 | tf_op jit(solution)/shard_map/ppermute | solution.py:327
  24.5 8.7 %collective-permute-start.8 = (f32[4,64,256]{2,1,0:T(8,128)S(1)}, f32[4,64,256]{2,1,0:T(8,128)S(1)}, u32[]{:S(2)}, u32[]{:S(2)}) collective-permute-start(f32[4,64,256]{2,1,0:T(8,128)S(1)} %get-tuple-element.61), channel_id=1, source_target_pairs={{1,2},{3,4},{5,6},{2,1},{4,3},{6,5},{9,10},{11,12},{13,14},{10,9},... | collective-permute-start | bytes 786440 | tf_op jit(solution)/shard_map/ppermute | solution.py:327
  25.2 20.1 %collective-permute-start.9 = (f32[4,64,256]{2,1,0:T(8,128)S(1)}, f32[4,64,256]{2,1,0:T(8,128)S(1)}, u32[]{:S(2)}, u32[]{:S(2)}) collective-permute-start(f32[4,64,256]{2,1,0:T(8,128)S(1)} %get-tuple-element.62), channel_id=1, source_target_pairs={{0,1},{1,0},{2,3},{3,2},{4,5},{5,4},{6,7},{7,6},{8,9},{9,8},{10,11... | collective-permute-start | bytes 786440 | tf_op jit(solution)/shard_map/ppermute | solution.py:328
  32.4 20.6 %collective-permute-start.2 = (f32[4,64,256]{2,1,0:T(8,128)S(1)}, f32[4,64,256]{2,1,0:T(8,128)S(1)}, u32[]{:S(2)}, u32[]{:S(2)}) collective-permute-start(f32[4,64,256]{2,1,0:T(8,128)S(1)} %get-tuple-element.52), channel_id=1, source_target_pairs={{0,1},{1,0},{2,3},{3,2},{4,5},{5,4},{6,7},{7,6},{8,9},{9,8},{10,11... | collective-permute-start | bytes 786440 | tf_op jit(solution)/shard_map/ppermute | solution.py:328
  32.5 20.5 %collective-permute-start.3 = (f32[4,64,256]{2,1,0:T(8,128)S(1)}, f32[4,64,256]{2,1,0:T(8,128)S(1)}, u32[]{:S(2)}, u32[]{:S(2)}) collective-permute-start(f32[4,64,256]{2,1,0:T(8,128)S(1)} %get-tuple-element.53), channel_id=1, source_target_pairs={{1,2},{3,4},{5,6},{2,1},{4,3},{6,5},{9,10},{11,12},{13,14},{10,9},... | collective-permute-start | bytes 786440 | tf_op jit(solution)/shard_map/ppermute | solution.py:327
  47.0 8.6 %collective-permute-start.10 = (f32[4,64,256]{2,1,0:T(8,128)S(1)}, f32[4,64,256]{2,1,0:T(8,128)S(1)}, u32[]{:S(2)}, u32[]{:S(2)}) collective-permute-start(f32[4,64,256]{2,1,0:T(8,128)S(1)} %get-tuple-element.65), channel_id=1, source_target_pairs={{1,2},{3,4},{5,6},{2,1},{4,3},{6,5},{9,10},{11,12},{13,14},{10,9},... | collective-permute-start | bytes 786440 | tf_op jit(solution)/shard_map/ppermute | solution.py:327
  47.8 19.7 %collective-permute-start.11 = (f32[4,64,256]{2,1,0:T(8,128)S(1)}, f32[4,64,256]{2,1,0:T(8,128)S(1)}, u32[]{:S(2)}, u32[]{:S(2)}) collective-permute-start(f32[4,64,256]{2,1,0:T(8,128)S(1)} %get-tuple-element.66), channel_id=1, source_target_pairs={{0,1},{1,0},{2,3},{3,2},{4,5},{5,4},{6,7},{7,6},{8,9},{9,8},{10,11... | collective-permute-start | bytes 786440 | tf_op jit(solution)/shard_map/ppermute | solution.py:328
  54.8 20.1 %collective-permute-start.4 = (f32[4,64,256]{2,1,0:T(8,128)S(1)}, f32[4,64,256]{2,1,0:T(8,128)S(1)}, u32[]{:S(2)}, u32[]{:S(2)}) collective-permute-start(f32[4,64,256]{2,1,0:T(8,128)S(1)} %get-tuple-element.55), channel_id=1, source_target_pairs={{0,1},{1,0},{2,3},{3,2},{4,5},{5,4},{6,7},{7,6},{8,9},{9,8},{10,11... | collective-permute-start | bytes 786440 | tf_op jit(solution)/shard_map/ppermute | solution.py:328
  54.9 20.1 %collective-permute-start.5 = (f32[4,64,256]{2,1,0:T(8,128)S(1)}, f32[4,64,256]{2,1,0:T(8,128)S(1)}, u32[]{:S(2)}, u32[]{:S(2)}) collective-permute-start(f32[4,64,256]{2,1,0:T(8,128)S(1)} %get-tuple-element.56), channel_id=1, source_target_pairs={{1,2},{3,4},{5,6},{2,1},{4,3},{6,5},{9,10},{11,12},{13,14},{10,9},... | collective-permute-start | bytes 786440 | tf_op jit(solution)/shard_map/ppermute | solution.py:327
  69.2 15.9 %collective-permute-start.18 = (f32[4,64,256]{2,1,0:T(8,128)S(1)}, f32[4,64,256]{2,1,0:T(8,128)S(1)}, u32[]{:S(2)}, u32[]{:S(2)}) collective-permute-start(f32[4,64,256]{2,1,0:T(8,128)S(1)} %get-tuple-element.77), channel_id=1, source_target_pairs={{1,2},{3,4},{5,6},{2,1},{4,3},{6,5},{9,10},{11,12},{13,14},{10,9},... | collective-permute-start | bytes 786440 | tf_op jit(solution)/shard_map/ppermute | solution.py:327
  69.9 16.0 %collective-permute-start.19 = (f32[4,64,256]{2,1,0:T(8,128)S(1)}, f32[4,64,256]{2,1,0:T(8,128)S(1)}, u32[]{:S(2)}, u32[]{:S(2)}) collective-permute-start(f32[4,64,256]{2,1,0:T(8,128)S(1)} %get-tuple-element.78), channel_id=1, source_target_pairs={{0,1},{1,0},{2,3},{3,2},{4,5},{5,4},{6,7},{7,6},{8,9},{9,8},{10,11... | collective-permute-start | bytes 786440 | tf_op jit(solution)/shard_map/ppermute | solution.py:328
  77.8 1.3 %collective-permute-start.15 = (f32[1,64,256]{2,1,0:T(8,128)S(1)}, f32[1,64,256]{2,1,0:T(8,128)S(1)}, u32[]{:S(2)}, u32[]{:S(2)}) collective-permute-start(f32[1,64,256]{2,1,0:T(8,128)S(1)} %get-tuple-element.93), channel_id=1, source_target_pairs={{0,8},{8,0},{16,24},{24,16},{1,9},{9,1},{17,25},{25,17},{2,10},{10... | collective-permute-start | bytes 196616 | tf_op jit(solution)/shard_map/ppermute | solution.py:348
  77.8 1.4 %collective-permute-start.14 = (f32[1,64,256]{2,1,0:T(8,128)S(1)}, f32[1,64,256]{2,1,0:T(8,128)S(1)}, u32[]{:S(2)}, u32[]{:S(2)}) collective-permute-start(f32[1,64,256]{2,1,0:T(8,128)S(1)} %get-tuple-element.94), channel_id=1, source_target_pairs={{0,8},{8,0},{16,24},{24,16},{1,9},{9,1},{17,25},{25,17},{2,10},{10... | collective-permute-start | bytes 196616 | tf_op jit(solution)/shard_map/ppermute | solution.py:348
  80.4 8.4 %collective-permute-start.20 = (f32[4,64,256]{2,1,0:T(8,128)S(1)}, f32[4,64,256]{2,1,0:T(8,128)S(1)}, u32[]{:S(2)}, u32[]{:S(2)}) collective-permute-start(f32[4,64,256]{2,1,0:T(8,128)S(1)} %shard_map.129.refs_7_.a), channel_id=1, source_target_pairs={{0,16},{8,24},{16,0},{24,8},{1,17},{9,25},{17,1},{25,9},{2,18},{10... | collective-permute-start | bytes 786440 | tf_op jit(solution)/shard_map/ppermute | solution.py:355
  83.8 13.2 %collective-permute-start.16 = (f32[4,64,256]{2,1,0:T(8,128)S(1)}, f32[4,64,256]{2,1,0:T(8,128)S(1)}, u32[]{:S(2)}, u32[]{:S(2)}) collective-permute-start(f32[4,64,256]{2,1,0:T(8,128)S(1)} %get-tuple-element.75), channel_id=1, source_target_pairs={{0,1},{1,0},{2,3},{3,2},{4,5},{5,4},{6,7},{7,6},{8,9},{9,8},{10,11... | collective-permute-start | bytes 786440 | tf_op jit(solution)/shard_map/ppermute | solution.py:328
  84.4 12.6 %collective-permute-start.17 = (f32[4,64,256]{2,1,0:T(8,128)S(1)}, f32[4,64,256]{2,1,0:T(8,128)S(1)}, u32[]{:S(2)}, u32[]{:S(2)}) collective-permute-start(f32[4,64,256]{2,1,0:T(8,128)S(1)} %get-tuple-element.76), channel_id=1, source_target_pairs={{1,2},{3,4},{5,6},{2,1},{4,3},{6,5},{9,10},{11,12},{13,14},{10,9},... | collective-permute-start | bytes 786440 | tf_op jit(solution)/shard_map/ppermute | solution.py:327
  87.6 1.4 %collective-permute-start.23 = (f32[2,64,256]{2,1,0:T(8,128)S(1)}, f32[2,64,256]{2,1,0:T(8,128)S(1)}, u32[]{:S(2)}, u32[]{:S(2)}) collective-permute-start(f32[2,64,256]{2,1,0:T(8,128)S(1)} %get-tuple-element.91), channel_id=1, source_target_pairs={{0,8},{8,0},{16,24},{24,16},{1,9},{9,1},{17,25},{25,17},{2,10},{10... | collective-permute-start | bytes 393224 | tf_op jit(solution)/shard_map/ppermute | solution.py:348
  87.6 1.5 %collective-permute-start.22 = (f32[2,64,256]{2,1,0:T(8,128)S(1)}, f32[2,64,256]{2,1,0:T(8,128)S(1)}, u32[]{:S(2)}, u32[]{:S(2)}) collective-permute-start(f32[2,64,256]{2,1,0:T(8,128)S(1)} %get-tuple-element.92), channel_id=1, source_target_pairs={{0,8},{8,0},{16,24},{24,16},{1,9},{9,1},{17,25},{25,17},{2,10},{10... | collective-permute-start | bytes 393224 | tf_op jit(solution)/shard_map/ppermute | solution.py:348
  89.2 9.4 %collective-permute-start.24 = (f32[4,64,256]{2,1,0:T(8,128)S(1)}, f32[4,64,256]{2,1,0:T(8,128)S(1)}, u32[]{:S(2)}, u32[]{:S(2)}) collective-permute-start(f32[4,64,256]{2,1,0:T(8,128)S(1)} %shard_map.134.a), channel_id=1, source_target_pairs={{0,16},{8,24},{16,0},{24,8},{1,17},{9,25},{17,1},{25,9},{2,18},{10... | collective-permute-start | bytes 786440 | tf_op jit(solution)/shard_map/ppermute | solution.py:355
  98.5 1.6 %collective-permute-start.21 = (f32[4,64,256]{2,1,0:T(8,128)S(1)}, f32[4,64,256]{2,1,0:T(8,128)S(1)}, u32[]{:S(2)}, u32[]{:S(2)}) collective-permute-start(f32[4,64,256]{2,1,0:T(8,128)S(1)} %shard_map.133.inner_kept), channel_id=1, source_target_pairs={{0,8},{8,0},{16,24},{24,16},{1,9},{9,1},{17,25},{25,17},{2,10},{10... | collective-permute-start | bytes 786440 | tf_op jit(solution)/shard_map/ppermute | solution.py:367
  98.6 1.8 %collective-permute-start.25 = (f32[4,64,256]{2,1,0:T(8,128)S(1)}, f32[4,64,256]{2,1,0:T(8,128)S(1)}, u32[]{:S(2)}, u32[]{:S(2)}) collective-permute-start(f32[4,64,256]{2,1,0:T(8,128)S(1)} %shard_map.135.kept), channel_id=1, source_target_pairs={{0,8},{8,0},{16,24},{24,16},{1,9},{9,1},{17,25},{25,17},{2,10},{10... | collective-permute-start | bytes 786440 | tf_op jit(solution)/shard_map/ppermute | solution.py:367
  (7 other events, 62.6 us)

commit v5 on v4

--- a/solution.py
+++ b/solution.py
@@ -63,6 +63,7 @@
 
 def laplacian(field, at, along_y, along_z):
     _, nz, ny = field.shape
+    along_y, along_z = along_y[...], along_z[...]
     centre = field[pl.ds(at, halo)]
     high, middle, low = pieces(centre.reshape(halo * nz, ny))
     across = dot(low, along_y) + dot(along_z, low)
@@ -76,9 +77,20 @@
     return result
 
 
-def bands(field):
-    _, nz, ny = field.shape
-    return band(ny, ny), band(halo * nz, nz)
+def beyond(sides, side):
+    outside = sides[side]
+    result = None
+    for k in range(4, 0, -1):
+        if side == 0:
+            term = outside[halo - k : halo]
+        else:
+            term = outside[:k]
+        term = side_coefs[k - 1] * term
+        if k < halo:
+            empty = jnp.zeros((halo - k,) + outside.shape[1:], jnp.float32)
+            term = jnp.concatenate([term, empty] if side == 0 else [empty, term], axis=0)
+        result = term if result is None else result + term
+    return result
 
 
 def core():
@@ -91,6 +103,20 @@
     spot = jnp.where(odd == 1, 0, planes + halo)
     ext[pl.ds(spot, halo)] = near[...]
     ext[pl.ds(planes + halo - spot, halo)] = far[...]
+
+
+def place_sides(sides, near, far):
+    odd = lax.axis_index("dom") % 2
+    sides[1 - odd] = near[...]
+    sides[odd] = far[...]
+
+
+def alone(ext, block):
+    planes = block.shape[0]
+    empty = jnp.zeros((halo,) + block.shape[1:], jnp.float32)
+    ext[pl.ds(0, halo)] = empty
+    ext[pl.ds(planes + halo, halo)] = empty
+    ext[pl.ds(halo, planes)] = block
 
 
 def edge_spots(planes):
@@ -119,8 +145,8 @@
     table, labels, near_field, *refs
 ):
     sources, refs = refs[:3], refs[3:]
-    rate, near_edge, far_edge, field, *targets = refs[:7]
-    label, sems = refs[7:]
+    rate, near_edge, far_edge, along_y, along_z, field, *targets = refs[:9]
+    label, sems = refs[9:]
     planes = labels.shape[0]
     first = pltpu.make_async_copy(labels, label, sems.at[0])
     second = pltpu.make_async_copy(near_field, field, sems.at[1])
@@ -130,6 +156,9 @@
     for n in range(3):
         others.append(pltpu.make_async_copy(sources[n], targets[n], sems.at[2 + n]))
         others[n].start()
+    _, nz, ny = labels.shape
+    along_y[...] = band(ny, ny)
+    along_z[...] = band(halo * nz, nz)
     first.wait()
     for part in range(planes // halo):
         here = pl.ds(part * halo, halo)
@@ -172,15 +201,16 @@
             injected[step, pl.ds(part * group, group)] = total.reshape(group, nz, ny)
 
 
-def forward_kernel(step, source, wavelet, *refs):
+def forward_kernel(step, *refs):
+    *bands, source, wavelet = refs[:4]
+    refs = refs[4:]
     current, previous, far, near, rate, _, upcoming, lap, near_edge, far_edge, ext = refs
     planes = current.shape[0]
     place(ext, near, far)
     ext[pl.ds(halo, planes)] = current[...]
-    along_y, along_z = bands(current)
     for first in range(0, planes, halo):
         here = pl.ds(first, halo)
-        value = laplacian(ext, first + halo, along_y, along_z)
+        value = laplacian(ext, first + halo, *bands)
         lap[here] = value
         upcoming[here] = 2.0 * current[here] - previous[here] + rate[here] * value
     add_source(upcoming, 0, planes, source, wavelet[0, step])
@@ -190,42 +220,48 @@
 
 
 def adjoint_kernel(step, *refs):
+    bands, refs = refs[:2], refs[2:]
     current, later, near, far, rate, injected, earlier, near_edge, far_edge, ext = refs
     planes = current.shape[0]
     place(ext, near, far)
     ext[pl.ds(halo, planes)] = rate[...] * current[...]
-    along_y, along_z = bands(current)
     for first in range(0, planes, halo):
         here = pl.ds(first, halo)
-        value = laplacian(ext, first + halo, along_y, along_z)
+        value = laplacian(ext, first + halo, *bands)
         earlier[here] = 2.0 * current[here] - later[here] + value + injected[step, here]
     near_at, far_at = edge_spots(planes)
     near_edge[...] = rate[pl.ds(near_at, halo)] * earlier[pl.ds(near_at, halo)]
     far_edge[...] = rate[pl.ds(far_at, halo)] * earlier[pl.ds(far_at, halo)]
 
 
-def turn_kernel(forward_step, step, source, wavelet, *refs):
+def turn_kernel(forward_step, step, *refs):
+    *bands, source, wavelet = refs[:4]
+    refs = refs[4:]
     (current, later, near, far, rate, injected, lap1, lap2, lap3, wave, before, a5,
-     earlier, near_edge, far_edge, rest, keep, send, inner, ext, grad) = refs
+     earlier, near_edge, far_edge, rest, part, keep, send, inner, ext, wide, grad) = refs
     planes = current.shape[0]
     place(ext, near, far)
     ext[pl.ds(halo, planes)] = rate[...] * current[...]
-    along_y, along_z = bands(current)
+    alone(wide, wave[...])
     for first in range(0, planes, halo):
         here = pl.ds(first, halo)
-        value = laplacian(ext, first + halo, along_y, along_z)
+        value = laplacian(ext, first + halo, *bands)
         value = 2.0 * current[here] - later[here] + value + injected[step, here]
         earlier[here] = value
         partial = later[here] * lap3[here] + current[here] * lap2[here] + value * lap1[here]
-        if first == 0:
-            rest[0] = partial
-        elif first == planes - halo:
-            rest[1] = partial
+        value = laplacian(wide, first + halo, *bands)
+        partial = partial + a5[here] * value
+        value = 2.0 * wave[here] - before[here] + rate[here] * value
+        if first == 0 or first == planes - halo:
+            side = 0 if first == 0 else 1
+            rest[side] = partial
+            part[side] = value
         else:
-            value = laplacian(wave, first, along_y, along_z)
             within = pl.ds(first - halo, halo)
-            inner[within] = 2.0 * wave[here] - before[here] + rate[here] * value
-            grad[within] = partial + a5[here] * value
+            inner[within] = value
+            grad[within] = partial
+    for side, first in enumerate((0, planes - halo)):
+        add_source(part.at[side], first, planes, source, wavelet[0, forward_step])
     add_source(inner, halo, planes, source, wavelet[0, forward_step])
     near_at, far_at = edge_spots(planes)
     near_edge[...] = rate[pl.ds(near_at, halo)] * earlier[pl.ds(near_at, halo)]
@@ -236,66 +272,51 @@
     send[...] = grad[pl.ds(half - mine, half)]
 
 
-def forward_outer_kernel(step, source, wavelet, *refs):
-    current, previous, far, near, rate, rest, a5, keep, send, outer, ext, grad = refs
-    planes = current.shape[0]
-    place(ext, near, far)
-    ext[pl.ds(halo, planes)] = current[...]
-    along_y, along_z = bands(current)
+def forward_outer_kernel(far, near, rate, part, rest, a5, keep, send, outer, sides, grad):
+    planes = rate.shape[0]
+    place_sides(sides, near, far)
     for side, first in enumerate((0, planes - halo)):
         here = pl.ds(first, halo)
-        value = laplacian(ext, first + halo, along_y, along_z)
-        outer[side] = 2.0 * current[here] - previous[here] + rate[here] * value
+        value = beyond(sides, side)
+        outer[side] = part[side] + rate[here] * value
         grad[side] = rest[side] + a5[here] * value
-        add_source(outer.at[side], first, planes, source, wavelet[0, step])
     keep[...] = grad[core()]
     send[...] = grad[1 - core()]
 
 
+def pass_kernel(near, far, _, near_edge, far_edge):
+    near_edge[...] = near[...]
+    far_edge[...] = far[...]
+
+
 def adjoint_inner_kernel(step, *refs):
-    (current, later, rate, injected, inner, near_in, far_in, _,
-     first_adjoint, final, near_edge, far_edge, ext, stage, sems) = refs
+    (*bands, current, later, rate, injected, inner, outer,
+     first_adjoint, final, part, ext, stage, sems) = refs
     planes = current.shape[0]
-    within = pl.ds(halo, planes - 2 * halo)
-    near_edge[...] = near_in[...]
-    far_edge[...] = far_in[...]
-    wave_copy = pltpu.make_async_copy(inner, final.at[within], sems.at[0])
-    wave_copy.start()
-    ext[...] = rate[...] * current[...]
-    along_y, along_z = bands(current)
-    for first in range(halo, planes - halo, halo):
+    edge = planes - halo
+    copies = []
+    for piece, low, high in ((inner, halo, edge), (outer.at[0], 0, halo), (outer.at[1], edge, planes)):
+        copies.append(pltpu.make_async_copy(piece, final.at[low:high], sems.at[len(copies)]))
+        copies[-1].start()
+    alone(ext, rate[...] * current[...])
+    for first in range(0, planes, halo):
         here = pl.ds(first, halo)
-        value = laplacian(ext, first, along_y, along_z)
-        stage[pl.ds(first - halo, halo)] = (
-            2.0 * current[here] - later[here] + value + injected[step, here]
-        )
-    copy = pltpu.make_async_copy(stage, first_adjoint.at[within], sems.at[1])
-    copy.start()
-    wave_copy.wait()
-    copy.wait()
-
-
-def adjoint_outer_kernel(step, *refs):
-    (current, later, near, far, rate, injected, outer_wave, _,
-     outer, final, ext, sems) = refs
-    planes = current.shape[0]
-    copies = []
-    for side, first in enumerate((0, planes - halo)):
-        copies.append(
-            pltpu.make_async_copy(
-                outer_wave.at[side], final.at[pl.ds(first, halo)], sems.at[side]
-            )
-        )
-        copies[side].start()
-    place(ext, near, far)
-    ext[pl.ds(halo, planes)] = rate[...] * current[...]
-    along_y, along_z = bands(current)
-    for side, first in enumerate((0, planes - halo)):
-        here = pl.ds(first, halo)
-        value = laplacian(ext, first + halo, along_y, along_z)
-        outer[side] = 2.0 * current[here] - later[here] + value + injected[step, here]
+        value = laplacian(ext, first + halo, *bands)
+        value = 2.0 * current[here] - later[here] + value + injected[step, here]
+        if first == 0 or first == edge:
+            part[0 if first == 0 else 1] = value
+        else:
+            stage[pl.ds(first - halo, halo)] = value
+    copies.append(pltpu.make_async_copy(stage, first_adjoint.at[halo:edge], sems.at[3]))
+    copies[-1].start()
     for copy in copies:
         copy.wait()
+
+
+def adjoint_outer_kernel(near, far, part, outer, sides):
+    place_sides(sides, near, far)
+    for side in range(2):
+        outer[side] = part[side] + beyond(sides, side)
 
 
 def finish_kernel(inner_kept, inner_got, kept, got, outer, _, first_adjoint, total, sems):
@@ -395,18 +416,19 @@
     pair = (f32(2, halo, nz, ny), vmem)
     ext = pltpu.VMEM((planes + 2 * halo, nz, ny), jnp.float32)
     within = pltpu.VMEM((inner, nz, ny), jnp.float32)
-    outer = pltpu.VMEM((2, halo, nz, ny), jnp.float32)
 
     near_at = jnp.where(odd == 1, 0, planes - halo)
     near_edge = lax.dynamic_slice_in_dim(wave_current[0], near_at, halo, axis=0)
     far_edge = lax.dynamic_slice_in_dim(wave_current[0], planes - halo - near_at, halo, axis=0)
     u_halo = swap(near_edge, far_edge)
 
-    rate, near_edge, far_edge, a5, u1, u0, a6 = call(
+    rate, near_edge, far_edge, *bands, a5, u1, u0, a6 = call(
         prepare_kernel,
         (table, labels, a5, u1, u0, a6),
         [vmem] + [hbm] * 5,
-        [block, edge, edge] + [block] * 4,
+        [block, edge, edge]
+        + [(jax.ShapeDtypeStruct((n, n), jnp.bfloat16), vmem) for n in (ny, halo * nz)]
+        + [block] * 4,
         [pltpu.VMEM((planes, nz, ny), jnp.int32), pltpu.SemaphoreType.DMA((5,))],
     )
     a_halo = swap(near_edge, far_edge)
@@ -424,8 +446,8 @@
     for n in range(steps - 1):
         upcoming, lap, near_edge, far_edge = call(
             functools.partial(forward_kernel, n),
-            (source_index, wavelet, current, previous, *u_halo[::-1], rate, injected),
-            [vmem] * 7 + [wherever],
+            (*bands, source_index, wavelet, current, previous, *u_halo[::-1], rate, injected),
+            [vmem] * 9 + [wherever],
             [block, block, edge, edge],
             [ext],
         )
@@ -436,48 +458,54 @@
         if n < steps - 2:
             earlier, near_edge, far_edge = call(
                 functools.partial(adjoint_kernel, step),
-                (adjoint, later, *a_halo, rate, injected),
-                [vmem] * 6,
+                (*bands, adjoint, later, *a_halo, rate, injected),
+                [vmem] * 8,
                 [block, edge, edge],
                 [ext],
             )
         else:
-            earlier, near_edge, far_edge, rest, keep, send, inner_wave = call(
+            earlier, near_edge, far_edge, rest, part, keep, send, inner_wave = call(
                 functools.partial(turn_kernel, steps - 1, step),
-                (source_index, wavelet, adjoint, later, *a_halo, rate, injected, *laps,
+                (*bands, source_index, wavelet, adjoint, later, *a_halo, rate, injected, *laps,
                  current, previous, a5),
-                [vmem] * 14,
-                [block, edge, edge, pair, quarter, quarter, (f32(inner, nz, ny), vmem)],
-                [ext, within],
+                [vmem] * 16,
+                [block, edge, edge, pair, pair, quarter, quarter, (f32(inner, nz, ny), vmem)],
+                [ext, ext, within],
             )
         if n < steps - 2:
             a_halo = swap(near_edge, far_edge)
         later, adjoint = adjoint, earlier
 
     inner_sum = first_sum(keep, send, keep, 4)
-    first_adjoint, final, near_edge, far_edge = call(
+    near_edge, far_edge = call(
+        pass_kernel,
+        (near_edge, far_edge, inner_sum[0]),
+        [vmem, vmem, wherever],
+        [edge, edge],
+    )
+    a_halo = swap(near_edge, far_edge)
+    outer = pltpu.VMEM((2, halo, nz, ny), jnp.float32)
+    keep, send, outer_wave = call(
+        forward_outer_kernel,
+        (*u_halo[::-1], rate, part, rest, a5),
+        [vmem] * 6,
+        [edge, edge, pair],
+        [outer, outer],
+    )
+    outer_sum = first_sum(keep, send, inner_sum[1], 2)
+    first_adjoint, final, part = call(
         functools.partial(adjoint_inner_kernel, 0),
-        (adjoint, later, rate, injected, inner_wave, near_edge, far_edge, inner_sum[0]),
-        [vmem] * 7 + [wherever],
-        [(whole, hbm), (whole, hbm), edge, edge],
-        [pltpu.VMEM((planes, nz, ny), jnp.float32), within, pltpu.SemaphoreType.DMA((2,))],
-    )
-    a_halo = swap(near_edge, far_edge)
-    keep, send, outer_wave = call(
-        functools.partial(forward_outer_kernel, steps - 1),
-        (source_index, wavelet, current, previous, *u_halo[::-1], rate, rest, a5),
-        [vmem] * 9,
-        [edge, edge, pair],
-        [ext, outer],
-    )
-    outer_sum = first_sum(keep, send, inner_sum[1], 2)
-    last_outer, final = call(
-        functools.partial(adjoint_outer_kernel, 0),
-        (adjoint, later, *a_halo, rate, injected, outer_wave, final),
-        [vmem] * 7 + [hbm],
-        [pair, (whole, hbm)],
-        [ext, pltpu.SemaphoreType.DMA((2,))],
-        {7: 1},
+        (*bands, adjoint, later, rate, injected, inner_wave, outer_wave),
+        [vmem] * 8,
+        [(whole, hbm), (whole, hbm), pair],
+        [ext, within, pltpu.SemaphoreType.DMA((4,))],
+    )
+    (last_outer,) = call(
+        adjoint_outer_kernel,
+        (*a_halo, part),
+        [vmem] * 3,
+        [pair],
+        [outer],
         cost=2000000000,
     )
     inner_kept, inner_got = second_sum(*inner_sum, last_outer)

time: 102 us -> 101 us (level)
    ppermute x2, waiting for transfers between devices: 0.67 us -> 3.09 us  [first_sum(): return (kept, lax.ppermute(kept, 'shot', across))]
    ppermute x8, waiting for transfers between devices: 33.1 us -> 30.9 us  [swap(): return (lax.ppermute(near_edge, 'dom', near_pairs), far)]
    pallas_call x16 -> x17, Pallas kernels: 27.4 us -> 26.4 us  [call(): pl.pallas_call(kernel, out_shape=[pltpu.VMEM(shape.shape, shape.dtype) if...]
  transfers between devices with their start and end apart: 26 -> 26, of which waited for: 13 -> 12; matrix products, arithmetic and copies ran while one was open for 0% -> 0% of each run, Pallas kernels for 26% -> 25%
where the time goes in v5:
time: 101 us
  waiting for transfers between devices  37.1 us (37%)
  starting transfers between devices  34.1 us (34%)
  Pallas kernels  26.4 us (26%)
  local copies, waits for them, and re-layouts  1.79 us (2%)
  between operations  1.09 us (1%)
    ppermute x8, waiting for transfers between devices, swap(): return (lax.ppermute(near_edge, 'dom', near_pairs), far)  30.9 us
    pallas_call x17, Pallas kernels, call(): pl.pallas_call(kernel, out_shape=[pltpu.VMEM(shape.shape, shape.dtype) if...  26.4 us
    ppermute x8, starting transfers between devices, swap(): return (lax.ppermute(near_edge, 'dom', near_pairs), far)  23.6 us
    ppermute x8, starting transfers between devices, swap(): far = lax.ppermute(far_edge, 'dom', far_pairs)  5.55 us
    ppermute x2, starting transfers between devices, first_sum(): return (kept, lax.ppermute(kept, 'shot', across))  3.17 us
    ppermute x2, waiting for transfers between devices, first_sum(): return (kept, lax.ppermute(kept, 'shot', across))  3.09 us
  transfers between devices with their start and end apart: 26, of which 12 were waited for; matrix products, arithmetic and copies ran while one was open for 0% of the time, Pallas kernels for 25%

profile of v5, /device:TPU:0, one launch (start us, length us, event | category | flops | bytes accessed | tf_op | source)
XLA Modules:
  0.0 100.5 jit_solution(4923990474790117962)
XLA Ops:
  0.7 1.1 %dynamic-slice_bitcast_fusion = (f32[4,64,256]{2,1,0:T(8,128)S(1)}, f32[4,64,256]{2,1,0:T(8,128)S(1)}) fusion(f32[1,16,64,256]{3,2,1,0:T(8,128)} %param.11, s32[]{:T(128)S(6)} %select_n.16, s32[]{:T(128)S(6)} %select_n.17), kind=kLoop, calls=%fused_computation | loop fusion | bytes 1048584 | tf_op jit(solution)/shard_map/dynamic_slice | solution.py:421
  1.7 3.0 %collective-permute-start.7 = (f32[4,64,256]{2,1,0:T(8,128)S(1)}, f32[4,64,256]{2,1,0:T(8,128)S(1)}, u32[]{:S(2)}, u32[]{:S(2)}) collective-permute-start(f32[4,64,256]{2,1,0:T(8,128)S(1)} %get-tuple-element.93), channel_id=1, source_target_pairs={{0,1},{1,0},{2,3},{3,2},{4,5},{5,4},{6,7},{7,6},{8,9},{9,8},{10,11... | collective-permute-start | bytes 786440 | tf_op jit(solution)/shard_map/ppermute | solution.py:349
  6.1 2.6 %shard_map.121 = (f32[16,64,256]{2,1,0:T(8,128)S(1)}, f32[4,64,256]{2,1,0:T(8,128)S(1)}, f32[4,64,256]{2,1,0:T(8,128)S(1)}, bf16[256,256]{1,0:T(8,128)(2,1)S(1)}...) custom-call(f32[8]{0:T(128)S(1)} %copy-done.3, ...), custom_call_target="tpu_custom_call" | custom-call | flops 1024 | bytes 1024 | tf_op jit(solution)/shard_map/pallas_call | solution.py:22
  8.7 4.3 %collective-permute-start = (f32[4,64,256]{2,1,0:T(8,128)S(1)}, f32[4,64,256]{2,1,0:T(8,128)S(1)}, u32[]{:S(2)}, u32[]{:S(2)}) collective-permute-start(f32[4,64,256]{2,1,0:T(8,128)S(1)} %get-tuple-element.52), channel_id=1, source_target_pairs={{0,1},{1,0},{2,3},{3,2},{4,5},{5,4},{6,7},{7,6},{8,9},{9,8},{10,11... | collective-permute-start | bytes 786440 | tf_op jit(solution)/shard_map/ppermute | solution.py:349
  13.8 6.7 %shard_map.122.refs_7_.refs_9_.refs_5_ = f32[4,16,64,256]{3,2,1,0:T(8,128)S(1)} custom-call(s32[3,1024]{1,0:T(4,128)S(1)} %bitcast.16, f32[4,1024]{1,0:T(4,128)S(1)} %bitcast.17, f32[16,64,256]{2,1,0:T(8,128)S(1)} %get-tuple-element.54._.refs_6_.refs_8_.rate.refs_4_), custom_call_target="tpu_custom_call" | custom-call | flops 1024 | bytes 1024 | tf_op jit(solution)/shard_map/pallas_call | solution.py:22
  20.5 2.2 %collective-permute-done.7.refs_7_ = f32[4,64,256]{2,1,0:T(8,128)S(1)} collective-permute-done((f32[4,64,256]{2,1,0:T(8,128)S(1)}, f32[4,64,256]{2,1,0:T(8,128)S(1)}, u32[]{:S(2)}, u32[]{:S(2)}) %collective-permute-start.7) | collective-permute-done | bytes 262176 | tf_op jit(solution)/shard_map/ppermute | solution.py:349
  22.7 1.8 %shard_map.125 = (f32[16,64,256]{2,1,0:T(8,128)S(1)}, f32[16,64,256]{2,1,0:T(8,128)S(1)}, f32[4,64,256]{2,1,0:T(8,128)S(1)}, f32[4,64,256]{2,1,0:T(8,128)S(1)}) custom-call(bf16[256,256]{1,0:T(8,128)(2,1)S(1)} %get-tuple-element.48.refs_0_, bf16[256,256]{1,0:T(8,128)(2,1)S(1)} %get-tuple-element.49.refs_1_, s32[1,3]{1,0:T(1,128)S(1)} %copy-done.1, ...), custom_call_target="tpu_custom_call" | custom-call | flops 1024 | bytes 1024 | tf_op jit(solution)/shard_map/pallas_call | solution.py:22
  25.2 5.3 %collective-permute-start.9 = (f32[4,64,256]{2,1,0:T(8,128)S(1)}, f32[4,64,256]{2,1,0:T(8,128)S(1)}, u32[]{:S(2)}, u32[]{:S(2)}) collective-permute-start(f32[4,64,256]{2,1,0:T(8,128)S(1)} %get-tuple-element.66), channel_id=1, source_target_pairs={{0,1},{1,0},{2,3},{3,2},{4,5},{5,4},{6,7},{7,6},{8,9},{9,8},{10,11... | collective-permute-start | bytes 786440 | tf_op jit(solution)/shard_map/ppermute | solution.py:349
  30.6 1.8 %shard_map.123 = (f32[16,64,256]{2,1,0:T(8,128)S(1)}, f32[4,64,256]{2,1,0:T(8,128)S(1)}, f32[4,64,256]{2,1,0:T(8,128)S(1)}) custom-call(bf16[256,256]{1,0:T(8,128)(2,1)S(1)} %get-tuple-element.48.refs_0_, bf16[256,256]{1,0:T(8,128)(2,1)S(1)} %get-tuple-element.49.refs_1_, f32[16,64,256]{2,1,0:T(8,128)S(1)} %get-tuple-element.50.refs_2_.refs_3_.refs_15_.a5, ...), custom_call_target="tpu_custom_call" | custom-call | flops 1024 | bytes 1024 | tf_op jit(solution)/shard_map/pallas_call | solution.py:22
  33.2 12.1 %collective-permute-done.9.refs_7_ = f32[4,64,256]{2,1,0:T(8,128)S(1)} collective-permute-done((f32[4,64,256]{2,1,0:T(8,128)S(1)}, f32[4,64,256]{2,1,0:T(8,128)S(1)}, u32[]{:S(2)}, u32[]{:S(2)}) %collective-permute-start.9) | collective-permute-done | bytes 262176 | tf_op jit(solution)/shard_map/ppermute | solution.py:349
  45.3 1.8 %shard_map.126 = (f32[16,64,256]{2,1,0:T(8,128)S(1)}, f32[16,64,256]{2,1,0:T(8,128)S(1)}, f32[4,64,256]{2,1,0:T(8,128)S(1)}, f32[4,64,256]{2,1,0:T(8,128)S(1)}) custom-call(bf16[256,256]{1,0:T(8,128)(2,1)S(1)} %get-tuple-element.48.refs_0_, bf16[256,256]{1,0:T(8,128)(2,1)S(1)} %get-tuple-element.49.refs_1_, s32[1,3]{1,0:T(1,128)S(1)} %copy-done.1, ...), custom_call_target="tpu_custom_call" | custom-call | flops 1024 | bytes 1024 | tf_op jit(solution)/shard_map/pallas_call | solution.py:22
  47.9 5.2 %collective-permute-start.11 = (f32[4,64,256]{2,1,0:T(8,128)S(1)}, f32[4,64,256]{2,1,0:T(8,128)S(1)}, u32[]{:S(2)}, u32[]{:S(2)}) collective-permute-start(f32[4,64,256]{2,1,0:T(8,128)S(1)} %get-tuple-element.70), channel_id=1, source_target_pairs={{0,1},{1,0},{2,3},{3,2},{4,5},{5,4},{6,7},{7,6},{8,9},{9,8},{10,11... | collective-permute-start | bytes 786440 | tf_op jit(solution)/shard_map/ppermute | solution.py:349
  53.1 1.9 %shard_map.124 = (f32[16,64,256]{2,1,0:T(8,128)S(1)}, f32[4,64,256]{2,1,0:T(8,128)S(1)}, f32[4,64,256]{2,1,0:T(8,128)S(1)}) custom-call(bf16[256,256]{1,0:T(8,128)(2,1)S(1)} %get-tuple-element.48.refs_0_, bf16[256,256]{1,0:T(8,128)(2,1)S(1)} %get-tuple-element.49.refs_1_, f32[16,64,256]{2,1,0:T(8,128)S(1)} %get-tuple-element.55.refs_2_.refs_5_, ...), custom_call_target="tpu_custom_call" | custom-call | flops 1024 | bytes 1024 | tf_op jit(solution)/shard_map/pallas_call | solution.py:22
  55.7 11.9 %collective-permute-done.11.refs_7_ = f32[4,64,256]{2,1,0:T(8,128)S(1)} collective-permute-done((f32[4,64,256]{2,1,0:T(8,128)S(1)}, f32[4,64,256]{2,1,0:T(8,128)S(1)}, u32[]{:S(2)}, u32[]{:S(2)}) %collective-permute-start.11) | collective-permute-done | bytes 262176 | tf_op jit(solution)/shard_map/ppermute | solution.py:349
  67.6 1.7 %shard_map.127 = (f32[16,64,256]{2,1,0:T(8,128)S(1)}, f32[16,64,256]{2,1,0:T(8,128)S(1)}, f32[4,64,256]{2,1,0:T(8,128)S(1)}, f32[4,64,256]{2,1,0:T(8,128)S(1)}) custom-call(bf16[256,256]{1,0:T(8,128)(2,1)S(1)} %get-tuple-element.48.refs_0_, bf16[256,256]{1,0:T(8,128)(2,1)S(1)} %get-tuple-element.49.refs_1_, s32[1,3]{1,0:T(1,128)S(1)} %copy-done.1, ...), custom_call_target="tpu_custom_call" | custom-call | flops 1024 | bytes 1024 | tf_op jit(solution)/shard_map/pallas_call | solution.py:22
  70.0 5.1 %collective-permute-start.13 = (f32[4,64,256]{2,1,0:T(8,128)S(1)}, f32[4,64,256]{2,1,0:T(8,128)S(1)}, u32[]{:S(2)}, u32[]{:S(2)}) collective-permute-start(f32[4,64,256]{2,1,0:T(8,128)S(1)} %get-tuple-element.76), channel_id=1, source_target_pairs={{0,1},{1,0},{2,3},{3,2},{4,5},{5,4},{6,7},{7,6},{8,9},{9,8},{10,11... | collective-permute-start | bytes 786440 | tf_op jit(solution)/shard_map/ppermute | solution.py:349
  75.1 3.7 %shard_map.128 = (f32[16,64,256]{2,1,0:T(8,128)S(1)}, f32[4,64,256]{2,1,0:T(8,128)S(1)}, f32[4,64,256]{2,1,0:T(8,128)S(1)}, f32[2,4,64,256]{3,2,1,0:T(8,128)S(1)...) custom-call(bf16[256,256]{1,0:T(8,128)(2,1)S(1)} %get-tuple-element., ...), custom_call_target="tpu_custom_call" | custom-call | flops 1024 | bytes 1024 | tf_op jit(solution)/shard_map/pallas_call | solution.py:22
  81.4 1.6 %collective-permute-start.18 = (f32[4,64,256]{2,1,0:T(8,128)S(1)}, f32[4,64,256]{2,1,0:T(8,128)S(1)}, u32[]{:S(2)}, u32[]{:S(2)}) collective-permute-start(f32[4,64,256]{2,1,0:T(8,128)S(1)} %shard_map.131._.a), channel_id=1, source_target_pairs={{0,16},{8,24},{16,0},{24,8},{1,17},{9,25},{17,1},{25,9},{2,18},{10... | collective-permute-start | bytes 786440 | tf_op jit(solution)/shard_map/ppermute | solution.py:376
  84.3 1.7 %collective-permute-done.13.near = f32[4,64,256]{2,1,0:T(8,128)S(1)} collective-permute-done((f32[4,64,256]{2,1,0:T(8,128)S(1)}, f32[4,64,256]{2,1,0:T(8,128)S(1)}, u32[]{:S(2)}, u32[]{:S(2)}) %collective-permute-start.13) | collective-permute-done | bytes 262176 | tf_op jit(solution)/shard_map/ppermute | solution.py:349
  87.0 2.9 %collective-permute-done.18.b.refs_2_ = f32[4,64,256]{2,1,0:T(8,128)S(1)} collective-permute-done((f32[4,64,256]{2,1,0:T(8,128)S(1)}, f32[4,64,256]{2,1,0:T(8,128)S(1)}, u32[]{:S(2)}, u32[]{:S(2)}) %collective-permute-start.18) | collective-permute-done | bytes 262176 | tf_op jit(solution)/shard_map/ppermute | solution.py:376
  89.9 1.6 %collective-permute-start.24 = (f32[4,64,256]{2,1,0:T(8,128)S(1)}, f32[4,64,256]{2,1,0:T(8,128)S(1)}, u32[]{:S(2)}, u32[]{:S(2)}) collective-permute-start(f32[4,64,256]{2,1,0:T(8,128)S(1)} %shard_map.135.a), channel_id=1, source_target_pairs={{0,16},{8,24},{16,0},{24,8},{1,17},{9,25},{17,1},{25,9},{2,18},{10... | collective-permute-start | bytes 786440 | tf_op jit(solution)/shard_map/ppermute | solution.py:376
  91.5 2.4 %shard_map.130 = (f32[16,64,256]{2,1,0:T(8,128)}, f32[16,64,256]{2,1,0:T(8,128)}, f32[2,4,64,256]{3,2,1,0:T(8,128)S(1)}) custom-call(bf16[256,256]{1,0:T(8,128)(2,1)S(1)} %get-tuple-element.48.refs_0_, bf16[256,256]{1,0:T(8,128)(2,1)S(1)} %get-tuple-element.49.refs_1_, f32[16,64,256]{2,1,0:T(8,128)S(1)} %get-tuple-element.73.refs_2_, ...), custom_call_target="tpu_custom_call" | custom-call | flops 1024 | bytes 1024 | tf_op jit(solution)/shard_map/pallas_call | solution.py:22
  93.9 3.1 %collective-permute-done.19.near = f32[4,64,256]{2,1,0:T(8,128)S(1)} collective-permute-done((f32[4,64,256]{2,1,0:T(8,128)S(1)}, f32[4,64,256]{2,1,0:T(8,128)S(1)}, u32[]{:S(2)}, u32[]{:S(2)}) %collective-permute-start.19) | collective-permute-done | bytes 262176 | tf_op jit(solution)/shard_map/ppermute | solution.py:349
  99.2 1.2 %shard_map.137 = (f32[16,64,256]{2,1,0:T(8,128)}, f32[16,64,256]{2,1,0:T(8,128)}) custom-call(f32[4,64,256]{2,1,0:T(8,128)S(1)} %shard_map.134.inner_kept, f32[4,64,256]{2,1,0:T(8,128)S(1)} %collective-permute-done.21.inner_got, f32[4,64,256]{2,1,0:T(8,128)S(1)} %shard_map.136.kept, ...), custom_call_target="tpu_custom_call", output_to_operand_aliasing={{0}: (5, {})} | custom-call | flops 1024 | bytes 1024 | tf_op jit(solution)/shard_map/pallas_call | solution.py:22
  (59 shorter events, 12.9 us)
Async XLA Ops:
  1.7 21.0 %collective-permute-start.7 = (f32[4,64,256]{2,1,0:T(8,128)S(1)}, f32[4,64,256]{2,1,0:T(8,128)S(1)}, u32[]{:S(2)}, u32[]{:S(2)}) collective-permute-start(f32[4,64,256]{2,1,0:T(8,128)S(1)} %get-tuple-element.93), channel_id=1, source_target_pairs={{0,1},{1,0},{2,3},{3,2},{4,5},{5,4},{6,7},{7,6},{8,9},{9,8},{10,11... | collective-permute-start | bytes 786440 | tf_op jit(solution)/shard_map/ppermute | solution.py:349
  4.8 17.9 %collective-permute-start.6 = (f32[4,64,256]{2,1,0:T(8,128)S(1)}, f32[4,64,256]{2,1,0:T(8,128)S(1)}, u32[]{:S(2)}, u32[]{:S(2)}) collective-permute-start(f32[4,64,256]{2,1,0:T(8,128)S(1)} %get-tuple-element.94), channel_id=1, source_target_pairs={{1,2},{3,4},{5,6},{2,1},{4,3},{6,5},{9,10},{11,12},{13,14},{10,9},... | collective-permute-start | bytes 786440 | tf_op jit(solution)/shard_map/ppermute | solution.py:348
  8.7 21.8 %collective-permute-start = (f32[4,64,256]{2,1,0:T(8,128)S(1)}, f32[4,64,256]{2,1,0:T(8,128)S(1)}, u32[]{:S(2)}, u32[]{:S(2)}) collective-permute-start(f32[4,64,256]{2,1,0:T(8,128)S(1)} %get-tuple-element.52), channel_id=1, source_target_pairs={{0,1},{1,0},{2,3},{3,2},{4,5},{5,4},{6,7},{7,6},{8,9},{9,8},{10,11... | collective-permute-start | bytes 786440 | tf_op jit(solution)/shard_map/ppermute | solution.py:349
  13.1 17.5 %collective-permute-start.1 = (f32[4,64,256]{2,1,0:T(8,128)S(1)}, f32[4,64,256]{2,1,0:T(8,128)S(1)}, u32[]{:S(2)}, u32[]{:S(2)}) collective-permute-start(f32[4,64,256]{2,1,0:T(8,128)S(1)} %get-tuple-element.53), channel_id=1, source_target_pairs={{1,2},{3,4},{5,6},{2,1},{4,3},{6,5},{9,10},{11,12},{13,14},{10,9},... | collective-permute-start | bytes 786440 | tf_op jit(solution)/shard_map/ppermute | solution.py:348
  24.6 8.6 %collective-permute-start.8 = (f32[4,64,256]{2,1,0:T(8,128)S(1)}, f32[4,64,256]{2,1,0:T(8,128)S(1)}, u32[]{:S(2)}, u32[]{:S(2)}) collective-permute-start(f32[4,64,256]{2,1,0:T(8,128)S(1)} %get-tuple-element.65), channel_id=1, source_target_pairs={{1,2},{3,4},{5,6},{2,1},{4,3},{6,5},{9,10},{11,12},{13,14},{10,9},... | collective-permute-start | bytes 786440 | tf_op jit(solution)/shard_map/ppermute | solution.py:348
  25.2 20.0 %collective-permute-start.9 = (f32[4,64,256]{2,1,0:T(8,128)S(1)}, f32[4,64,256]{2,1,0:T(8,128)S(1)}, u32[]{:S(2)}, u32[]{:S(2)}) collective-permute-start(f32[4,64,256]{2,1,0:T(8,128)S(1)} %get-tuple-element.66), channel_id=1, source_target_pairs={{0,1},{1,0},{2,3},{3,2},{4,5},{5,4},{6,7},{7,6},{8,9},{9,8},{10,11... | collective-permute-start | bytes 786440 | tf_op jit(solution)/shard_map/ppermute | solution.py:349
  32.4 20.7 %collective-permute-start.2 = (f32[4,64,256]{2,1,0:T(8,128)S(1)}, f32[4,64,256]{2,1,0:T(8,128)S(1)}, u32[]{:S(2)}, u32[]{:S(2)}) collective-permute-start(f32[4,64,256]{2,1,0:T(8,128)S(1)} %get-tuple-element.56), channel_id=1, source_target_pairs={{0,1},{1,0},{2,3},{3,2},{4,5},{5,4},{6,7},{7,6},{8,9},{9,8},{10,11... | collective-permute-start | bytes 786440 | tf_op jit(solution)/shard_map/ppermute | solution.py:349
  32.5 20.6 %collective-permute-start.3 = (f32[4,64,256]{2,1,0:T(8,128)S(1)}, f32[4,64,256]{2,1,0:T(8,128)S(1)}, u32[]{:S(2)}, u32[]{:S(2)}) collective-permute-start(f32[4,64,256]{2,1,0:T(8,128)S(1)} %get-tuple-element.57), channel_id=1, source_target_pairs={{1,2},{3,4},{5,6},{2,1},{4,3},{6,5},{9,10},{11,12},{13,14},{10,9},... | collective-permute-start | bytes 786440 | tf_op jit(solution)/shard_map/ppermute | solution.py:348
  47.1 8.7 %collective-permute-start.10 = (f32[4,64,256]{2,1,0:T(8,128)S(1)}, f32[4,64,256]{2,1,0:T(8,128)S(1)}, u32[]{:S(2)}, u32[]{:S(2)}) collective-permute-start(f32[4,64,256]{2,1,0:T(8,128)S(1)} %get-tuple-element.69), channel_id=1, source_target_pairs={{1,2},{3,4},{5,6},{2,1},{4,3},{6,5},{9,10},{11,12},{13,14},{10,9},... | collective-permute-start | bytes 786440 | tf_op jit(solution)/shard_map/ppermute | solution.py:348
  47.9 19.7 %collective-permute-start.11 = (f32[4,64,256]{2,1,0:T(8,128)S(1)}, f32[4,64,256]{2,1,0:T(8,128)S(1)}, u32[]{:S(2)}, u32[]{:S(2)}) collective-permute-start(f32[4,64,256]{2,1,0:T(8,128)S(1)} %get-tuple-element.70), channel_id=1, source_target_pairs={{0,1},{1,0},{2,3},{3,2},{4,5},{5,4},{6,7},{7,6},{8,9},{9,8},{10,11... | collective-permute-start | bytes 786440 | tf_op jit(solution)/shard_map/ppermute | solution.py:349
  55.0 20.1 %collective-permute-start.4 = (f32[4,64,256]{2,1,0:T(8,128)S(1)}, f32[4,64,256]{2,1,0:T(8,128)S(1)}, u32[]{:S(2)}, u32[]{:S(2)}) collective-permute-start(f32[4,64,256]{2,1,0:T(8,128)S(1)} %get-tuple-element.59), channel_id=1, source_target_pairs={{0,1},{1,0},{2,3},{3,2},{4,5},{5,4},{6,7},{7,6},{8,9},{9,8},{10,11... | collective-permute-start | bytes 786440 | tf_op jit(solution)/shard_map/ppermute | solution.py:349
  55.0 20.1 %collective-permute-start.5 = (f32[4,64,256]{2,1,0:T(8,128)S(1)}, f32[4,64,256]{2,1,0:T(8,128)S(1)}, u32[]{:S(2)}, u32[]{:S(2)}) collective-permute-start(f32[4,64,256]{2,1,0:T(8,128)S(1)} %get-tuple-element.60), channel_id=1, source_target_pairs={{1,2},{3,4},{5,6},{2,1},{4,3},{6,5},{9,10},{11,12},{13,14},{10,9},... | collective-permute-start | bytes 786440 | tf_op jit(solution)/shard_map/ppermute | solution.py:348
  69.3 14.9 %collective-permute-start.12 = (f32[4,64,256]{2,1,0:T(8,128)S(1)}, f32[4,64,256]{2,1,0:T(8,128)S(1)}, u32[]{:S(2)}, u32[]{:S(2)}) collective-permute-start(f32[4,64,256]{2,1,0:T(8,128)S(1)} %get-tuple-element.75), channel_id=1, source_target_pairs={{1,2},{3,4},{5,6},{2,1},{4,3},{6,5},{9,10},{11,12},{13,14},{10,9},... | collective-permute-start | bytes 786440 | tf_op jit(solution)/shard_map/ppermute | solution.py:348
  70.0 16.0 %collective-permute-start.13 = (f32[4,64,256]{2,1,0:T(8,128)S(1)}, f32[4,64,256]{2,1,0:T(8,128)S(1)}, u32[]{:S(2)}, u32[]{:S(2)}) collective-permute-start(f32[4,64,256]{2,1,0:T(8,128)S(1)} %get-tuple-element.76), channel_id=1, source_target_pairs={{0,1},{1,0},{2,3},{3,2},{4,5},{5,4},{6,7},{7,6},{8,9},{9,8},{10,11... | collective-permute-start | bytes 786440 | tf_op jit(solution)/shard_map/ppermute | solution.py:349
  78.8 1.3 %collective-permute-start.17 = (f32[1,64,256]{2,1,0:T(8,128)S(1)}, f32[1,64,256]{2,1,0:T(8,128)S(1)}, u32[]{:S(2)}, u32[]{:S(2)}) collective-permute-start(f32[1,64,256]{2,1,0:T(8,128)S(1)} %get-tuple-element.97), channel_id=1, source_target_pairs={{0,8},{8,0},{16,24},{24,16},{1,9},{9,1},{17,25},{25,17},{2,10},{10... | collective-permute-start | bytes 196616 | tf_op jit(solution)/shard_map/ppermute | solution.py:369
  78.9 1.4 %collective-permute-start.16 = (f32[1,64,256]{2,1,0:T(8,128)S(1)}, f32[1,64,256]{2,1,0:T(8,128)S(1)}, u32[]{:S(2)}, u32[]{:S(2)}) collective-permute-start(f32[1,64,256]{2,1,0:T(8,128)S(1)} %get-tuple-element.98), channel_id=1, source_target_pairs={{0,8},{8,0},{16,24},{24,16},{1,9},{9,1},{17,25},{25,17},{2,10},{10... | collective-permute-start | bytes 196616 | tf_op jit(solution)/shard_map/ppermute | solution.py:369
  81.4 8.4 %collective-permute-start.18 = (f32[4,64,256]{2,1,0:T(8,128)S(1)}, f32[4,64,256]{2,1,0:T(8,128)S(1)}, u32[]{:S(2)}, u32[]{:S(2)}) collective-permute-start(f32[4,64,256]{2,1,0:T(8,128)S(1)} %shard_map.131._.a), channel_id=1, source_target_pairs={{0,16},{8,24},{16,0},{24,8},{1,17},{9,25},{17,1},{25,9},{2,18},{10... | collective-permute-start | bytes 786440 | tf_op jit(solution)/shard_map/ppermute | solution.py:376
  83.0 13.9 %collective-permute-start.19 = (f32[4,64,256]{2,1,0:T(8,128)S(1)}, f32[4,64,256]{2,1,0:T(8,128)S(1)}, u32[]{:S(2)}, u32[]{:S(2)}) collective-permute-start(f32[4,64,256]{2,1,0:T(8,128)S(1)} %get-tuple-element.85), channel_id=1, source_target_pairs={{0,1},{1,0},{2,3},{3,2},{4,5},{5,4},{6,7},{7,6},{8,9},{9,8},{10,11... | collective-permute-start | bytes 786440 | tf_op jit(solution)/shard_map/ppermute | solution.py:349
  83.6 13.3 %collective-permute-start.20 = (f32[4,64,256]{2,1,0:T(8,128)S(1)}, f32[4,64,256]{2,1,0:T(8,128)S(1)}, u32[]{:S(2)}, u32[]{:S(2)}) collective-permute-start(f32[4,64,256]{2,1,0:T(8,128)S(1)} %get-tuple-element.86), channel_id=1, source_target_pairs={{1,2},{3,4},{5,6},{2,1},{4,3},{6,5},{9,10},{11,12},{13,14},{10,9},... | collective-permute-start | bytes 786440 | tf_op jit(solution)/shard_map/ppermute | solution.py:348
  86.4 3.4 %collective-permute-start.23 = (f32[2,64,256]{2,1,0:T(8,128)S(1)}, f32[2,64,256]{2,1,0:T(8,128)S(1)}, u32[]{:S(2)}, u32[]{:S(2)}) collective-permute-start(f32[2,64,256]{2,1,0:T(8,128)S(1)} %get-tuple-element.95), channel_id=1, source_target_pairs={{0,8},{8,0},{16,24},{24,16},{1,9},{9,1},{17,25},{25,17},{2,10},{10... | collective-permute-start | bytes 393224 | tf_op jit(solution)/shard_map/ppermute | solution.py:369
  86.5 3.4 %collective-permute-start.22 = (f32[2,64,256]{2,1,0:T(8,128)S(1)}, f32[2,64,256]{2,1,0:T(8,128)S(1)}, u32[]{:S(2)}, u32[]{:S(2)}) collective-permute-start(f32[2,64,256]{2,1,0:T(8,128)S(1)} %get-tuple-element.96), channel_id=1, source_target_pairs={{0,8},{8,0},{16,24},{24,16},{1,9},{9,1},{17,25},{25,17},{2,10},{10... | collective-permute-start | bytes 393224 | tf_op jit(solution)/shard_map/ppermute | solution.py:369
  89.9 7.6 %collective-permute-start.24 = (f32[4,64,256]{2,1,0:T(8,128)S(1)}, f32[4,64,256]{2,1,0:T(8,128)S(1)}, u32[]{:S(2)}, u32[]{:S(2)}) collective-permute-start(f32[4,64,256]{2,1,0:T(8,128)S(1)} %shard_map.135.a), channel_id=1, source_target_pairs={{0,16},{8,24},{16,0},{24,8},{1,17},{9,25},{17,1},{25,9},{2,18},{10... | collective-permute-start | bytes 786440 | tf_op jit(solution)/shard_map/ppermute | solution.py:376
  97.2 1.6 %collective-permute-start.21 = (f32[4,64,256]{2,1,0:T(8,128)S(1)}, f32[4,64,256]{2,1,0:T(8,128)S(1)}, u32[]{:S(2)}, u32[]{:S(2)}) collective-permute-start(f32[4,64,256]{2,1,0:T(8,128)S(1)} %shard_map.134.inner_kept), channel_id=1, source_target_pairs={{0,8},{8,0},{16,24},{24,16},{1,9},{9,1},{17,25},{25,17},{2,10},{10... | collective-permute-start | bytes 786440 | tf_op jit(solution)/shard_map/ppermute | solution.py:388
  97.5 1.6 %collective-permute-start.25 = (f32[4,64,256]{2,1,0:T(8,128)S(1)}, f32[4,64,256]{2,1,0:T(8,128)S(1)}, u32[]{:S(2)}, u32[]{:S(2)}) collective-permute-start(f32[4,64,256]{2,1,0:T(8,128)S(1)} %shard_map.136.kept), channel_id=1, source_target_pairs={{0,8},{8,0},{16,24},{24,16},{1,9},{9,1},{17,25},{25,17},{2,10},{10... | collective-permute-start | bytes 786440 | tf_op jit(solution)/shard_map/ppermute | solution.py:388
  (7 other events, 62.7 us)

commit v6 on v5

--- a/solution.py
+++ b/solution.py
@@ -319,25 +319,36 @@
         outer[side] = part[side] + beyond(sides, side)
 
 
-def finish_kernel(inner_kept, inner_got, kept, got, outer, _, first_adjoint, total, sems):
-    planes = total.shape[0]
-    half = inner_kept.shape[0]
-    mine = core() * half
-    side = core() * (planes - halo)
-    spots = (
-        (inner_kept, total, halo + mine, half),
-        (inner_got, total, halo + half - mine, half),
-        (kept, total, side, halo),
-        (got, total, planes - halo - side, halo),
-        (outer.at[0], first_adjoint, 0, halo),
-        (outer.at[1], first_adjoint, planes - halo, halo),
-    )
+def write(moves, sems):
     copies = []
-    for n, (piece, target, at, count) in enumerate(spots):
+    for n, (piece, target, at, count) in enumerate(moves):
         copies.append(pltpu.make_async_copy(piece, target.at[pl.ds(at, count)], sems.at[n]))
         copies[n].start()
     for copy in copies:
         copy.wait()
+
+
+def early_kernel(inner_kept, kept, outer, _, first_adjoint, total, sems):
+    planes = total.shape[0]
+    half = inner_kept.shape[0]
+    moves = (
+        (inner_kept, total, halo + core() * half, half),
+        (kept, total, core() * (planes - halo), halo),
+        (outer.at[0], first_adjoint, 0, halo),
+        (outer.at[1], first_adjoint, planes - halo, halo),
+    )
+    write(moves, sems)
+
+
+def finish_kernel(inner_got, got, _, total, sems):
+    planes = total.shape[0]
+    half = inner_got.shape[0]
+    other = 1 - core()
+    moves = (
+        (inner_got, total, halo + other * half, half),
+        (got, total, other * (planes - halo), halo),
+    )
+    write(moves, sems)
 
 
 def swap(near_edge, far_edge):
@@ -511,12 +522,20 @@
     inner_kept, inner_got = second_sum(*inner_sum, last_outer)
     kept, got = second_sum(*outer_sum, last_outer)
     first_adjoint, total = call(
+        early_kernel,
+        (inner_kept, kept, last_outer, first_adjoint),
+        [vmem] * 3 + [hbm],
+        [(whole, hbm), (whole, hbm)],
+        [pltpu.SemaphoreType.DMA((4,))],
+        {3: 0},
+    )
+    (total,) = call(
         finish_kernel,
-        (inner_kept, inner_got, kept, got, last_outer, first_adjoint),
-        [vmem] * 5 + [hbm],
-        [(whole, hbm), (whole, hbm)],
-        [pltpu.SemaphoreType.DMA((6,))],
-        {5: 0},
+        (inner_got, got, total),
+        [vmem] * 2 + [hbm],
+        [(whole, hbm)],
+        [pltpu.SemaphoreType.DMA((2,))],
+        {2: 0},
     )
     return (final[None], first_adjoint[None], total)
 

time: 101 us -> 100 us (0.990)
    pallas_call x17 -> x18, Pallas kernels: 26.4 us -> 27 us  [call(): pl.pallas_call(kernel, out_shape=[pltpu.VMEM(shape.shape, shape.dtype) if...]
  transfers between devices with their start and end apart: 26 -> 26, of which waited for: 12 -> 11; matrix products, arithmetic and copies ran while one was open for 0% -> 0% of each run, Pallas kernels for 25% -> 26%
where the time goes in v6:
time: 100 us
  waiting for transfers between devices  36.1 us (36%)
  starting transfers between devices  34.1 us (34%)
  Pallas kernels  27 us (27%)
  local copies, waits for them, and re-layouts  1.79 us (2%)
  between operations  1.1 us (1%)
    ppermute x8, waiting for transfers between devices, swap(): return (lax.ppermute(near_edge, 'dom', near_pairs), far)  30.9 us
    pallas_call x18, Pallas kernels, call(): pl.pallas_call(kernel, out_shape=[pltpu.VMEM(shape.shape, shape.dtype) if...  27 us
    ppermute x8, starting transfers between devices, swap(): return (lax.ppermute(near_edge, 'dom', near_pairs), far)  23.6 us
    ppermute x8, starting transfers between devices, swap(): far = lax.ppermute(far_edge, 'dom', far_pairs)  5.55 us
    ppermute x2, starting transfers between devices, first_sum(): return (kept, lax.ppermute(kept, 'shot', across))  3.17 us
    ppermute x2, waiting for transfers between devices, first_sum(): return (kept, lax.ppermute(kept, 'shot', across))  3.09 us
  transfers between devices with their start and end apart: 26, of which 11 were waited for; matrix products, arithmetic and copies ran while one was open for 0% of the time, Pallas kernels for 26%

profile of v6, /device:TPU:0, one launch (start us, length us, event | category | flops | bytes accessed | tf_op | source)
XLA Modules:
  0.0 100.1 jit_solution(8083544783035112067)
XLA Ops:
  0.7 1.1 %dynamic-slice_bitcast_fusion = (f32[4,64,256]{2,1,0:T(8,128)S(1)}, f32[4,64,256]{2,1,0:T(8,128)S(1)}) fusion(f32[1,16,64,256]{3,2,1,0:T(8,128)} %param.11, s32[]{:T(128)S(6)} %select_n.16, s32[]{:T(128)S(6)} %select_n.17), kind=kLoop, calls=%fused_computation | loop fusion | bytes 1048584 | tf_op jit(solution)/shard_map/dynamic_slice | solution.py:432
  1.7 3.0 %collective-permute-start.7 = (f32[4,64,256]{2,1,0:T(8,128)S(1)}, f32[4,64,256]{2,1,0:T(8,128)S(1)}, u32[]{:S(2)}, u32[]{:S(2)}) collective-permute-start(f32[4,64,256]{2,1,0:T(8,128)S(1)} %get-tuple-element.93), channel_id=1, source_target_pairs={{0,1},{1,0},{2,3},{3,2},{4,5},{5,4},{6,7},{7,6},{8,9},{9,8},{10,11... | collective-permute-start | bytes 786440 | tf_op jit(solution)/shard_map/ppermute | solution.py:360
  6.1 2.6 %shard_map.121 = (f32[16,64,256]{2,1,0:T(8,128)S(1)}, f32[4,64,256]{2,1,0:T(8,128)S(1)}, f32[4,64,256]{2,1,0:T(8,128)S(1)}, bf16[256,256]{1,0:T(8,128)(2,1)S(1)}...) custom-call(f32[8]{0:T(128)S(1)} %copy-done.3, ...), custom_call_target="tpu_custom_call" | custom-call | flops 1024 | bytes 1024 | tf_op jit(solution)/shard_map/pallas_call | solution.py:22
  8.7 4.3 %collective-permute-start = (f32[4,64,256]{2,1,0:T(8,128)S(1)}, f32[4,64,256]{2,1,0:T(8,128)S(1)}, u32[]{:S(2)}, u32[]{:S(2)}) collective-permute-start(f32[4,64,256]{2,1,0:T(8,128)S(1)} %get-tuple-element.52), channel_id=1, source_target_pairs={{0,1},{1,0},{2,3},{3,2},{4,5},{5,4},{6,7},{7,6},{8,9},{9,8},{10,11... | collective-permute-start | bytes 786440 | tf_op jit(solution)/shard_map/ppermute | solution.py:360
  13.8 6.7 %shard_map.122.refs_7_.refs_9_.refs_5_ = f32[4,16,64,256]{3,2,1,0:T(8,128)S(1)} custom-call(s32[3,1024]{1,0:T(4,128)S(1)} %bitcast.16, f32[4,1024]{1,0:T(4,128)S(1)} %bitcast.17, f32[16,64,256]{2,1,0:T(8,128)S(1)} %get-tuple-element.54._.refs_6_.refs_8_.rate.refs_4_), custom_call_target="tpu_custom_call" | custom-call | flops 1024 | bytes 1024 | tf_op jit(solution)/shard_map/pallas_call | solution.py:22
  20.5 2.2 %collective-permute-done.7.refs_7_ = f32[4,64,256]{2,1,0:T(8,128)S(1)} collective-permute-done((f32[4,64,256]{2,1,0:T(8,128)S(1)}, f32[4,64,256]{2,1,0:T(8,128)S(1)}, u32[]{:S(2)}, u32[]{:S(2)}) %collective-permute-start.7) | collective-permute-done | bytes 262176 | tf_op jit(solution)/shard_map/ppermute | solution.py:360
  22.7 1.8 %shard_map.125 = (f32[16,64,256]{2,1,0:T(8,128)S(1)}, f32[16,64,256]{2,1,0:T(8,128)S(1)}, f32[4,64,256]{2,1,0:T(8,128)S(1)}, f32[4,64,256]{2,1,0:T(8,128)S(1)}) custom-call(bf16[256,256]{1,0:T(8,128)(2,1)S(1)} %get-tuple-element.48.refs_0_, bf16[256,256]{1,0:T(8,128)(2,1)S(1)} %get-tuple-element.49.refs_1_, s32[1,3]{1,0:T(1,128)S(1)} %copy-done.1, ...), custom_call_target="tpu_custom_call" | custom-call | flops 1024 | bytes 1024 | tf_op jit(solution)/shard_map/pallas_call | solution.py:22
  25.2 5.3 %collective-permute-start.9 = (f32[4,64,256]{2,1,0:T(8,128)S(1)}, f32[4,64,256]{2,1,0:T(8,128)S(1)}, u32[]{:S(2)}, u32[]{:S(2)}) collective-permute-start(f32[4,64,256]{2,1,0:T(8,128)S(1)} %get-tuple-element.66), channel_id=1, source_target_pairs={{0,1},{1,0},{2,3},{3,2},{4,5},{5,4},{6,7},{7,6},{8,9},{9,8},{10,11... | collective-permute-start | bytes 786440 | tf_op jit(solution)/shard_map/ppermute | solution.py:360
  30.6 1.8 %shard_map.123 = (f32[16,64,256]{2,1,0:T(8,128)S(1)}, f32[4,64,256]{2,1,0:T(8,128)S(1)}, f32[4,64,256]{2,1,0:T(8,128)S(1)}) custom-call(bf16[256,256]{1,0:T(8,128)(2,1)S(1)} %get-tuple-element.48.refs_0_, bf16[256,256]{1,0:T(8,128)(2,1)S(1)} %get-tuple-element.49.refs_1_, f32[16,64,256]{2,1,0:T(8,128)S(1)} %get-tuple-element.50.refs_2_.refs_3_.refs_15_.a5, ...), custom_call_target="tpu_custom_call" | custom-call | flops 1024 | bytes 1024 | tf_op jit(solution)/shard_map/pallas_call | solution.py:22
  33.2 12.1 %collective-permute-done.9.refs_7_ = f32[4,64,256]{2,1,0:T(8,128)S(1)} collective-permute-done((f32[4,64,256]{2,1,0:T(8,128)S(1)}, f32[4,64,256]{2,1,0:T(8,128)S(1)}, u32[]{:S(2)}, u32[]{:S(2)}) %collective-permute-start.9) | collective-permute-done | bytes 262176 | tf_op jit(solution)/shard_map/ppermute | solution.py:360
  45.3 1.8 %shard_map.126 = (f32[16,64,256]{2,1,0:T(8,128)S(1)}, f32[16,64,256]{2,1,0:T(8,128)S(1)}, f32[4,64,256]{2,1,0:T(8,128)S(1)}, f32[4,64,256]{2,1,0:T(8,128)S(1)}) custom-call(bf16[256,256]{1,0:T(8,128)(2,1)S(1)} %get-tuple-element.48.refs_0_, bf16[256,256]{1,0:T(8,128)(2,1)S(1)} %get-tuple-element.49.refs_1_, s32[1,3]{1,0:T(1,128)S(1)} %copy-done.1, ...), custom_call_target="tpu_custom_call" | custom-call | flops 1024 | bytes 1024 | tf_op jit(solution)/shard_map/pallas_call | solution.py:22
  47.9 5.2 %collective-permute-start.11 = (f32[4,64,256]{2,1,0:T(8,128)S(1)}, f32[4,64,256]{2,1,0:T(8,128)S(1)}, u32[]{:S(2)}, u32[]{:S(2)}) collective-permute-start(f32[4,64,256]{2,1,0:T(8,128)S(1)} %get-tuple-element.70), channel_id=1, source_target_pairs={{0,1},{1,0},{2,3},{3,2},{4,5},{5,4},{6,7},{7,6},{8,9},{9,8},{10,11... | collective-permute-start | bytes 786440 | tf_op jit(solution)/shard_map/ppermute | solution.py:360
  53.1 1.9 %shard_map.124 = (f32[16,64,256]{2,1,0:T(8,128)S(1)}, f32[4,64,256]{2,1,0:T(8,128)S(1)}, f32[4,64,256]{2,1,0:T(8,128)S(1)}) custom-call(bf16[256,256]{1,0:T(8,128)(2,1)S(1)} %get-tuple-element.48.refs_0_, bf16[256,256]{1,0:T(8,128)(2,1)S(1)} %get-tuple-element.49.refs_1_, f32[16,64,256]{2,1,0:T(8,128)S(1)} %get-tuple-element.55.refs_2_.refs_5_, ...), custom_call_target="tpu_custom_call" | custom-call | flops 1024 | bytes 1024 | tf_op jit(solution)/shard_map/pallas_call | solution.py:22
  55.7 11.9 %collective-permute-done.11.refs_7_ = f32[4,64,256]{2,1,0:T(8,128)S(1)} collective-permute-done((f32[4,64,256]{2,1,0:T(8,128)S(1)}, f32[4,64,256]{2,1,0:T(8,128)S(1)}, u32[]{:S(2)}, u32[]{:S(2)}) %collective-permute-start.11) | collective-permute-done | bytes 262176 | tf_op jit(solution)/shard_map/ppermute | solution.py:360
  67.6 1.7 %shard_map.127 = (f32[16,64,256]{2,1,0:T(8,128)S(1)}, f32[16,64,256]{2,1,0:T(8,128)S(1)}, f32[4,64,256]{2,1,0:T(8,128)S(1)}, f32[4,64,256]{2,1,0:T(8,128)S(1)}) custom-call(bf16[256,256]{1,0:T(8,128)(2,1)S(1)} %get-tuple-element.48.refs_0_, bf16[256,256]{1,0:T(8,128)(2,1)S(1)} %get-tuple-element.49.refs_1_, s32[1,3]{1,0:T(1,128)S(1)} %copy-done.1, ...), custom_call_target="tpu_custom_call" | custom-call | flops 1024 | bytes 1024 | tf_op jit(solution)/shard_map/pallas_call | solution.py:22
  70.0 5.1 %collective-permute-start.13 = (f32[4,64,256]{2,1,0:T(8,128)S(1)}, f32[4,64,256]{2,1,0:T(8,128)S(1)}, u32[]{:S(2)}, u32[]{:S(2)}) collective-permute-start(f32[4,64,256]{2,1,0:T(8,128)S(1)} %get-tuple-element.76), channel_id=1, source_target_pairs={{0,1},{1,0},{2,3},{3,2},{4,5},{5,4},{6,7},{7,6},{8,9},{9,8},{10,11... | collective-permute-start | bytes 786440 | tf_op jit(solution)/shard_map/ppermute | solution.py:360
  75.1 3.7 %shard_map.128 = (f32[16,64,256]{2,1,0:T(8,128)S(1)}, f32[4,64,256]{2,1,0:T(8,128)S(1)}, f32[4,64,256]{2,1,0:T(8,128)S(1)}, f32[2,4,64,256]{3,2,1,0:T(8,128)S(1)...) custom-call(bf16[256,256]{1,0:T(8,128)(2,1)S(1)} %get-tuple-element., ...), custom_call_target="tpu_custom_call" | custom-call | flops 1024 | bytes 1024 | tf_op jit(solution)/shard_map/pallas_call | solution.py:22
  81.4 1.6 %collective-permute-start.18 = (f32[4,64,256]{2,1,0:T(8,128)S(1)}, f32[4,64,256]{2,1,0:T(8,128)S(1)}, u32[]{:S(2)}, u32[]{:S(2)}) collective-permute-start(f32[4,64,256]{2,1,0:T(8,128)S(1)} %shard_map.131._.a), channel_id=1, source_target_pairs={{0,16},{8,24},{16,0},{24,8},{1,17},{9,25},{17,1},{25,9},{2,18},{10... | collective-permute-start | bytes 786440 | tf_op jit(solution)/shard_map/ppermute | solution.py:387
  84.3 1.7 %collective-permute-done.13.near = f32[4,64,256]{2,1,0:T(8,128)S(1)} collective-permute-done((f32[4,64,256]{2,1,0:T(8,128)S(1)}, f32[4,64,256]{2,1,0:T(8,128)S(1)}, u32[]{:S(2)}, u32[]{:S(2)}) %collective-permute-start.13) | collective-permute-done | bytes 262176 | tf_op jit(solution)/shard_map/ppermute | solution.py:360
  87.0 2.9 %collective-permute-done.18.b.refs_2_ = f32[4,64,256]{2,1,0:T(8,128)S(1)} collective-permute-done((f32[4,64,256]{2,1,0:T(8,128)S(1)}, f32[4,64,256]{2,1,0:T(8,128)S(1)}, u32[]{:S(2)}, u32[]{:S(2)}) %collective-permute-start.18) | collective-permute-done | bytes 262176 | tf_op jit(solution)/shard_map/ppermute | solution.py:387
  89.9 1.6 %collective-permute-start.23 = (f32[4,64,256]{2,1,0:T(8,128)S(1)}, f32[4,64,256]{2,1,0:T(8,128)S(1)}, u32[]{:S(2)}, u32[]{:S(2)}) collective-permute-start(f32[4,64,256]{2,1,0:T(8,128)S(1)} %shard_map.135.a), channel_id=1, source_target_pairs={{0,16},{8,24},{16,0},{24,8},{1,17},{9,25},{17,1},{25,9},{2,18},{10... | collective-permute-start | bytes 786440 | tf_op jit(solution)/shard_map/ppermute | solution.py:387
  91.5 2.4 %shard_map.130 = (f32[16,64,256]{2,1,0:T(8,128)}, f32[16,64,256]{2,1,0:T(8,128)}, f32[2,4,64,256]{3,2,1,0:T(8,128)S(1)}) custom-call(bf16[256,256]{1,0:T(8,128)(2,1)S(1)} %get-tuple-element.48.refs_0_, bf16[256,256]{1,0:T(8,128)(2,1)S(1)} %get-tuple-element.49.refs_1_, f32[16,64,256]{2,1,0:T(8,128)S(1)} %get-tuple-element.73.refs_2_, ...), custom_call_target="tpu_custom_call" | custom-call | flops 1024 | bytes 1024 | tf_op jit(solution)/shard_map/pallas_call | solution.py:22
  93.9 3.1 %collective-permute-done.19.near = f32[4,64,256]{2,1,0:T(8,128)S(1)} collective-permute-done((f32[4,64,256]{2,1,0:T(8,128)S(1)}, f32[4,64,256]{2,1,0:T(8,128)S(1)}, u32[]{:S(2)}, u32[]{:S(2)}) %collective-permute-start.19) | collective-permute-done | bytes 262176 | tf_op jit(solution)/shard_map/ppermute | solution.py:360
  97.9 1.0 shard_map.137
  (60 shorter events, 12.7 us)
Async XLA Ops:
  1.7 21.0 %collective-permute-start.7 = (f32[4,64,256]{2,1,0:T(8,128)S(1)}, f32[4,64,256]{2,1,0:T(8,128)S(1)}, u32[]{:S(2)}, u32[]{:S(2)}) collective-permute-start(f32[4,64,256]{2,1,0:T(8,128)S(1)} %get-tuple-element.93), channel_id=1, source_target_pairs={{0,1},{1,0},{2,3},{3,2},{4,5},{5,4},{6,7},{7,6},{8,9},{9,8},{10,11... | collective-permute-start | bytes 786440 | tf_op jit(solution)/shard_map/ppermute | solution.py:360
  4.8 17.9 %collective-permute-start.6 = (f32[4,64,256]{2,1,0:T(8,128)S(1)}, f32[4,64,256]{2,1,0:T(8,128)S(1)}, u32[]{:S(2)}, u32[]{:S(2)}) collective-permute-start(f32[4,64,256]{2,1,0:T(8,128)S(1)} %get-tuple-element.94), channel_id=1, source_target_pairs={{1,2},{3,4},{5,6},{2,1},{4,3},{6,5},{9,10},{11,12},{13,14},{10,9},... | collective-permute-start | bytes 786440 | tf_op jit(solution)/shard_map/ppermute | solution.py:359
  8.7 21.8 %collective-permute-start = (f32[4,64,256]{2,1,0:T(8,128)S(1)}, f32[4,64,256]{2,1,0:T(8,128)S(1)}, u32[]{:S(2)}, u32[]{:S(2)}) collective-permute-start(f32[4,64,256]{2,1,0:T(8,128)S(1)} %get-tuple-element.52), channel_id=1, source_target_pairs={{0,1},{1,0},{2,3},{3,2},{4,5},{5,4},{6,7},{7,6},{8,9},{9,8},{10,11... | collective-permute-start | bytes 786440 | tf_op jit(solution)/shard_map/ppermute | solution.py:360
  13.1 17.5 %collective-permute-start.1 = (f32[4,64,256]{2,1,0:T(8,128)S(1)}, f32[4,64,256]{2,1,0:T(8,128)S(1)}, u32[]{:S(2)}, u32[]{:S(2)}) collective-permute-start(f32[4,64,256]{2,1,0:T(8,128)S(1)} %get-tuple-element.53), channel_id=1, source_target_pairs={{1,2},{3,4},{5,6},{2,1},{4,3},{6,5},{9,10},{11,12},{13,14},{10,9},... | collective-permute-start | bytes 786440 | tf_op jit(solution)/shard_map/ppermute | solution.py:359
  24.6 8.6 %collective-permute-start.8 = (f32[4,64,256]{2,1,0:T(8,128)S(1)}, f32[4,64,256]{2,1,0:T(8,128)S(1)}, u32[]{:S(2)}, u32[]{:S(2)}) collective-permute-start(f32[4,64,256]{2,1,0:T(8,128)S(1)} %get-tuple-element.65), channel_id=1, source_target_pairs={{1,2},{3,4},{5,6},{2,1},{4,3},{6,5},{9,10},{11,12},{13,14},{10,9},... | collective-permute-start | bytes 786440 | tf_op jit(solution)/shard_map/ppermute | solution.py:359
  25.2 20.0 %collective-permute-start.9 = (f32[4,64,256]{2,1,0:T(8,128)S(1)}, f32[4,64,256]{2,1,0:T(8,128)S(1)}, u32[]{:S(2)}, u32[]{:S(2)}) collective-permute-start(f32[4,64,256]{2,1,0:T(8,128)S(1)} %get-tuple-element.66), channel_id=1, source_target_pairs={{0,1},{1,0},{2,3},{3,2},{4,5},{5,4},{6,7},{7,6},{8,9},{9,8},{10,11... | collective-permute-start | bytes 786440 | tf_op jit(solution)/shard_map/ppermute | solution.py:360
  32.4 20.7 %collective-permute-start.2 = (f32[4,64,256]{2,1,0:T(8,128)S(1)}, f32[4,64,256]{2,1,0:T(8,128)S(1)}, u32[]{:S(2)}, u32[]{:S(2)}) collective-permute-start(f32[4,64,256]{2,1,0:T(8,128)S(1)} %get-tuple-element.56), channel_id=1, source_target_pairs={{0,1},{1,0},{2,3},{3,2},{4,5},{5,4},{6,7},{7,6},{8,9},{9,8},{10,11... | collective-permute-start | bytes 786440 | tf_op jit(solution)/shard_map/ppermute | solution.py:360
  32.5 20.6 %collective-permute-start.3 = (f32[4,64,256]{2,1,0:T(8,128)S(1)}, f32[4,64,256]{2,1,0:T(8,128)S(1)}, u32[]{:S(2)}, u32[]{:S(2)}) collective-permute-start(f32[4,64,256]{2,1,0:T(8,128)S(1)} %get-tuple-element.57), channel_id=1, source_target_pairs={{1,2},{3,4},{5,6},{2,1},{4,3},{6,5},{9,10},{11,12},{13,14},{10,9},... | collective-permute-start | bytes 786440 | tf_op jit(solution)/shard_map/ppermute | solution.py:359
  47.1 8.7 %collective-permute-start.10 = (f32[4,64,256]{2,1,0:T(8,128)S(1)}, f32[4,64,256]{2,1,0:T(8,128)S(1)}, u32[]{:S(2)}, u32[]{:S(2)}) collective-permute-start(f32[4,64,256]{2,1,0:T(8,128)S(1)} %get-tuple-element.69), channel_id=1, source_target_pairs={{1,2},{3,4},{5,6},{2,1},{4,3},{6,5},{9,10},{11,12},{13,14},{10,9},... | collective-permute-start | bytes 786440 | tf_op jit(solution)/shard_map/ppermute | solution.py:359
  47.9 19.7 %collective-permute-start.11 = (f32[4,64,256]{2,1,0:T(8,128)S(1)}, f32[4,64,256]{2,1,0:T(8,128)S(1)}, u32[]{:S(2)}, u32[]{:S(2)}) collective-permute-start(f32[4,64,256]{2,1,0:T(8,128)S(1)} %get-tuple-element.70), channel_id=1, source_target_pairs={{0,1},{1,0},{2,3},{3,2},{4,5},{5,4},{6,7},{7,6},{8,9},{9,8},{10,11... | collective-permute-start | bytes 786440 | tf_op jit(solution)/shard_map/ppermute | solution.py:360
  55.0 20.1 %collective-permute-start.4 = (f32[4,64,256]{2,1,0:T(8,128)S(1)}, f32[4,64,256]{2,1,0:T(8,128)S(1)}, u32[]{:S(2)}, u32[]{:S(2)}) collective-permute-start(f32[4,64,256]{2,1,0:T(8,128)S(1)} %get-tuple-element.59), channel_id=1, source_target_pairs={{0,1},{1,0},{2,3},{3,2},{4,5},{5,4},{6,7},{7,6},{8,9},{9,8},{10,11... | collective-permute-start | bytes 786440 | tf_op jit(solution)/shard_map/ppermute | solution.py:360
  55.0 20.1 %collective-permute-start.5 = (f32[4,64,256]{2,1,0:T(8,128)S(1)}, f32[4,64,256]{2,1,0:T(8,128)S(1)}, u32[]{:S(2)}, u32[]{:S(2)}) collective-permute-start(f32[4,64,256]{2,1,0:T(8,128)S(1)} %get-tuple-element.60), channel_id=1, source_target_pairs={{1,2},{3,4},{5,6},{2,1},{4,3},{6,5},{9,10},{11,12},{13,14},{10,9},... | collective-permute-start | bytes 786440 | tf_op jit(solution)/shard_map/ppermute | solution.py:359
  69.3 14.9 %collective-permute-start.12 = (f32[4,64,256]{2,1,0:T(8,128)S(1)}, f32[4,64,256]{2,1,0:T(8,128)S(1)}, u32[]{:S(2)}, u32[]{:S(2)}) collective-permute-start(f32[4,64,256]{2,1,0:T(8,128)S(1)} %get-tuple-element.75), channel_id=1, source_target_pairs={{1,2},{3,4},{5,6},{2,1},{4,3},{6,5},{9,10},{11,12},{13,14},{10,9},... | collective-permute-start | bytes 786440 | tf_op jit(solution)/shard_map/ppermute | solution.py:359
  70.0 16.0 %collective-permute-start.13 = (f32[4,64,256]{2,1,0:T(8,128)S(1)}, f32[4,64,256]{2,1,0:T(8,128)S(1)}, u32[]{:S(2)}, u32[]{:S(2)}) collective-permute-start(f32[4,64,256]{2,1,0:T(8,128)S(1)} %get-tuple-element.76), channel_id=1, source_target_pairs={{0,1},{1,0},{2,3},{3,2},{4,5},{5,4},{6,7},{7,6},{8,9},{9,8},{10,11... | collective-permute-start | bytes 786440 | tf_op jit(solution)/shard_map/ppermute | solution.py:360
  78.8 1.3 %collective-permute-start.17 = (f32[1,64,256]{2,1,0:T(8,128)S(1)}, f32[1,64,256]{2,1,0:T(8,128)S(1)}, u32[]{:S(2)}, u32[]{:S(2)}) collective-permute-start(f32[1,64,256]{2,1,0:T(8,128)S(1)} %get-tuple-element.97), channel_id=1, source_target_pairs={{0,8},{8,0},{16,24},{24,16},{1,9},{9,1},{17,25},{25,17},{2,10},{10... | collective-permute-start | bytes 196616 | tf_op jit(solution)/shard_map/ppermute | solution.py:380
  78.9 1.4 %collective-permute-start.16 = (f32[1,64,256]{2,1,0:T(8,128)S(1)}, f32[1,64,256]{2,1,0:T(8,128)S(1)}, u32[]{:S(2)}, u32[]{:S(2)}) collective-permute-start(f32[1,64,256]{2,1,0:T(8,128)S(1)} %get-tuple-element.98), channel_id=1, source_target_pairs={{0,8},{8,0},{16,24},{24,16},{1,9},{9,1},{17,25},{25,17},{2,10},{10... | collective-permute-start | bytes 196616 | tf_op jit(solution)/shard_map/ppermute | solution.py:380
  81.4 8.4 %collective-permute-start.18 = (f32[4,64,256]{2,1,0:T(8,128)S(1)}, f32[4,64,256]{2,1,0:T(8,128)S(1)}, u32[]{:S(2)}, u32[]{:S(2)}) collective-permute-start(f32[4,64,256]{2,1,0:T(8,128)S(1)} %shard_map.131._.a), channel_id=1, source_target_pairs={{0,16},{8,24},{16,0},{24,8},{1,17},{9,25},{17,1},{25,9},{2,18},{10... | collective-permute-start | bytes 786440 | tf_op jit(solution)/shard_map/ppermute | solution.py:387
  83.0 13.9 %collective-permute-start.19 = (f32[4,64,256]{2,1,0:T(8,128)S(1)}, f32[4,64,256]{2,1,0:T(8,128)S(1)}, u32[]{:S(2)}, u32[]{:S(2)}) collective-permute-start(f32[4,64,256]{2,1,0:T(8,128)S(1)} %get-tuple-element.85), channel_id=1, source_target_pairs={{0,1},{1,0},{2,3},{3,2},{4,5},{5,4},{6,7},{7,6},{8,9},{9,8},{10,11... | collective-permute-start | bytes 786440 | tf_op jit(solution)/shard_map/ppermute | solution.py:360
  83.6 13.3 %collective-permute-start.20 = (f32[4,64,256]{2,1,0:T(8,128)S(1)}, f32[4,64,256]{2,1,0:T(8,128)S(1)}, u32[]{:S(2)}, u32[]{:S(2)}) collective-permute-start(f32[4,64,256]{2,1,0:T(8,128)S(1)} %get-tuple-element.86), channel_id=1, source_target_pairs={{1,2},{3,4},{5,6},{2,1},{4,3},{6,5},{9,10},{11,12},{13,14},{10,9},... | collective-permute-start | bytes 786440 | tf_op jit(solution)/shard_map/ppermute | solution.py:359
  86.4 3.4 %collective-permute-start.22 = (f32[2,64,256]{2,1,0:T(8,128)S(1)}, f32[2,64,256]{2,1,0:T(8,128)S(1)}, u32[]{:S(2)}, u32[]{:S(2)}) collective-permute-start(f32[2,64,256]{2,1,0:T(8,128)S(1)} %get-tuple-element.95), channel_id=1, source_target_pairs={{0,8},{8,0},{16,24},{24,16},{1,9},{9,1},{17,25},{25,17},{2,10},{10... | collective-permute-start | bytes 393224 | tf_op jit(solution)/shard_map/ppermute | solution.py:380
  86.5 3.4 %collective-permute-start.21 = (f32[2,64,256]{2,1,0:T(8,128)S(1)}, f32[2,64,256]{2,1,0:T(8,128)S(1)}, u32[]{:S(2)}, u32[]{:S(2)}) collective-permute-start(f32[2,64,256]{2,1,0:T(8,128)S(1)} %get-tuple-element.96), channel_id=1, source_target_pairs={{0,8},{8,0},{16,24},{24,16},{1,9},{9,1},{17,25},{25,17},{2,10},{10... | collective-permute-start | bytes 393224 | tf_op jit(solution)/shard_map/ppermute | solution.py:380
  89.9 7.6 %collective-permute-start.23 = (f32[4,64,256]{2,1,0:T(8,128)S(1)}, f32[4,64,256]{2,1,0:T(8,128)S(1)}, u32[]{:S(2)}, u32[]{:S(2)}) collective-permute-start(f32[4,64,256]{2,1,0:T(8,128)S(1)} %shard_map.135.a), channel_id=1, source_target_pairs={{0,16},{8,24},{16,0},{24,8},{1,17},{9,25},{17,1},{25,9},{2,18},{10... | collective-permute-start | bytes 786440 | tf_op jit(solution)/shard_map/ppermute | solution.py:387
  97.2 1.7 %collective-permute-start.24 = (f32[4,64,256]{2,1,0:T(8,128)S(1)}, f32[4,64,256]{2,1,0:T(8,128)S(1)}, u32[]{:S(2)}, u32[]{:S(2)}) collective-permute-start(f32[4,64,256]{2,1,0:T(8,128)S(1)} %shard_map.134.inner_kept), channel_id=1, source_target_pairs={{0,8},{8,0},{16,24},{24,16},{1,9},{9,1},{17,25},{25,17},{2,10},{10... | collective-permute-start | bytes 786440 | tf_op jit(solution)/shard_map/ppermute | solution.py:399
  97.5 1.6 %collective-permute-start.25 = (f32[4,64,256]{2,1,0:T(8,128)S(1)}, f32[4,64,256]{2,1,0:T(8,128)S(1)}, u32[]{:S(2)}, u32[]{:S(2)}) collective-permute-start(f32[4,64,256]{2,1,0:T(8,128)S(1)} %shard_map.136.kept), channel_id=1, source_target_pairs={{0,8},{8,0},{16,24},{24,16},{1,9},{9,1},{17,25},{25,17},{2,10},{10... | collective-permute-start | bytes 786440 | tf_op jit(solution)/shard_map/ppermute | solution.py:399
  (7 other events, 62.7 us)

commit v7 on v6

--- a/solution.py
+++ b/solution.py
@@ -234,19 +234,30 @@
     far_edge[...] = rate[pl.ds(far_at, halo)] * earlier[pl.ds(far_at, halo)]
 
 
-def turn_kernel(forward_step, step, *refs):
+def ahead_kernel(step, *refs):
+    (*bands, current, later, rate, injected, earlier, ext) = refs
+    alone(ext, rate[...] * current[...])
+    for first in range(0, current.shape[0], halo):
+        here = pl.ds(first, halo)
+        value = laplacian(ext, first + halo, *bands)
+        earlier[here] = 2.0 * current[here] - later[here] + value + injected[step, here]
+
+
+def turn_kernel(forward_step, *refs):
     *bands, source, wavelet = refs[:4]
     refs = refs[4:]
-    (current, later, near, far, rate, injected, lap1, lap2, lap3, wave, before, a5,
-     earlier, near_edge, far_edge, rest, part, keep, send, inner, ext, wide, grad) = refs
+    (current, later, near, far, rate, known, lap1, lap2, lap3, wave, before, a5,
+     earlier, near_edge, far_edge, rest, part, keep, send, inner, sides, wide, grad) = refs
     planes = current.shape[0]
-    place(ext, near, far)
-    ext[pl.ds(halo, planes)] = rate[...] * current[...]
+    place_sides(sides, near, far)
     alone(wide, wave[...])
     for first in range(0, planes, halo):
         here = pl.ds(first, halo)
-        value = laplacian(ext, first + halo, *bands)
-        value = 2.0 * current[here] - later[here] + value + injected[step, here]
+        value = known[here]
+        if first == 0:
+            value = value + beyond(sides, 0)
+        elif first == planes - halo:
+            value = value + beyond(sides, 1)
         earlier[here] = value
         partial = later[here] * lap3[here] + current[here] * lap2[here] + value * lap1[here]
         value = laplacian(wide, first + halo, *bands)
@@ -284,36 +295,43 @@
     send[...] = grad[1 - core()]
 
 
-def pass_kernel(near, far, _, near_edge, far_edge):
+def last_edges_kernel(step, *refs):
+    (*bands, current, later, rate, injected, near, far, _,
+     near_edge, far_edge, part, ext) = refs
+    planes = current.shape[0]
     near_edge[...] = near[...]
     far_edge[...] = far[...]
+    alone(ext, rate[...] * current[...])
+    for side, first in enumerate((0, planes - halo)):
+        here = pl.ds(first, halo)
+        value = laplacian(ext, first + halo, *bands)
+        part[side] = 2.0 * current[here] - later[here] + value + injected[step, here]
 
 
 def adjoint_inner_kernel(step, *refs):
     (*bands, current, later, rate, injected, inner, outer,
-     first_adjoint, final, part, ext, stage, sems) = refs
+     first_adjoint, final, token, scaled, stage, sems) = refs
     planes = current.shape[0]
     edge = planes - halo
     copies = []
     for piece, low, high in ((inner, halo, edge), (outer.at[0], 0, halo), (outer.at[1], edge, planes)):
         copies.append(pltpu.make_async_copy(piece, final.at[low:high], sems.at[len(copies)]))
         copies[-1].start()
-    alone(ext, rate[...] * current[...])
-    for first in range(0, planes, halo):
-        here = pl.ds(first, halo)
-        value = laplacian(ext, first + halo, *bands)
-        value = 2.0 * current[here] - later[here] + value + injected[step, here]
-        if first == 0 or first == edge:
-            part[0 if first == 0 else 1] = value
-        else:
-            stage[pl.ds(first - halo, halo)] = value
+    token[...] = jnp.zeros_like(token)
+    scaled[...] = rate[...] * current[...]
+    for first in range(halo, edge, halo):
+        here = pl.ds(first, halo)
+        value = laplacian(scaled, first, *bands)
+        stage[pl.ds(first - halo, halo)] = (
+            2.0 * current[here] - later[here] + value + injected[step, here]
+        )
     copies.append(pltpu.make_async_copy(stage, first_adjoint.at[halo:edge], sems.at[3]))
     copies[-1].start()
     for copy in copies:
         copy.wait()
 
 
-def adjoint_outer_kernel(near, far, part, outer, sides):
+def adjoint_outer_kernel(near, far, part, _, outer, sides):
     place_sides(sides, near, far)
     for side in range(2):
         outer[side] = part[side] + beyond(sides, side)
@@ -451,13 +469,23 @@
         [(f32(steps, planes, nz, ny), vmem)],
     )
 
+    outer = pltpu.VMEM((2, halo, nz, ny), jnp.float32)
     laps = []
+    known = injected
     previous, current = u0, u1
     later, adjoint = a6, a5
     for n in range(steps - 1):
+        if n == steps - 2:
+            (known,) = call(
+                functools.partial(ahead_kernel, 1),
+                (*bands, adjoint, later, rate, injected),
+                [vmem] * 6,
+                [block],
+                [ext],
+            )
         upcoming, lap, near_edge, far_edge = call(
             functools.partial(forward_kernel, n),
-            (*bands, source_index, wavelet, current, previous, *u_halo[::-1], rate, injected),
+            (*bands, source_index, wavelet, current, previous, *u_halo[::-1], rate, known),
             [vmem] * 9 + [wherever],
             [block, block, edge, edge],
             [ext],
@@ -476,26 +504,26 @@
             )
         else:
             earlier, near_edge, far_edge, rest, part, keep, send, inner_wave = call(
-                functools.partial(turn_kernel, steps - 1, step),
-                (*bands, source_index, wavelet, adjoint, later, *a_halo, rate, injected, *laps,
+                functools.partial(turn_kernel, steps - 1),
+                (*bands, source_index, wavelet, adjoint, later, *a_halo, rate, known, *laps,
                  current, previous, a5),
                 [vmem] * 16,
                 [block, edge, edge, pair, pair, quarter, quarter, (f32(inner, nz, ny), vmem)],
-                [ext, ext, within],
+                [outer, ext, within],
             )
         if n < steps - 2:
             a_halo = swap(near_edge, far_edge)
         later, adjoint = adjoint, earlier
 
     inner_sum = first_sum(keep, send, keep, 4)
-    near_edge, far_edge = call(
-        pass_kernel,
-        (near_edge, far_edge, inner_sum[0]),
-        [vmem, vmem, wherever],
-        [edge, edge],
+    near_edge, far_edge, last_part = call(
+        functools.partial(last_edges_kernel, 0),
+        (*bands, adjoint, later, rate, injected, near_edge, far_edge, inner_sum[0]),
+        [vmem] * 8 + [wherever],
+        [edge, edge, pair],
+        [ext],
     )
     a_halo = swap(near_edge, far_edge)
-    outer = pltpu.VMEM((2, halo, nz, ny), jnp.float32)
     keep, send, outer_wave = call(
         forward_outer_kernel,
         (*u_halo[::-1], rate, part, rest, a5),
@@ -504,17 +532,17 @@
         [outer, outer],
     )
     outer_sum = first_sum(keep, send, inner_sum[1], 2)
-    first_adjoint, final, part = call(
+    first_adjoint, final, token = call(
         functools.partial(adjoint_inner_kernel, 0),
         (*bands, adjoint, later, rate, injected, inner_wave, outer_wave),
         [vmem] * 8,
-        [(whole, hbm), (whole, hbm), pair],
-        [ext, within, pltpu.SemaphoreType.DMA((4,))],
+        [(whole, hbm), (whole, hbm), (f32(8, 128), vmem)],
+        [pltpu.VMEM((planes, nz, ny), jnp.float32), within, pltpu.SemaphoreType.DMA((4,))],
     )
     (last_outer,) = call(
         adjoint_outer_kernel,
-        (*a_halo, part),
-        [vmem] * 3,
+        (*a_halo, last_part, token),
+        [vmem] * 3 + [wherever],
         [pair],
         [outer],
         cost=2000000000,

time: 100 us -> 101 us (1.010)
    ppermute x2, waiting for transfers between devices: 3.09 us -> 1.74 us  [first_sum(): return (kept, lax.ppermute(kept, 'shot', across))]
    pallas_call x18 -> x19, Pallas kernels: 27 us -> 27.8 us  [call(): pl.pallas_call(kernel, out_shape=[pltpu.VMEM(shape.shape, shape.dtype) if...]
  transfers between devices with their start and end apart: 26 -> 26, of which waited for: 11 -> 10; matrix products, arithmetic and copies ran while one was open for 0% -> 0% of each run, Pallas kernels for 26% -> 27%
where the time goes in v7:
time: 101 us; the launch traced here: 100 us
  waiting for transfers between devices  35.2 us (35%)
  starting transfers between devices  34.4 us (34%)
  Pallas kernels  27.8 us (28%)
  local copies, waits for them, and re-layouts  1.79 us (2%)
  between operations  1.12 us (1%)
    ppermute x8, waiting for transfers between devices, swap(): return (lax.ppermute(near_edge, 'dom', near_pairs), far)  31.4 us
    pallas_call x19, Pallas kernels, call(): pl.pallas_call(kernel, out_shape=[pltpu.VMEM(shape.shape, shape.dtype) if...  27.8 us
    ppermute x8, starting transfers between devices, swap(): return (lax.ppermute(near_edge, 'dom', near_pairs), far)  23.6 us
    ppermute x8, starting transfers between devices, swap(): far = lax.ppermute(far_edge, 'dom', far_pairs)  5.55 us
    ppermute x2, starting transfers between devices, first_sum(): return (kept, lax.ppermute(kept, 'shot', across))  3.18 us
  transfers between devices with their start and end apart: 26, of which 10 were waited for; matrix products, arithmetic and copies ran while one was open for 0% of the time, Pallas kernels for 27%

profile of v7, /device:TPU:0, one launch (start us, length us, event | category | flops | bytes accessed | tf_op | source)
XLA Modules:
  0.0 100.3 jit_solution(4782980349909202362)
XLA Ops:
  0.7 1.1 %dynamic-slice_bitcast_fusion = (f32[4,64,256]{2,1,0:T(8,128)S(1)}, f32[4,64,256]{2,1,0:T(8,128)S(1)}) fusion(f32[1,16,64,256]{3,2,1,0:T(8,128)} %param.11, s32[]{:T(128)S(6)} %select_n.16, s32[]{:T(128)S(6)} %select_n.17), kind=kLoop, calls=%fused_computation | loop fusion | bytes 1048584 | tf_op jit(solution)/shard_map/dynamic_slice | solution.py:450
  1.7 3.0 %collective-permute-start.7 = (f32[4,64,256]{2,1,0:T(8,128)S(1)}, f32[4,64,256]{2,1,0:T(8,128)S(1)}, u32[]{:S(2)}, u32[]{:S(2)}) collective-permute-start(f32[4,64,256]{2,1,0:T(8,128)S(1)} %get-tuple-element.95), channel_id=1, source_target_pairs={{0,1},{1,0},{2,3},{3,2},{4,5},{5,4},{6,7},{7,6},{8,9},{9,8},{10,11... | collective-permute-start | bytes 786440 | tf_op jit(solution)/shard_map/ppermute | solution.py:378
  6.1 2.6 %shard_map.121 = (f32[16,64,256]{2,1,0:T(8,128)S(1)}, f32[4,64,256]{2,1,0:T(8,128)S(1)}, f32[4,64,256]{2,1,0:T(8,128)S(1)}, bf16[256,256]{1,0:T(8,128)(2,1)S(1)}...) custom-call(f32[8]{0:T(128)S(1)} %copy-done.3, ...), custom_call_target="tpu_custom_call" | custom-call | flops 1024 | bytes 1024 | tf_op jit(solution)/shard_map/pallas_call | solution.py:22
  8.7 4.3 %collective-permute-start = (f32[4,64,256]{2,1,0:T(8,128)S(1)}, f32[4,64,256]{2,1,0:T(8,128)S(1)}, u32[]{:S(2)}, u32[]{:S(2)}) collective-permute-start(f32[4,64,256]{2,1,0:T(8,128)S(1)} %get-tuple-element.53), channel_id=1, source_target_pairs={{0,1},{1,0},{2,3},{3,2},{4,5},{5,4},{6,7},{7,6},{8,9},{9,8},{10,11... | collective-permute-start | bytes 786440 | tf_op jit(solution)/shard_map/ppermute | solution.py:378
  13.8 6.7 %shard_map.122.refs_7_.refs_5_.refs_9_ = f32[4,16,64,256]{3,2,1,0:T(8,128)S(1)} custom-call(s32[3,1024]{1,0:T(4,128)S(1)} %bitcast.16, f32[4,1024]{1,0:T(4,128)S(1)} %bitcast.17, f32[16,64,256]{2,1,0:T(8,128)S(1)} %get-tuple-element.55._.refs_6_.refs_4_.refs_8_.rate), custom_call_target="tpu_custom_call" | custom-call | flops 1024 | bytes 1024 | tf_op jit(solution)/shard_map/pallas_call | solution.py:22
  20.5 2.2 %collective-permute-done.7.refs_7_ = f32[4,64,256]{2,1,0:T(8,128)S(1)} collective-permute-done((f32[4,64,256]{2,1,0:T(8,128)S(1)}, f32[4,64,256]{2,1,0:T(8,128)S(1)}, u32[]{:S(2)}, u32[]{:S(2)}) %collective-permute-start.7) | collective-permute-done | bytes 262176 | tf_op jit(solution)/shard_map/ppermute | solution.py:378
  22.7 1.8 %shard_map.126 = (f32[16,64,256]{2,1,0:T(8,128)S(1)}, f32[16,64,256]{2,1,0:T(8,128)S(1)}, f32[4,64,256]{2,1,0:T(8,128)S(1)}, f32[4,64,256]{2,1,0:T(8,128)S(1)}) custom-call(bf16[256,256]{1,0:T(8,128)(2,1)S(1)} %get-tuple-element.49.refs_0_, bf16[256,256]{1,0:T(8,128)(2,1)S(1)} %get-tuple-element.50.refs_1_, s32[1,3]{1,0:T(1,128)S(1)} %copy-done.1, ...), custom_call_target="tpu_custom_call" | custom-call | flops 1024 | bytes 1024 | tf_op jit(solution)/shard_map/pallas_call | solution.py:22
  25.2 5.3 %collective-permute-start.9 = (f32[4,64,256]{2,1,0:T(8,128)S(1)}, f32[4,64,256]{2,1,0:T(8,128)S(1)}, u32[]{:S(2)}, u32[]{:S(2)}) collective-permute-start(f32[4,64,256]{2,1,0:T(8,128)S(1)} %get-tuple-element.67), channel_id=1, source_target_pairs={{0,1},{1,0},{2,3},{3,2},{4,5},{5,4},{6,7},{7,6},{8,9},{9,8},{10,11... | collective-permute-start | bytes 786440 | tf_op jit(solution)/shard_map/ppermute | solution.py:378
  30.5 1.8 %shard_map.123 = (f32[16,64,256]{2,1,0:T(8,128)S(1)}, f32[4,64,256]{2,1,0:T(8,128)S(1)}, f32[4,64,256]{2,1,0:T(8,128)S(1)}) custom-call(bf16[256,256]{1,0:T(8,128)(2,1)S(1)} %get-tuple-element.49.refs_0_, bf16[256,256]{1,0:T(8,128)(2,1)S(1)} %get-tuple-element.50.refs_1_, f32[16,64,256]{2,1,0:T(8,128)S(1)} %get-tuple-element.51.refs_2_.refs_3_.refs_15_.a5, ...), custom_call_target="tpu_custom_call" | custom-call | flops 1024 | bytes 1024 | tf_op jit(solution)/shard_map/pallas_call | solution.py:22
  33.1 12.1 %collective-permute-done.9.refs_7_ = f32[4,64,256]{2,1,0:T(8,128)S(1)} collective-permute-done((f32[4,64,256]{2,1,0:T(8,128)S(1)}, f32[4,64,256]{2,1,0:T(8,128)S(1)}, u32[]{:S(2)}, u32[]{:S(2)}) %collective-permute-start.9) | collective-permute-done | bytes 262176 | tf_op jit(solution)/shard_map/ppermute | solution.py:378
  45.2 1.8 %shard_map.127 = (f32[16,64,256]{2,1,0:T(8,128)S(1)}, f32[16,64,256]{2,1,0:T(8,128)S(1)}, f32[4,64,256]{2,1,0:T(8,128)S(1)}, f32[4,64,256]{2,1,0:T(8,128)S(1)}) custom-call(bf16[256,256]{1,0:T(8,128)(2,1)S(1)} %get-tuple-element.49.refs_0_, bf16[256,256]{1,0:T(8,128)(2,1)S(1)} %get-tuple-element.50.refs_1_, s32[1,3]{1,0:T(1,128)S(1)} %copy-done.1, ...), custom_call_target="tpu_custom_call" | custom-call | flops 1024 | bytes 1024 | tf_op jit(solution)/shard_map/pallas_call | solution.py:22
  47.8 5.2 %collective-permute-start.11 = (f32[4,64,256]{2,1,0:T(8,128)S(1)}, f32[4,64,256]{2,1,0:T(8,128)S(1)}, u32[]{:S(2)}, u32[]{:S(2)}) collective-permute-start(f32[4,64,256]{2,1,0:T(8,128)S(1)} %get-tuple-element.71), channel_id=1, source_target_pairs={{0,1},{1,0},{2,3},{3,2},{4,5},{5,4},{6,7},{7,6},{8,9},{9,8},{10,11... | collective-permute-start | bytes 786440 | tf_op jit(solution)/shard_map/ppermute | solution.py:378
  53.0 1.8 %shard_map.124 = (f32[16,64,256]{2,1,0:T(8,128)S(1)}, f32[4,64,256]{2,1,0:T(8,128)S(1)}, f32[4,64,256]{2,1,0:T(8,128)S(1)}) custom-call(bf16[256,256]{1,0:T(8,128)(2,1)S(1)} %get-tuple-element.49.refs_0_, bf16[256,256]{1,0:T(8,128)(2,1)S(1)} %get-tuple-element.50.refs_1_, f32[16,64,256]{2,1,0:T(8,128)S(1)} %get-tuple-element.56.refs_2_.refs_3_.refs_5_, ...), custom_call_target="tpu_custom_call" | custom-call | flops 1024 | bytes 1024 | tf_op jit(solution)/shard_map/pallas_call | solution.py:22
  55.6 1.6 %shard_map.125.refs_9_ = f32[16,64,256]{2,1,0:T(8,128)S(1)} custom-call(bf16[256,256]{1,0:T(8,128)(2,1)S(1)} %get-tuple-element.49.refs_0_, bf16[256,256]{1,0:T(8,128)(2,1)S(1)} %get-tuple-element.50.refs_1_, f32[16,64,256]{2,1,0:T(8,128)S(1)} %get-tuple-element.59.refs_2_.refs_4_.refs_3_, f32[16,64,256]{2,1,0:T(8,128)S(1)} %get-tuple-element.56.refs_2_.refs_3_.refs_5_, ...), custom_call_target="tpu_custom_call" | custom-call | flops 1024 | bytes 1024 | tf_op jit(solution)/shard_map/pallas_call | solution.py:22
  57.2 10.3 %collective-permute-done.11.refs_7_ = f32[4,64,256]{2,1,0:T(8,128)S(1)} collective-permute-done((f32[4,64,256]{2,1,0:T(8,128)S(1)}, f32[4,64,256]{2,1,0:T(8,128)S(1)}, u32[]{:S(2)}, u32[]{:S(2)}) %collective-permute-start.11) | collective-permute-done | bytes 262176 | tf_op jit(solution)/shard_map/ppermute | solution.py:378
  67.5 1.8 %shard_map.128 = (f32[16,64,256]{2,1,0:T(8,128)S(1)}, f32[16,64,256]{2,1,0:T(8,128)S(1)}, f32[4,64,256]{2,1,0:T(8,128)S(1)}, f32[4,64,256]{2,1,0:T(8,128)S(1)}) custom-call(bf16[256,256]{1,0:T(8,128)(2,1)S(1)} %get-tuple-element.49.refs_0_, bf16[256,256]{1,0:T(8,128)(2,1)S(1)} %get-tuple-element.50.refs_1_, s32[1,3]{1,0:T(1,128)S(1)} %copy-done.1, ...), custom_call_target="tpu_custom_call" | custom-call | flops 1024 | bytes 1024 | tf_op jit(solution)/shard_map/pallas_call | solution.py:22
  70.0 5.1 %collective-permute-start.13 = (f32[4,64,256]{2,1,0:T(8,128)S(1)}, f32[4,64,256]{2,1,0:T(8,128)S(1)}, u32[]{:S(2)}, u32[]{:S(2)}) collective-permute-start(f32[4,64,256]{2,1,0:T(8,128)S(1)} %get-tuple-element.77), channel_id=1, source_target_pairs={{0,1},{1,0},{2,3},{3,2},{4,5},{5,4},{6,7},{7,6},{8,9},{9,8},{10,11... | collective-permute-start | bytes 786440 | tf_op jit(solution)/shard_map/ppermute | solution.py:378
  75.0 2.5 %shard_map.129 = (f32[16,64,256]{2,1,0:T(8,128)S(1)}, f32[4,64,256]{2,1,0:T(8,128)S(1)}, f32[4,64,256]{2,1,0:T(8,128)S(1)}, f32[2,4,64,256]{3,2,1,0:T(8,128)S(1)...) custom-call(bf16[256,256]{1,0:T(8,128)(2,1)S(1)} %get-tuple-element., ...), custom_call_target="tpu_custom_call" | custom-call | flops 1024 | bytes 1024 | tf_op jit(solution)/shard_map/pallas_call | solution.py:22
  80.2 1.6 %collective-permute-start.18 = (f32[4,64,256]{2,1,0:T(8,128)S(1)}, f32[4,64,256]{2,1,0:T(8,128)S(1)}, u32[]{:S(2)}, u32[]{:S(2)}) collective-permute-start(f32[4,64,256]{2,1,0:T(8,128)S(1)} %shard_map.132.refs_8_.a), channel_id=1, source_target_pairs={{0,16},{8,24},{16,0},{24,8},{1,17},{9,25},{17,1},{25,9},{2,18},{10... | collective-permute-start | bytes 786440 | tf_op jit(solution)/shard_map/ppermute | solution.py:405
  84.1 1.8 %collective-permute-done.13.near = f32[4,64,256]{2,1,0:T(8,128)S(1)} collective-permute-done((f32[4,64,256]{2,1,0:T(8,128)S(1)}, f32[4,64,256]{2,1,0:T(8,128)S(1)}, u32[]{:S(2)}, u32[]{:S(2)}) %collective-permute-start.13) | collective-permute-done | bytes 262176 | tf_op jit(solution)/shard_map/ppermute | solution.py:378
  86.9 1.7 %collective-permute-done.18.b.refs_2_ = f32[4,64,256]{2,1,0:T(8,128)S(1)} collective-permute-done((f32[4,64,256]{2,1,0:T(8,128)S(1)}, f32[4,64,256]{2,1,0:T(8,128)S(1)}, u32[]{:S(2)}, u32[]{:S(2)}) %collective-permute-start.18) | collective-permute-done | bytes 262176 | tf_op jit(solution)/shard_map/ppermute | solution.py:405
  88.7 1.6 %collective-permute-start.23 = (f32[4,64,256]{2,1,0:T(8,128)S(1)}, f32[4,64,256]{2,1,0:T(8,128)S(1)}, u32[]{:S(2)}, u32[]{:S(2)}) collective-permute-start(f32[4,64,256]{2,1,0:T(8,128)S(1)} %shard_map.136.a), channel_id=1, source_target_pairs={{0,16},{8,24},{16,0},{24,8},{1,17},{9,25},{17,1},{25,9},{2,18},{10... | collective-permute-start | bytes 786440 | tf_op jit(solution)/shard_map/ppermute | solution.py:405
  90.3 1.8 %shard_map.131 = (f32[16,64,256]{2,1,0:T(8,128)}, f32[16,64,256]{2,1,0:T(8,128)}, f32[8,128]{1,0:T(8,128)S(1)}) custom-call(bf16[256,256]{1,0:T(8,128)(2,1)S(1)} %get-tuple-element.49.refs_0_, bf16[256,256]{1,0:T(8,128)(2,1)S(1)} %get-tuple-element.50.refs_1_, f32[16,64,256]{2,1,0:T(8,128)S(1)} %get-tuple-element.74.refs_2_, ...), custom_call_target="tpu_custom_call" | custom-call | flops 1024 | bytes 1024 | tf_op jit(solution)/shard_map/pallas_call | solution.py:22
  92.1 4.9 %collective-permute-done.19.near = f32[4,64,256]{2,1,0:T(8,128)S(1)} collective-permute-done((f32[4,64,256]{2,1,0:T(8,128)S(1)}, f32[4,64,256]{2,1,0:T(8,128)S(1)}, u32[]{:S(2)}, u32[]{:S(2)}) %collective-permute-start.19) | collective-permute-done | bytes 262176 | tf_op jit(solution)/shard_map/ppermute | solution.py:378
  (61 shorter events, 14.6 us)
Async XLA Ops:
  1.7 21.0 %collective-permute-start.7 = (f32[4,64,256]{2,1,0:T(8,128)S(1)}, f32[4,64,256]{2,1,0:T(8,128)S(1)}, u32[]{:S(2)}, u32[]{:S(2)}) collective-permute-start(f32[4,64,256]{2,1,0:T(8,128)S(1)} %get-tuple-element.95), channel_id=1, source_target_pairs={{0,1},{1,0},{2,3},{3,2},{4,5},{5,4},{6,7},{7,6},{8,9},{9,8},{10,11... | collective-permute-start | bytes 786440 | tf_op jit(solution)/shard_map/ppermute | solution.py:378
  4.8 17.9 %collective-permute-start.6 = (f32[4,64,256]{2,1,0:T(8,128)S(1)}, f32[4,64,256]{2,1,0:T(8,128)S(1)}, u32[]{:S(2)}, u32[]{:S(2)}) collective-permute-start(f32[4,64,256]{2,1,0:T(8,128)S(1)} %get-tuple-element.96), channel_id=1, source_target_pairs={{1,2},{3,4},{5,6},{2,1},{4,3},{6,5},{9,10},{11,12},{13,14},{10,9},... | collective-permute-start | bytes 786440 | tf_op jit(solution)/shard_map/ppermute | solution.py:377
  8.7 21.8 %collective-permute-start = (f32[4,64,256]{2,1,0:T(8,128)S(1)}, f32[4,64,256]{2,1,0:T(8,128)S(1)}, u32[]{:S(2)}, u32[]{:S(2)}) collective-permute-start(f32[4,64,256]{2,1,0:T(8,128)S(1)} %get-tuple-element.53), channel_id=1, source_target_pairs={{0,1},{1,0},{2,3},{3,2},{4,5},{5,4},{6,7},{7,6},{8,9},{9,8},{10,11... | collective-permute-start | bytes 786440 | tf_op jit(solution)/shard_map/ppermute | solution.py:378
  13.1 17.4 %collective-permute-start.1 = (f32[4,64,256]{2,1,0:T(8,128)S(1)}, f32[4,64,256]{2,1,0:T(8,128)S(1)}, u32[]{:S(2)}, u32[]{:S(2)}) collective-permute-start(f32[4,64,256]{2,1,0:T(8,128)S(1)} %get-tuple-element.54), channel_id=1, source_target_pairs={{1,2},{3,4},{5,6},{2,1},{4,3},{6,5},{9,10},{11,12},{13,14},{10,9},... | collective-permute-start | bytes 786440 | tf_op jit(solution)/shard_map/ppermute | solution.py:377
  24.5 8.6 %collective-permute-start.8 = (f32[4,64,256]{2,1,0:T(8,128)S(1)}, f32[4,64,256]{2,1,0:T(8,128)S(1)}, u32[]{:S(2)}, u32[]{:S(2)}) collective-permute-start(f32[4,64,256]{2,1,0:T(8,128)S(1)} %get-tuple-element.66), channel_id=1, source_target_pairs={{1,2},{3,4},{5,6},{2,1},{4,3},{6,5},{9,10},{11,12},{13,14},{10,9},... | collective-permute-start | bytes 786440 | tf_op jit(solution)/shard_map/ppermute | solution.py:377
  25.2 20.0 %collective-permute-start.9 = (f32[4,64,256]{2,1,0:T(8,128)S(1)}, f32[4,64,256]{2,1,0:T(8,128)S(1)}, u32[]{:S(2)}, u32[]{:S(2)}) collective-permute-start(f32[4,64,256]{2,1,0:T(8,128)S(1)} %get-tuple-element.67), channel_id=1, source_target_pairs={{0,1},{1,0},{2,3},{3,2},{4,5},{5,4},{6,7},{7,6},{8,9},{9,8},{10,11... | collective-permute-start | bytes 786440 | tf_op jit(solution)/shard_map/ppermute | solution.py:378
  32.3 20.7 %collective-permute-start.2 = (f32[4,64,256]{2,1,0:T(8,128)S(1)}, f32[4,64,256]{2,1,0:T(8,128)S(1)}, u32[]{:S(2)}, u32[]{:S(2)}) collective-permute-start(f32[4,64,256]{2,1,0:T(8,128)S(1)} %get-tuple-element.57), channel_id=1, source_target_pairs={{0,1},{1,0},{2,3},{3,2},{4,5},{5,4},{6,7},{7,6},{8,9},{9,8},{10,11... | collective-permute-start | bytes 786440 | tf_op jit(solution)/shard_map/ppermute | solution.py:378
  32.4 20.6 %collective-permute-start.3 = (f32[4,64,256]{2,1,0:T(8,128)S(1)}, f32[4,64,256]{2,1,0:T(8,128)S(1)}, u32[]{:S(2)}, u32[]{:S(2)}) collective-permute-start(f32[4,64,256]{2,1,0:T(8,128)S(1)} %get-tuple-element.58), channel_id=1, source_target_pairs={{1,2},{3,4},{5,6},{2,1},{4,3},{6,5},{9,10},{11,12},{13,14},{10,9},... | collective-permute-start | bytes 786440 | tf_op jit(solution)/shard_map/ppermute | solution.py:377
  47.0 10.2 %collective-permute-start.10 = (f32[4,64,256]{2,1,0:T(8,128)S(1)}, f32[4,64,256]{2,1,0:T(8,128)S(1)}, u32[]{:S(2)}, u32[]{:S(2)}) collective-permute-start(f32[4,64,256]{2,1,0:T(8,128)S(1)} %get-tuple-element.70), channel_id=1, source_target_pairs={{1,2},{3,4},{5,6},{2,1},{4,3},{6,5},{9,10},{11,12},{13,14},{10,9},... | collective-permute-start | bytes 786440 | tf_op jit(solution)/shard_map/ppermute | solution.py:377
  47.8 19.7 %collective-permute-start.11 = (f32[4,64,256]{2,1,0:T(8,128)S(1)}, f32[4,64,256]{2,1,0:T(8,128)S(1)}, u32[]{:S(2)}, u32[]{:S(2)}) collective-permute-start(f32[4,64,256]{2,1,0:T(8,128)S(1)} %get-tuple-element.71), channel_id=1, source_target_pairs={{0,1},{1,0},{2,3},{3,2},{4,5},{5,4},{6,7},{7,6},{8,9},{9,8},{10,11... | collective-permute-start | bytes 786440 | tf_op jit(solution)/shard_map/ppermute | solution.py:378
  54.9 20.2 %collective-permute-start.4 = (f32[4,64,256]{2,1,0:T(8,128)S(1)}, f32[4,64,256]{2,1,0:T(8,128)S(1)}, u32[]{:S(2)}, u32[]{:S(2)}) collective-permute-start(f32[4,64,256]{2,1,0:T(8,128)S(1)} %get-tuple-element.60), channel_id=1, source_target_pairs={{0,1},{1,0},{2,3},{3,2},{4,5},{5,4},{6,7},{7,6},{8,9},{9,8},{10,11... | collective-permute-start | bytes 786440 | tf_op jit(solution)/shard_map/ppermute | solution.py:378
  54.9 20.1 %collective-permute-start.5 = (f32[4,64,256]{2,1,0:T(8,128)S(1)}, f32[4,64,256]{2,1,0:T(8,128)S(1)}, u32[]{:S(2)}, u32[]{:S(2)}) collective-permute-start(f32[4,64,256]{2,1,0:T(8,128)S(1)} %get-tuple-element.61), channel_id=1, source_target_pairs={{1,2},{3,4},{5,6},{2,1},{4,3},{6,5},{9,10},{11,12},{13,14},{10,9},... | collective-permute-start | bytes 786440 | tf_op jit(solution)/shard_map/ppermute | solution.py:377
  69.3 14.8 %collective-permute-start.12 = (f32[4,64,256]{2,1,0:T(8,128)S(1)}, f32[4,64,256]{2,1,0:T(8,128)S(1)}, u32[]{:S(2)}, u32[]{:S(2)}) collective-permute-start(f32[4,64,256]{2,1,0:T(8,128)S(1)} %get-tuple-element.76), channel_id=1, source_target_pairs={{1,2},{3,4},{5,6},{2,1},{4,3},{6,5},{9,10},{11,12},{13,14},{10,9},... | collective-permute-start | bytes 786440 | tf_op jit(solution)/shard_map/ppermute | solution.py:377
  70.0 16.0 %collective-permute-start.13 = (f32[4,64,256]{2,1,0:T(8,128)S(1)}, f32[4,64,256]{2,1,0:T(8,128)S(1)}, u32[]{:S(2)}, u32[]{:S(2)}) collective-permute-start(f32[4,64,256]{2,1,0:T(8,128)S(1)} %get-tuple-element.77), channel_id=1, source_target_pairs={{0,1},{1,0},{2,3},{3,2},{4,5},{5,4},{6,7},{7,6},{8,9},{9,8},{10,11... | collective-permute-start | bytes 786440 | tf_op jit(solution)/shard_map/ppermute | solution.py:378
  77.6 1.3 %collective-permute-start.17 = (f32[1,64,256]{2,1,0:T(8,128)S(1)}, f32[1,64,256]{2,1,0:T(8,128)S(1)}, u32[]{:S(2)}, u32[]{:S(2)}) collective-permute-start(f32[1,64,256]{2,1,0:T(8,128)S(1)} %get-tuple-element.99), channel_id=1, source_target_pairs={{0,8},{8,0},{16,24},{24,16},{1,9},{9,1},{17,25},{25,17},{2,10},{10... | collective-permute-start | bytes 196616 | tf_op jit(solution)/shard_map/ppermute | solution.py:398
  77.7 1.4 %collective-permute-start.16 = (f32[1,64,256]{2,1,0:T(8,128)S(1)}, f32[1,64,256]{2,1,0:T(8,128)S(1)}, u32[]{:S(2)}, u32[]{:S(2)}) collective-permute-start(f32[1,64,256]{2,1,0:T(8,128)S(1)} %get-tuple-element.100), channel_id=1, source_target_pairs={{0,8},{8,0},{16,24},{24,16},{1,9},{9,1},{17,25},{25,17},{2,10},{10... | collective-permute-start | bytes 196616 | tf_op jit(solution)/shard_map/ppermute | solution.py:398
  80.2 8.4 %collective-permute-start.18 = (f32[4,64,256]{2,1,0:T(8,128)S(1)}, f32[4,64,256]{2,1,0:T(8,128)S(1)}, u32[]{:S(2)}, u32[]{:S(2)}) collective-permute-start(f32[4,64,256]{2,1,0:T(8,128)S(1)} %shard_map.132.refs_8_.a), channel_id=1, source_target_pairs={{0,16},{8,24},{16,0},{24,8},{1,17},{9,25},{17,1},{25,9},{2,18},{10... | collective-permute-start | bytes 786440 | tf_op jit(solution)/shard_map/ppermute | solution.py:405
  82.8 14.2 %collective-permute-start.19 = (f32[4,64,256]{2,1,0:T(8,128)S(1)}, f32[4,64,256]{2,1,0:T(8,128)S(1)}, u32[]{:S(2)}, u32[]{:S(2)}) collective-permute-start(f32[4,64,256]{2,1,0:T(8,128)S(1)} %get-tuple-element.86), channel_id=1, source_target_pairs={{0,1},{1,0},{2,3},{3,2},{4,5},{5,4},{6,7},{7,6},{8,9},{9,8},{10,11... | collective-permute-start | bytes 786440 | tf_op jit(solution)/shard_map/ppermute | solution.py:378
  83.4 13.7 %collective-permute-start.20 = (f32[4,64,256]{2,1,0:T(8,128)S(1)}, f32[4,64,256]{2,1,0:T(8,128)S(1)}, u32[]{:S(2)}, u32[]{:S(2)}) collective-permute-start(f32[4,64,256]{2,1,0:T(8,128)S(1)} %get-tuple-element.87), channel_id=1, source_target_pairs={{1,2},{3,4},{5,6},{2,1},{4,3},{6,5},{9,10},{11,12},{13,14},{10,9},... | collective-permute-start | bytes 786440 | tf_op jit(solution)/shard_map/ppermute | solution.py:377
  86.4 2.3 %collective-permute-start.22 = (f32[2,64,256]{2,1,0:T(8,128)S(1)}, f32[2,64,256]{2,1,0:T(8,128)S(1)}, u32[]{:S(2)}, u32[]{:S(2)}) collective-permute-start(f32[2,64,256]{2,1,0:T(8,128)S(1)} %get-tuple-element.97), channel_id=1, source_target_pairs={{0,8},{8,0},{16,24},{24,16},{1,9},{9,1},{17,25},{25,17},{2,10},{10... | collective-permute-start | bytes 393224 | tf_op jit(solution)/shard_map/ppermute | solution.py:398
  86.4 2.2 %collective-permute-start.21 = (f32[2,64,256]{2,1,0:T(8,128)S(1)}, f32[2,64,256]{2,1,0:T(8,128)S(1)}, u32[]{:S(2)}, u32[]{:S(2)}) collective-permute-start(f32[2,64,256]{2,1,0:T(8,128)S(1)} %get-tuple-element.98), channel_id=1, source_target_pairs={{0,8},{8,0},{16,24},{24,16},{1,9},{9,1},{17,25},{25,17},{2,10},{10... | collective-permute-start | bytes 393224 | tf_op jit(solution)/shard_map/ppermute | solution.py:398
  88.7 8.7 %collective-permute-start.23 = (f32[4,64,256]{2,1,0:T(8,128)S(1)}, f32[4,64,256]{2,1,0:T(8,128)S(1)}, u32[]{:S(2)}, u32[]{:S(2)}) collective-permute-start(f32[4,64,256]{2,1,0:T(8,128)S(1)} %shard_map.136.a), channel_id=1, source_target_pairs={{0,16},{8,24},{16,0},{24,8},{1,17},{9,25},{17,1},{25,9},{2,18},{10... | collective-permute-start | bytes 786440 | tf_op jit(solution)/shard_map/ppermute | solution.py:405
  97.3 1.7 %collective-permute-start.24 = (f32[4,64,256]{2,1,0:T(8,128)S(1)}, f32[4,64,256]{2,1,0:T(8,128)S(1)}, u32[]{:S(2)}, u32[]{:S(2)}) collective-permute-start(f32[4,64,256]{2,1,0:T(8,128)S(1)} %shard_map.135.inner_kept), channel_id=1, source_target_pairs={{0,8},{8,0},{16,24},{24,16},{1,9},{9,1},{17,25},{25,17},{2,10},{10... | collective-permute-start | bytes 786440 | tf_op jit(solution)/shard_map/ppermute | solution.py:417
  97.4 1.8 %collective-permute-start.25 = (f32[4,64,256]{2,1,0:T(8,128)S(1)}, f32[4,64,256]{2,1,0:T(8,128)S(1)}, u32[]{:S(2)}, u32[]{:S(2)}) collective-permute-start(f32[4,64,256]{2,1,0:T(8,128)S(1)} %shard_map.137.kept), channel_id=1, source_target_pairs={{0,8},{8,0},{16,24},{24,16},{1,9},{9,1},{17,25},{25,17},{2,10},{10... | collective-permute-start | bytes 786440 | tf_op jit(solution)/shard_map/ppermute | solution.py:417
  (7 other events, 62.7 us)
